TPU v7x, 32 devices: a whole 2x2x4 slice. The times are simulated.
32 devices in a mesh: row: 8 (over y, x, core), col: 4 (over z).
Axes of the slice: x: 2, y: 2, z: 4, core: 2. Of those that a mesh axis runs over, the one named last changes fastest.
Arguments:
- images: bfloat16 [2, 32, 64, 2048], P(None, 'row', None, 'col'), may hold values from -6 to 6
- dw_kernel: float32 [7, 7, 2048], P(None, None, 'col'), may hold values from -3 to 3
- norm_gain: float32 [2048], P('col'), may hold values from 0.5 to 1.5
- proj_in: bfloat16 [2048, 8192], P('row', 'col'), may hold values from -0.125 to 0.125
- proj_out: bfloat16 [2048, 8192], P('row', 'col'), may hold values from -0.0625 to 0.0625
- layer_scale: float32 [2048], P('col'), may hold values from 0.1 to 1.9
- cotangent: bfloat16 [2, 32, 64, 2048], P(None, 'row', None, 'col'), may hold values from -0.59765625 to 0.59765625
Outputs:
- block_out: bfloat16 [2, 32, 64, 2048], P(None, 'row', None, 'col')
- grad_images: bfloat16 [2, 32, 64, 2048], P(None, 'row', None, 'col')
- grad_proj_in: bfloat16 [2048, 8192], P('row', 'col')
- grad_proj_out: bfloat16 [2048, 8192], P('row', 'col')
All inputs are finite; a program needn't handle non-finite values.
Results may differ from a plain program's by a relative error of at most 0.023.
Values may be sent and summed in bfloat16 or wider, within the bound.
No kernel may reach another device: no remote copies, remote signals or barrier semaphores. Data moves between devices by JAX's collectives and lax.ppermute only.
A program may use at most 128 MiB of HBM per device.

v0:
```python
import jax
import jax.numpy as jnp
from jax import lax
from jax.sharding import PartitionSpec as P

C = 2048
KS = 7


def with_halo(block, sides, width):
    for axis, dim in sides:
        count = lax.axis_size(axis)
        forward = [(i, i + 1) for i in range(count - 1)]
        backward = [(target, source) for source, target in forward]
        low = lax.ppermute(
            lax.slice_in_dim(block, block.shape[dim] - width, None, axis=dim), axis, forward
        )
        high = lax.ppermute(lax.slice_in_dim(block, 0, width, axis=dim), axis, backward)
        block = jnp.concatenate([low, block, high], axis=dim)
    return block


def taps_sum(padded, dw_kernel, img_rows, img_cols, flipped):
    total = jnp.zeros(padded.shape[:1] + (img_rows, img_cols) + padded.shape[3:], jnp.float32)
    reach = 2 * (KS // 2)
    for tap_row in range(KS):
        for tap_col in range(KS):
            off_row = reach - tap_row if flipped else tap_row
            off_col = reach - tap_col if flipped else tap_col
            total = (
                total
                + dw_kernel[tap_row, tap_col]
                * padded[:, off_row : off_row + img_rows, off_col : off_col + img_cols, :]
            )
    return total


def gelu_slope(values):
    return (
        0.5 * (1.0 + lax.erf(values * 0.7071067811865476))
        + values * jnp.exp(-0.5 * values * values) * 0.3989422804014327
    )


def on_device(images, dw_kernel, norm_gain, proj_in, proj_out, layer_scale, cotangent):
    img_batch, strip_rows, img_cols, local_ch = images.shape
    pixels = img_batch * strip_rows * img_cols
    reach = KS // 2
    contract_last = (((1,), (1,)), ((), ()))
    contract_first = (((0,), (0,)), ((), ()))
    rimmed = with_halo(images, (("row", 1),), reach)
    padded = jnp.pad(rimmed.astype(jnp.float32), ((0, 0), (0, 0), (reach, reach), (0, 0)))
    conv_out = taps_sum(padded, dw_kernel, strip_rows, img_cols, False).reshape(pixels, local_ch)
    row_mean = lax.psum(jnp.sum(conv_out, axis=1), "col") / C
    centred = conv_out - row_mean[:, None]
    row_var = lax.psum(jnp.sum(centred * centred, axis=1), "col") / C
    inv_std = lax.rsqrt(row_var + 1e-06)
    normed = centred * inv_std[:, None]
    scaled = (normed * norm_gain).astype(jnp.bfloat16)
    full_in = lax.all_gather(scaled, "col", axis=1, tiled=True)
    in_panel = lax.all_gather(proj_in, "row", axis=0, tiled=True)
    out_panel = lax.all_gather(proj_out, "row", axis=0, tiled=True)
    hidden_pre = jnp.dot(full_in, in_panel, preferred_element_type=jnp.float32)
    hidden = jax.nn.gelu(hidden_pre, approximate=False).astype(jnp.bfloat16)
    contrib = lax.dot_general(hidden, out_panel, contract_last, preferred_element_type=jnp.float32)
    branch = lax.psum_scatter(
        contrib.astype(jnp.bfloat16), "col", scatter_dimension=1, tiled=True
    ).astype(jnp.float32)
    residual_in = images.reshape(pixels, local_ch).astype(jnp.float32)
    block_out = (residual_in + layer_scale * branch).astype(jnp.bfloat16).reshape(images.shape)
    cot_flat = cotangent.reshape(pixels, local_ch).astype(jnp.float32)
    grad_branch = (cot_flat * layer_scale).astype(jnp.bfloat16)
    full_grad = lax.all_gather(grad_branch, "col", axis=1, tiled=True)
    grad_proj_out = lax.psum_scatter(
        lax.dot_general(
            full_grad, hidden, contract_first, preferred_element_type=jnp.float32
        ).astype(jnp.bfloat16),
        "row",
        scatter_dimension=0,
        tiled=True,
    )
    grad_hidden = jnp.dot(full_grad, out_panel, preferred_element_type=jnp.float32)
    grad_pre = (grad_hidden * gelu_slope(hidden_pre)).astype(jnp.bfloat16)
    grad_proj_in = lax.psum_scatter(
        lax.dot_general(
            full_in, grad_pre, contract_first, preferred_element_type=jnp.float32
        ).astype(jnp.bfloat16),
        "row",
        scatter_dimension=0,
        tiled=True,
    )
    back_part = lax.dot_general(
        grad_pre, in_panel, contract_last, preferred_element_type=jnp.float32
    )
    grad_scaled = lax.psum_scatter(
        back_part.astype(jnp.bfloat16), "col", scatter_dimension=1, tiled=True
    ).astype(jnp.float32)
    weighted = grad_scaled * norm_gain
    sum_one, sum_two = lax.psum(
        (jnp.sum(weighted, axis=1), jnp.sum(weighted * normed, axis=1)), "col"
    )
    grad_conv = inv_std[:, None] * (weighted - sum_one[:, None] / C - normed * sum_two[:, None] / C)
    grad_conv = grad_conv.reshape(img_batch, strip_rows, img_cols, local_ch)
    grad_rim = with_halo(grad_conv.astype(jnp.bfloat16), (("row", 1),), reach).astype(
        grad_conv.dtype
    )
    grad_pad = jnp.pad(grad_rim, ((0, 0), (0, 0), (reach, reach), (0, 0)))
    input_grad = taps_sum(grad_pad, dw_kernel, strip_rows, img_cols, True)
    grad_images = (cotangent.astype(jnp.float32) + input_grad).astype(jnp.bfloat16)
    return (block_out, grad_images, grad_proj_in, grad_proj_out)


def solution(mesh):
    placed = (
        P(None, "row", None, "col"),
        P(None, None, "col"),
        P("col"),
        P("row", "col"),
        P("row", "col"),
        P("col"),
        P(None, "row", None, "col"),
    )
    return jax.shard_map(
        on_device,
        mesh=mesh,
        in_specs=placed,
        out_specs=(
            P(None, "row", None, "col"),
            P(None, "row", None, "col"),
            P("row", "col"),
            P("row", "col"),
        ),
        check_vma=False,
    )
```

profile of v0, /device:TPU:0, one launch (start us, length us, event | category | flops | bytes accessed | tf_op | source)
XLA Modules:
  0.0 533.2 jit_solution(18388212945756421054)
XLA Ops:
  8.4 2.4 collective-permute-start
  17.7 8.7 %fusion.202 = (f32[2,4,64]{2,1,0:T(4,128)S(1)}, f32[2,4,64,512]{3,2,1,0:T(8,128)}) fusion(f32[512]{0:T(512)S(1)} %bitcast.139, f32[512]{0:T(512)S(1)} %bitcast.141, f32[512]{0:T(512)S(1)} %bitcast.85, f32[2,10,64,512]{3,2,1,0:T(8,128)S(1)} %maximum_convert_fusion, f32[512]{0:T(512)S(1)} %bitcast.87, f32[512]{0:T(512)S(1)} %bitcast.89, f32[512]{0:T(512)S(1)} %bitcast.91, ...), kind=kLoop, calls=%fused_computation.327 | loop fusion | flops 25689600 | bytes 11112448 | tf_op jit(solution)/shard_map/reduce_sum | solution.py:54
  26.5 11.9 %psum.28 = f32[512]{0:T(512)S(1)} all-reduce(f32[512]{0:T(512)S(1)} %reduce_sum.41), channel_id=1, replica_groups=mesh['row'=8,'col'=4] {'col'}, use_global_device_ids=true, to_apply=%region_1.2 | all-reduce | flops 512 | bytes 4096 | tf_op jit(solution)/shard_map/psum | solution.py:54
  40.1 8.3 %psum.29 = f32[512]{0:T(512)S(1)} all-reduce(f32[512]{0:T(512)S(1)} %reduce_sum.43), channel_id=1, replica_groups=mesh['row'=8,'col'=4] {'col'}, use_global_device_ids=true, to_apply=%region_3.4 | all-reduce | flops 512 | bytes 4096 | tf_op jit(solution)/shard_map/psum | solution.py:56
  48.5 2.2 multiply_convert_fusion.1
  52.4 48.8 %all-gather.5.cloned.1.call-done = bf16[512,2048]{1,0:T(8,128)(2,1)} async-done(((bf16[512,512]{1,0:T(8,128)(2,1)}), bf16[512,2048]{1,0:T(8,128)(2,1)}) %all-gather.5.cloned.1.call-update) | async-done | bytes 2097168 | tf_op jit(solution)/shard_map/all_gather | solution.py:60
  101.2 55.0 %all-gather.7.cloned.1.call-done = bf16[2048,2048]{1,0:T(8,128)(2,1)} async-done(((bf16[256,2048]{1,0:T(8,128)(2,1)}), bf16[2048,2048]{1,0:T(8,128)(2,1)}) %all-gather.7.cloned.1.call-update) | async-done | bytes 8388624 | tf_op jit(solution)/shard_map/all_gather | solution.py:61
  156.3 17.3 %fusion.2 = (bf16[512,2048]{1,0:T(8,128)(2,1)S(1)}, f32[512,2048]{1,0:T(8,128)}) fusion(bf16[512,2048]{1,0:T(8,128)(2,1)} %all-gather.5.cloned.1.call-done, bf16[2048,2048]{1,0:T(8,128)(2,1)} %all-gather.7.cloned.1.call-done), kind=kOutput, calls=%fused_computation.6 | convolution fusion | flops 4363124736 | bytes 16777216 | tf_op jit(solution)/shard_map/dot_general | solution.py:63
  173.5 39.0 %all-gather.9.cloned.1.call-done = bf16[2048,2048]{1,0:T(8,128)(2,1)} async-done(((bf16[256,2048]{1,0:T(8,128)(2,1)}), bf16[2048,2048]{1,0:T(8,128)(2,1)}) %all-gather.9.cloned.1.call-update) | async-done | bytes 8388624 | tf_op jit(solution)/shard_map/all_gather | solution.py:62
  212.6 9.2 %convolution_convert_fusion.3 = bf16[512,2048]{1,0:T(8,128)(2,1)} fusion(bf16[512,2048]{1,0:T(8,128)(2,1)S(1)} %get-tuple-element.65, bf16[2048,2048]{1,0:T(8,128)(2,1)} %all-gather.9.cloned.1.call-done), kind=kOutput, calls=%fused_computation.29 | convolution fusion | flops 4296015872 | bytes 12582912 | tf_op jit(solution)/shard_map/dot_general | solution.py:65
  221.8 44.0 %reduce-scatter.5.cloned.1.call-done = bf16[512,512]{1,0:T(8,128)(2,1)} async-done(((bf16[512,2048]{1,0:T(8,128)(2,1)}), bf16[512,512]{1,0:T(8,128)(2,1)}) %reduce-scatter.5.cloned.1.call-update) | async-done | bytes 524304 | tf_op jit(solution)/shard_map/reduce_scatter | solution.py:66
  265.8 2.3 fusion.199
  268.4 45.1 %all-gather.11.cloned.1.call-done = bf16[512,2048]{1,0:T(8,128)(2,1)} async-done(((bf16[512,512]{1,0:T(8,128)(2,1)}), bf16[512,2048]{1,0:T(8,128)(2,1)}) %all-gather.11.cloned.1.call-update) | async-done | bytes 2097168 | tf_op jit(solution)/shard_map/all_gather | solution.py:73
  313.5 9.1 %fusion.8 = bf16[512,2048]{1,0:T(8,128)(2,1)S(1)} fusion(f32[512,2048]{1,0:T(8,128)} %get-tuple-element.66, bf16[512,2048]{1,0:T(8,128)(2,1)} %all-gather.11.cloned.1.call-done, bf16[2048,2048]{1,0:T(8,128)(2,1)} %all-gather.9.cloned.1.call-done), kind=kOutput, calls=%fused_computation.12 | convolution fusion | flops 4305453056 | bytes 16777216 | tf_op jit(solution)/shard_map/dot_general | solution.py:82
  324.0 9.3 %convolution_convert_fusion.2 = bf16[512,2048]{1,0:T(8,128)(2,1)} fusion(bf16[512,2048]{1,0:T(8,128)(2,1)S(1)} %fusion.8, bf16[2048,2048]{1,0:T(8,128)(2,1)} %all-gather.7.cloned.1.call-done), kind=kOutput, calls=%fused_computation.28 | convolution fusion | flops 4296015872 | bytes 12582912 | tf_op jit(solution)/shard_map/dot_general | solution.py:92
  333.3 8.4 %convolution_convert_fusion.1 = bf16[2048,2048]{1,0:T(8,128)(2,1)} fusion(bf16[512,2048]{1,0:T(8,128)(2,1)S(1)} %copy-done.5, bf16[512,2048]{1,0:T(8,128)(2,1)} %copy-done.8), kind=kOutput, calls=%fused_computation.1 | convolution fusion | flops 4299161600 | bytes 12582912 | tf_op jit(solution)/shard_map/dot_general | solution.py:85
  341.8 1.5 copy-done.6
  343.3 8.3 %convolution_convert_fusion = bf16[2048,2048]{1,0:T(8,128)(2,1)} fusion(bf16[512,2048]{1,0:T(8,128)(2,1)S(1)} %copy-done.6, bf16[512,2048]{1,0:T(8,128)(2,1)} %copy-done.7), kind=kOutput, calls=%fused_computation | convolution fusion | flops 4299161600 | bytes 12582912 | tf_op jit(solution)/shard_map/dot_general | solution.py:75
  351.6 24.4 %reduce-scatter.7.cloned.1.call-done = bf16[512,512]{1,0:T(8,128)(2,1)} async-done(((bf16[512,2048]{1,0:T(8,128)(2,1)}), bf16[512,512]{1,0:T(8,128)(2,1)}) %reduce-scatter.7.cloned.1.call-update) | async-done | bytes 524304 | tf_op jit(solution)/shard_map/reduce_scatter | solution.py:95
  377.5 9.8 %all-reduce.2 = (f32[512]{0:T(512)S(1)}, f32[512]{0:T(512)S(1)}) all-reduce(f32[512]{0:T(512)S(1)} %get-tuple-element.5, f32[512]{0:T(512)S(1)} %get-tuple-element.4), channel_id=1, replica_groups=mesh['row'=8,'col'=4] {'col'}, use_global_device_ids=true, to_apply=%region_9.10 | all-reduce | flops 1024 | bytes 8192 | tf_op jit(solution)/shard_map/psum | solution.py:99
  391.6 4.2 collective-permute-done.3
  395.9 8.5 %fusion.193 = bf16[2,4,64,512]{3,2,1,0:T(8,128)(2,1)} fusion(f32[2,10,64,512]{3,2,1,0:T(8,128)S(1)} %maximum_convert_fusion.1, f32[512]{0:T(512)S(1)} %bitcast.140, f32[512]{0:T(512)S(1)} %bitcast.142, f32[512]{0:T(512)S(1)} %bitcast.86, f32[512]{0:T(512)S(1)} %bitcast.88, f32[512]{0:T(512)S(1)} %bitcast.90, f32[512]{0:T(512)S(1)} %bitcast.92, ...), kind=kLoop, calls=%fused_computation.293 | loop fusion | flops 26214400 | bytes 11110400 | tf_op jit(solution)/shard_map/convert_element_type | solution.py:109
  404.4 46.2 %reduce-scatter.9.cloned.1.call-done = bf16[256,2048]{1,0:T(8,128)(2,1)} async-done(((bf16[2048,2048]{1,0:T(8,128)(2,1)}), bf16[256,2048]{1,0:T(8,128)(2,1)}) %reduce-scatter.9.cloned.1.call-update) | async-done | bytes 1048592 | tf_op jit(solution)/shard_map/reduce_scatter | solution.py:84
  450.6 75.7 %reduce-scatter.11.cloned.1.call-done = bf16[256,2048]{1,0:T(8,128)(2,1)} async-done(((bf16[2048,2048]{1,0:T(8,128)(2,1)}), bf16[256,2048]{1,0:T(8,128)(2,1)}) %reduce-scatter.11.cloned.1.call-update) | async-done | bytes 1048592 | tf_op jit(solution)/shard_map/reduce_scatter | solution.py:74
  (55 shorter events, 19.2 us)
Async XLA Ops:
  7.2 94.1 %all-gather.5.cloned.1.call-start = ((), (), s32[]{:S(2)}) async-start(), calls=%async_computation.4 | async-start | bytes 2621440 | tf_op jit(solution)/shard_map/all_gather | solution.py:60
  8.4 6.9 %collective-permute-start = (bf16[2,3,64,512]{3,2,1,0:T(8,128)(2,1)S(1)}, bf16[2,3,64,512]{3,2,1,0:T(8,128)(2,1)S(1)}, u32[]{:S(2)}, u32[]{:S(2)}) collective-permute-start(bf16[2,3,64,512]{3,2,1,0:T(8,128)(2,1)S(1)} %get-tuple-element.12), channel_id=1, source_target_pairs={{0,4},{4,8},{8,12},{12,16},{16,20},{20,24},{24,28},{1,5},{5,9},{9,... | collective-permute-start | bytes 1179656 | tf_op jit(solution)/shard_map/ppermute | solution.py:15
  10.8 5.7 %collective-permute-start.1 = (bf16[2,3,64,512]{3,2,1,0:T(8,128)(2,1)S(1)}, bf16[2,3,64,512]{3,2,1,0:T(8,128)(2,1)S(1)}, u32[]{:S(2)}, u32[]{:S(2)}) collective-permute-start(bf16[2,3,64,512]{3,2,1,0:T(8,128)(2,1)S(1)} %get-tuple-element.13), channel_id=1, source_target_pairs={{4,0},{8,4},{12,8},{16,12},{20,16},{24,20},{28,24},{5,1},{9,5},{13... | collective-permute-start | bytes 1179656 | tf_op jit(solution)/shard_map/ppermute | solution.py:18
  17.7 30.7 %copy-start.3 = (f32[512]{0:T(512)S(1)}, f32[512]{0:T(512)}, u32[]{:S(2)}) copy-start(f32[512]{0:T(512)} %param.9) | copy-start | bytes 6148
  50.7 105.5 %all-gather.7.cloned.1.call-start = ((), (), s32[]{:S(2)}) async-start(), calls=%async_computation.5 | async-start | bytes 9437184 | tf_op jit(solution)/shard_map/all_gather | solution.py:61
  51.5 161.1 %all-gather.9.cloned.1.call-start = ((), (), s32[]{:S(2)}) async-start(), calls=%async_computation.6 | async-start | bytes 9437184 | tf_op jit(solution)/shard_map/all_gather | solution.py:62
  52.2 213.6 %reduce-scatter.5.cloned.1.call-start = ((), (), s32[]{:S(2)}) async-start(), calls=%async_computation.7 | async-start | bytes 2621440 | tf_op jit(solution)/shard_map/reduce_scatter | solution.py:66
  173.5 48.2 %copy-start.7 = (bf16[512,2048]{1,0:T(8,128)(2,1)}, bf16[512,2048]{1,0:T(8,128)(2,1)S(1)}, u32[]{:S(2)}) copy-start(bf16[512,2048]{1,0:T(8,128)(2,1)S(1)} %get-tuple-element.65) | copy-start | bytes 6291460
  212.6 53.3 %copy-start.1 = (bf16[2,4,64,512]{3,2,1,0:T(8,128)(2,1)S(1)}, bf16[2,4,64,512]{3,2,1,0:T(8,128)(2,1)}, u32[]{:S(2)}) copy-start(bf16[2,4,64,512]{3,2,1,0:T(8,128)(2,1)} %param.7) | copy-start | bytes 1572868
  212.6 53.3 %copy-start.2 = (bf16[2,4,64,512]{3,2,1,0:T(8,128)(2,1)S(1)}, bf16[2,4,64,512]{3,2,1,0:T(8,128)(2,1)}, u32[]{:S(2)}) copy-start(bf16[2,4,64,512]{3,2,1,0:T(8,128)(2,1)} %param.13) | copy-start | bytes 1572868
  212.6 53.3 %copy-start.4 = (f32[512]{0:T(512)S(1)}, f32[512]{0:T(512)}, u32[]{:S(2)}) copy-start(f32[512]{0:T(512)} %param.12) | copy-start | bytes 6148
  221.8 91.8 %all-gather.11.cloned.1.call-start = ((), (), s32[]{:S(2)}) async-start(), calls=%async_computation.8 | async-start | bytes 2621440 | tf_op jit(solution)/shard_map/all_gather | solution.py:73
  268.1 107.9 %reduce-scatter.7.cloned.1.call-start = ((), (), s32[]{:S(2)}) async-start(), calls=%async_computation.9 | async-start | bytes 2621440 | tf_op jit(solution)/shard_map/reduce_scatter | solution.py:95
  322.6 1.3 copy-start.8
  324.0 9.4 %copy-start.5 = (bf16[512,2048]{1,0:T(8,128)(2,1)S(1)}, bf16[512,2048]{1,0:T(8,128)(2,1)}, u32[]{:S(2)}) copy-start(bf16[512,2048]{1,0:T(8,128)(2,1)} %all-gather.5.cloned.1.call-done) | copy-start | bytes 6291460
  333.3 117.4 %reduce-scatter.9.cloned.1.call-start = ((), (), s32[]{:S(2)}) async-start(), calls=%async_computation.10 | async-start | bytes 9437184 | tf_op jit(solution)/shard_map/reduce_scatter | solution.py:84
  341.7 1.6 copy-start.6
  341.7 184.7 %reduce-scatter.11.cloned.1.call-start = ((), (), s32[]{:S(2)}) async-start(), calls=%async_computation.11 | async-start | bytes 9437184 | tf_op jit(solution)/shard_map/reduce_scatter | solution.py:74
  351.6 24.4 %copy-start = (f32[2,4,64,512]{3,2,1,0:T(8,128)S(1)}, f32[2,4,64,512]{3,2,1,0:T(8,128)}, u32[]{:S(2)}) copy-start(f32[2,4,64,512]{3,2,1,0:T(8,128)} %get-tuple-element.9) | copy-start | bytes 3145732
  388.9 2.6 collective-permute-start.2
  390.2 5.5 %collective-permute-start.3 = (bf16[2,3,64,512]{3,2,1,0:T(8,128)(2,1)S(1)}, bf16[2,3,64,512]{3,2,1,0:T(8,128)(2,1)S(1)}, u32[]{:S(2)}, u32[]{:S(2)}) collective-permute-start(bf16[2,3,64,512]{3,2,1,0:T(8,128)(2,1)S(1)} %get-tuple-element.11), channel_id=1, source_target_pairs={{4,0},{8,4},{12,8},{16,12},{20,16},{24,20},{28,24},{5,1},{9,5},{13... | collective-permute-start | bytes 1179656 | tf_op jit(solution)/shard_map/ppermute | solution.py:18
Sparse Core Ops, SparseCore 0:
  50.8 50.3 all-gather.4
  103.1 53.0 all-gather.6
  158.2 54.3 all-gather.8
  221.9 43.8 reduce-scatter.4
  268.2 45.2 all-gather.10
  333.4 42.5 reduce-scatter.6
  380.0 70.5 reduce-scatter.8
  455.1 71.2 reduce-scatter.10
where the time goes:
time: 534 us; the launch traced here: 533 us
  waiting for transfers between devices  385 us (72%)
  matrix products  61.5 us (12%)
  blocking collectives  30.1 us (6%)
  other arithmetic  27.6 us (5%)
  between operations  14.3 us (3%)
  local copies, waits for them, and re-layouts  7.51 us (1%)
  starting transfers between devices  7 us (1%)
    reduce_scatter x1, waiting for transfers between devices, on_device(): lax.psum_scatter(lax.dot_general(full_grad, hidden, contract_first, prefe...  75.7 us
    all_gather x1, waiting for transfers between devices, on_device(): in_panel = lax.all_gather(proj_in, 'row', axis=0, tiled=True)  55 us
    all_gather x1, waiting for transfers between devices, on_device(): full_in = lax.all_gather(scaled, 'col', axis=1, tiled=True)  48.8 us
    reduce_scatter x1, waiting for transfers between devices, on_device(): lax.psum_scatter(lax.dot_general(full_in, grad_pre, contract_first, prefe...  46.2 us
    all_gather x1, waiting for transfers between devices, on_device(): full_grad = lax.all_gather(grad_branch, 'col', axis=1, tiled=True)  45.1 us
    reduce_scatter x1, waiting for transfers between devices, on_device(): lax.psum_scatter(contrib.astype(jnp.bfloat16), 'col', scatter_dimension=1...  44 us
    all_gather x1, waiting for transfers between devices, on_device(): out_panel = lax.all_gather(proj_out, 'row', axis=0, tiled=True)  39 us
    reduce_scatter x1, waiting for transfers between devices, on_device(): lax.psum_scatter(back_part.astype(jnp.bfloat16), 'col', scatter_dimension...  24.4 us
  transfers between devices with their start and end apart: 12, of which 10 were waited for; matrix products, arithmetic and copies ran while one was open for 9% of the time, Pallas kernels for 0%

commit v1 on v0

v1 whole, which is shorter than its diff:
```python
import jax
import jax.numpy as jnp
from jax import lax
from jax.sharding import PartitionSpec as P

C = 2048
KS = 7
F32 = jnp.float32
BF16 = jnp.bfloat16


def taps_sum(padded, dw_kernel, img_rows, img_cols, flipped):
    total = jnp.zeros(padded.shape[:1] + (img_rows, img_cols) + padded.shape[3:], F32)
    reach = 2 * (KS // 2)
    for tap_row in range(KS):
        for tap_col in range(KS):
            off_row = reach - tap_row if flipped else tap_row
            off_col = reach - tap_col if flipped else tap_col
            total = (
                total
                + dw_kernel[tap_row, tap_col]
                * padded[:, off_row : off_row + img_rows, off_col : off_col + img_cols, :]
            )
    return total


def with_halo(block, width):
    count = lax.axis_size("row")
    forward = [(i, i + 1) for i in range(count - 1)]
    backward = [(target, source) for source, target in forward]
    low = lax.ppermute(block[:, -width:], "row", forward)
    high = lax.ppermute(block[:, :width], "row", backward)
    return jnp.concatenate([low, block, high], axis=1)


def gelu_slope(values):
    return (
        0.5 * (1.0 + lax.erf(values * 0.7071067811865476))
        + values * jnp.exp(-0.5 * values * values) * 0.3989422804014327
    )


class Ring:
    def __init__(self):
        count = lax.axis_size("row")
        chips = count // 2
        half = chips // 2
        order = list(range(half)) + list(range(chips - 1, half - 1, -1))
        self.chips = chips
        self.order = jnp.array(order, jnp.int32)
        self.sibling = [(i, i ^ 1) for i in range(count)]
        self.ahead, self.behind = [], []
        for place, chip in enumerate(order):
            after, before = order[(place + 1) % chips], order[(place - 1) % chips]
            self.ahead += [(2 * chip, 2 * after), (2 * chip + 1, 2 * before + 1)]
            self.behind += [(2 * chip, 2 * before), (2 * chip + 1, 2 * after + 1)]
        index = lax.axis_index("row")
        self.core = index % 2
        places = [order.index(chip) for chip in range(chips)]
        self.place = jnp.array(places, jnp.int32)[index // 2]
        self.sense = 1 - 2 * self.core
        self.groups = [list(range(0, count, 2)), list(range(1, count, 2))]

    def chip_at(self, steps):
        return self.order[(self.place + self.sense * steps + self.chips) % self.chips]

    def swap(self, block):
        return lax.ppermute(block, "row", self.sibling)

    def gather(self, block):
        half = self.chips // 2
        panel = jnp.zeros((self.chips,) + block.shape, block.dtype)
        panel = lax.dynamic_update_index_in_dim(panel, block, self.chip_at(0), 0)
        one, two = block, block
        for step in range(1, half + 1):
            one = lax.ppermute(one, "row", self.ahead)
            panel = lax.dynamic_update_index_in_dim(panel, one, self.chip_at(-step), 0)
            if step < half:
                two = lax.ppermute(two, "row", self.behind)
                panel = lax.dynamic_update_index_in_dim(panel, two, self.chip_at(step), 0)
        return panel.reshape(-1, block.shape[-1])

    def scatter(self, whole):
        half = self.chips // 2
        parts = whole.reshape(self.chips, -1, whole.shape[-1])

        def part(steps):
            return lax.dynamic_index_in_dim(parts, self.chip_at(steps), 0, False).astype(F32)

        one = part(-half)
        two = part(half - 1)
        for step in range(half - 1, 0, -1):
            one = lax.ppermute(one.astype(BF16), "row", self.behind).astype(F32) + part(-step)
            if step < half - 1:
                two = lax.ppermute(two.astype(BF16), "row", self.ahead).astype(F32) + part(step)
        one = lax.ppermute(one.astype(BF16), "row", self.behind).astype(F32)
        if half > 1:
            two = lax.ppermute(two.astype(BF16), "row", self.ahead).astype(F32)
        else:
            two = 0.0
        return one + two + part(0)


def chip_block(ring, weight):
    width = weight.shape[1] // 2
    keep = lax.dynamic_slice_in_dim(weight, ring.core * width, width, 1)
    give = lax.dynamic_slice_in_dim(weight, (1 - ring.core) * width, width, 1)
    other = ring.swap(give)
    return jnp.where(
        ring.core == 0,
        jnp.concatenate([keep, other], axis=0),
        jnp.concatenate([other, keep], axis=0),
    )


def own_rows(ring, block):
    rows = block.shape[0] // 2
    keep = lax.dynamic_slice_in_dim(block, ring.core * rows, rows, 0)
    give = lax.dynamic_slice_in_dim(block, (1 - ring.core) * rows, rows, 0)
    other = ring.swap(give)
    return jnp.where(
        ring.core == 0,
        jnp.concatenate([keep, other], axis=1),
        jnp.concatenate([other, keep], axis=1),
    )


UP = [(0, 1), (1, 2), (2, 3)]
DOWN = [(1, 0), (2, 1), (3, 2)]
ACROSS = [(0, 2), (1, 3), (2, 0), (3, 1)]


def col_gather(block):
    count = lax.axis_size("col")
    if count != 4:
        return lax.all_gather(block, "col", axis=1, tiled=True)
    z = lax.axis_index("col")
    across = lax.ppermute(block, "col", ACROSS)
    below = lax.ppermute(block, "col", UP)
    above = lax.ppermute(block, "col", DOWN)
    far = lax.ppermute(across, "col", [(1, 0), (2, 3)])
    below = jnp.where(z == 0, far, below)
    above = jnp.where(z == 3, far, above)
    width = block.shape[1]
    full = jnp.zeros((block.shape[0], width * count), block.dtype)
    for shift, part in ((0, block), (1, above), (2, across), (3, below)):
        full = lax.dynamic_update_slice_in_dim(full, part, (z + shift) % count * width, 1)
    return full


def col_scatter(whole):
    count = lax.axis_size("col")
    if count != 4:
        return lax.psum_scatter(whole, "col", scatter_dimension=1, tiled=True).astype(F32)
    z = lax.axis_index("col")
    width = whole.shape[1] // count

    def part(index):
        return lax.dynamic_slice_in_dim(whole, index * width, width, 1)

    far = lax.ppermute(part(3 - z), "col", [(0, 1), (3, 2)])
    below = lax.ppermute(part(jnp.minimum(z + 1, 3)), "col", UP)
    above = lax.ppermute(part(jnp.maximum(z - 1, 0)), "col", DOWN)
    pair = (part((z + 2) % count).astype(F32) + far.astype(F32)).astype(BF16)
    across = lax.ppermute(pair, "col", ACROSS)
    return part(z).astype(F32) + below.astype(F32) + above.astype(F32) + across.astype(F32)


def col_all(small):
    count = lax.axis_size("col")
    shifts = [
        lax.ppermute(small, "col", [(i, (i + step) % count) for i in range(count)])
        for step in range(1, count)
    ]
    return jnp.stack([small] + shifts)


def on_device(images, dw_kernel, norm_gain, proj_in, proj_out, layer_scale, cotangent):
    img_batch, strip_rows, img_cols, local_ch = images.shape
    pixels = img_batch * strip_rows * img_cols
    reach = KS // 2
    contract_last = (((1,), (1,)), ((), ()))
    contract_first = (((0,), (0,)), ((), ()))
    ring = Ring()

    in_panel = ring.gather(chip_block(ring, proj_in))
    out_panel = lax.all_gather(
        chip_block(ring, proj_out), "row", axis=0, tiled=True, axis_index_groups=ring.groups
    )
    cot_flat = cotangent.reshape(pixels, local_ch).astype(F32)
    grad_branch = (cot_flat * layer_scale).astype(BF16)
    strip_grad = col_gather(grad_branch)
    full_grad = jnp.concatenate([strip_grad, ring.swap(strip_grad)], axis=0)

    rimmed = with_halo(images, reach)
    padded = jnp.pad(rimmed.astype(F32), ((0, 0), (0, 0), (reach, reach), (0, 0)))
    conv_out = taps_sum(padded, dw_kernel, strip_rows, img_cols, False).reshape(pixels, local_ch)
    own_mean = jnp.mean(conv_out, axis=1)
    own_dev = conv_out - own_mean[:, None]
    stats = col_all(jnp.stack([own_mean, jnp.sum(own_dev * own_dev, axis=1)]))
    row_mean = jnp.mean(stats[:, 0], axis=0)
    spread = stats[:, 0] - row_mean
    row_var = jnp.sum(stats[:, 1] + local_ch * (spread * spread), axis=0) / C
    inv_std = lax.rsqrt(row_var + 1e-06)
    normed = (conv_out - row_mean[:, None]) * inv_std[:, None]
    scaled = (normed * norm_gain).astype(BF16)
    strip_in = col_gather(scaled)
    full_in = jnp.concatenate([strip_in, ring.swap(strip_in)], axis=0)

    hidden_pre = jnp.dot(full_in, in_panel, preferred_element_type=F32)
    hidden = jax.nn.gelu(hidden_pre, approximate=False).astype(BF16)
    out_part = lax.dot_general(
        full_grad, hidden, contract_first, preferred_element_type=F32
    ).astype(BF16)
    out_rows = lax.psum_scatter(
        out_part, "row", scatter_dimension=0, tiled=True, axis_index_groups=ring.groups
    )
    grad_hidden = jnp.dot(full_grad, out_panel, preferred_element_type=F32)
    grad_pre = (grad_hidden * gelu_slope(hidden_pre)).astype(BF16)

    def strip_sum(both):
        both = both.astype(BF16)
        other = ring.swap(both[pixels:])
        return (both[:pixels].astype(F32) + other.astype(F32)).astype(BF16)

    back_part = lax.dot_general(grad_pre, in_panel, contract_last, preferred_element_type=F32)
    grad_scaled = col_scatter(strip_sum(back_part))
    in_part = lax.dot_general(
        full_in, grad_pre, contract_first, preferred_element_type=F32
    ).astype(BF16)
    in_rows = ring.scatter(in_part)
    contrib = lax.dot_general(hidden, out_panel, contract_last, preferred_element_type=F32)
    branch = col_scatter(strip_sum(contrib))
    residual_in = images.reshape(pixels, local_ch).astype(F32)
    block_out = (residual_in + layer_scale * branch).astype(BF16).reshape(images.shape)

    weighted = grad_scaled * norm_gain
    sums = jnp.sum(
        col_all(jnp.stack([jnp.sum(weighted, axis=1), jnp.sum(weighted * normed, axis=1)])), axis=0
    )
    grad_conv = inv_std[:, None] * (
        weighted - sums[0][:, None] / C - normed * sums[1][:, None] / C
    )
    grad_conv = grad_conv.reshape(images.shape)
    grad_rim = with_halo(grad_conv.astype(BF16), reach).astype(F32)
    grad_pad = jnp.pad(grad_rim, ((0, 0), (0, 0), (reach, reach), (0, 0)))
    input_grad = taps_sum(grad_pad, dw_kernel, strip_rows, img_cols, True)
    grad_images = (cotangent.astype(F32) + input_grad).astype(BF16)
    return (
        block_out,
        grad_images,
        own_rows(ring, in_rows.astype(BF16)),
        own_rows(ring, out_rows),
    )


def solution(mesh):
    placed = (
        P(None, "row", None, "col"),
        P(None, None, "col"),
        P("col"),
        P("row", "col"),
        P("row", "col"),
        P("col"),
        P(None, "row", None, "col"),
    )
    return jax.shard_map(
        on_device,
        mesh=mesh,
        in_specs=placed,
        out_specs=(
            P(None, "row", None, "col"),
            P(None, "row", None, "col"),
            P("row", "col"),
            P("row", "col"),
        ),
        check_vma=False,
    )
```

time: 534 us -> 445 us (0.83); the launches traced: 533 us -> 436 us
  waiting for transfers between devices: 385 us -> 204 us
  starting transfers between devices: 7 us -> 80.6 us
  blocking collectives: 30.1 us -> 0 us
  other arithmetic: 27.6 us -> 49.7 us
  local copies, waits for them, and re-layouts: 7.51 us -> 27 us
  matrix products: 61.5 us -> 49.2 us
  between operations: 14.3 us -> 25.5 us
    ppermute x4 -> x40, waiting for transfers between devices: 5.4 us -> 204 us  [the longest x2 46.9 us: col_gather(): across = lax.ppermute(block, 'col', ACROSS)]
    reduce_scatter x4 -> x1, waiting for transfers between devices: 190 us -> 0.02 us  [on_device(): lax.psum_scatter(out_part, 'row', scatter_dimension=0, tiled=True, axis_i...]
    all_gather x4 -> x1, waiting for transfers between devices: 188 us -> 0.01 us  [on_device(): lax.all_gather(chip_block(ring, proj_out), 'row', axis=0, tiled=True, axi...]
    ppermute x4 -> x40, starting transfers between devices: 6.28 us -> 80.5 us  [the longest x6 12.1 us: col_all(): lax.ppermute(small, 'col', [(i, (i + step) % count) for i in range(count)])]
    psum x3 -> x0, blocking collectives: 30.1 us -> none  [the longest x1 11.9 us: on_device(): row_mean = lax.psum(jnp.sum(conv_out, axis=1), 'col') / C]
    select_n x0 -> x4, other arithmetic: none -> 8.38 us  [the longest x2 4.45 us: chip_block(): jnp.where(ring.core == 0, jnp.concatenate([keep, other], axis=0), jnp.con...]
    dynamic_slice x0 -> x8, local copies, waits for them, and re-layouts: none -> 7.6 us  [the longest x2 2.29 us: part(): return lax.dynamic_slice_in_dim(whole, index * width, width, 1)]
    convert_element_type x6 -> x11, other arithmetic: 15.9 us -> 23.4 us  [the longest x1 9.38 us: on_device(): grad_images = (cotangent.astype(F32) + input_grad).astype(BF16)]
  transfers between devices with their start and end apart: 12 -> 42, of which waited for: 10 -> 23; matrix products, arithmetic and copies ran while one was open for 9% -> 18% of each run, Pallas kernels for 0% -> 0%
where the time goes in v1:
time: 445 us; the launch traced here: 436 us
  waiting for transfers between devices  204 us (46%)
  starting transfers between devices  80.6 us (18%)
  other arithmetic  49.7 us (11%)
  matrix products  49.2 us (11%)
  local copies, waits for them, and re-layouts  27 us (6%)
  between operations  25.5 us (6%)
    ppermute x2, waiting for transfers between devices, col_gather(): across = lax.ppermute(block, 'col', ACROSS)  46.9 us
    ppermute x2, waiting for transfers between devices, gather(): one = lax.ppermute(one, 'row', self.ahead)  39.8 us
    ppermute x1, waiting for transfers between devices, scatter(): lax.ppermute(one.astype(BF16), 'row', self.behind).astype(F32) + part(-step)  39.4 us
    ppermute x2, waiting for transfers between devices, col_scatter(): across = lax.ppermute(pair, 'col', ACROSS)  26.7 us
    dot_general x1, matrix products, on_device(): hidden_pre = jnp.dot(full_in, in_panel, preferred_element_type=F32)  15.2 us
    ppermute x2, waiting for transfers between devices, col_scatter(): above = lax.ppermute(part(jnp.maximum(z - 1, 0)), 'col', DOWN)  13.3 us
    ppermute x6, starting transfers between devices, col_all(): lax.ppermute(small, 'col', [(i, (i + step) % count) for i in range(count)])  12.1 us
    ppermute x2, waiting for transfers between devices, col_scatter(): far = lax.ppermute(part(3 - z), 'col', [(0, 1), (3, 2)])  10.9 us
  transfers between devices with their start and end apart: 42, of which 23 were waited for; matrix products, arithmetic and copies ran while one was open for 18% of the time, Pallas kernels for 0%

profile of v1, /device:TPU:0, one launch (start us, length us, event | category | flops | bytes accessed | tf_op | source)
XLA Modules:
  0.0 436.4 jit_solution(3593174222906048053)
XLA Ops:
  17.3 8.7 %fusion.217 = (f32[2,4,64]{2,1,0:T(4,128)S(1)}, f32[2,4,64,512]{3,2,1,0:T(8,128)}) fusion(f32[512]{0:T(512)S(1)} %bitcast.194, f32[512]{0:T(512)S(1)} %bitcast.196, f32[512]{0:T(512)S(1)} %bitcast.140, f32[2,10,64,512]{3,2,1,0:T(8,128)S(1)} %maximum_convert_fusion, f32[512]{0:T(512)S(1)} %bitcast.142, f32[512]{0:T(512)S(1)} %bitcast.144, ...), kind=kLoop, calls=%fused_computation.389 | loop fusion | flops 25689600 | bytes 11112448 | tf_op jit(solution)/shard_map/reduce_sum | solution.py:198
  27.7 5.1 %collective-permute-start.4 = (f32[2,512]{1,0:T(2,128)S(1)}, f32[2,512]{1,0:T(2,128)S(1)}, u32[]{:S(2)}, u32[]{:S(2)}) collective-permute-start(f32[2,512]{1,0:T(2,128)S(1)} %get-tuple-element.84), channel_id=1, source_target_pairs={{0,3},{1,0},{2,1},{3,2},{4,7},{5,4},{6,5},{7,6},{8,11},{9,8},{10,9... | collective-permute-start | bytes 12296 | tf_op jit(solution)/shard_map/ppermute | solution.py:172
  45.7 21.3 %collective-permute-done.5 = bf16[512,512]{1,0:T(8,128)(2,1)} collective-permute-done((bf16[512,512]{1,0:T(8,128)(2,1)}, bf16[512,512]{1,0:T(8,128)(2,1)}, u32[]{:S(2)}, u32[]{:S(2)}) %collective-permute-start.5) | collective-permute-done | bytes 524320 | tf_op jit(solution)/shard_map/ppermute | solution.py:138
  71.4 5.4 %collective-permute-start.8 = (bf16[512,512]{1,0:T(8,128)(2,1)}, bf16[512,512]{1,0:T(8,128)(2,1)S(1)}, u32[]{:S(2)}, u32[]{:S(2)}) collective-permute-start(bf16[512,512]{1,0:T(8,128)(2,1)} %get-tuple-element.92), channel_id=1, source_target_pairs={{0,1},{1,2},{2,3},{4,5},{5,6},{6,7},{8,9},{9,10},{10,11},{12,13},{... | collective-permute-start | bytes 1572872 | tf_op jit(solution)/shard_map/ppermute | solution.py:139
  93.7 22.6 %collective-permute-done.11 = bf16[512,1024]{1,0:T(8,128)(2,1)} collective-permute-done((bf16[512,1024]{1,0:T(8,128)(2,1)}, bf16[512,1024]{1,0:T(8,128)(2,1)}, u32[]{:S(2)}, u32[]{:S(2)}) %collective-permute-start.11) | collective-permute-done | bytes 1048608 | tf_op jit(solution)/shard_map/ppermute | solution.py:76
  134.2 17.2 %collective-permute-done.13 = bf16[512,1024]{1,0:T(8,128)(2,1)} collective-permute-done((bf16[512,1024]{1,0:T(8,128)(2,1)}, bf16[512,1024]{1,0:T(8,128)(2,1)}, u32[]{:S(2)}, u32[]{:S(2)}) %collective-permute-start.13) | collective-permute-done | bytes 1048608 | tf_op jit(solution)/shard_map/ppermute | solution.py:76
  154.9 15.2 %fusion.2 = (bf16[1024,1024]{1,0:T(8,128)(2,1)}, f32[1024,1024]{1,0:T(8,128)}) fusion(bf16[2048,1024]{1,0:T(8,128)(2,1)S(1)} %bitcast.130, bf16[512,2048]{1,0:T(8,128)(2,1)} %collective-permute-done.9, bf16[512,2048]{1,0:T(8,128)(2,1)S(1)} %select_dynamic-update-slice_fusion.2), kind=kOutput, calls=%fused_computation.4 | convolution fusion | flops 4371513344 | bytes 14680064 | tf_op jit(solution)/shard_map/dot_general | solution.py:210
  170.1 7.4 %convolution_convert_fusion.3 = bf16[1024,2048]{1,0:T(8,128)(2,1)S(1)} fusion(bf16[1024,1024]{1,0:T(8,128)(2,1)} %get-tuple-element.93, bf16[2048,1024]{1,0:T(8,128)(2,1)} %all-gather.2.cloned.1.call-done), kind=kOutput, calls=%fused_computation.33 | convolution fusion | flops 4297064448 | bytes 10485760 | tf_op jit(solution)/shard_map/dot_general | solution.py:232
  192.1 5.4 %collective-permute-start.16 = (bf16[512,512]{1,0:T(8,128)(2,1)}, bf16[512,512]{1,0:T(8,128)(2,1)}, u32[]{:S(2)}, u32[]{:S(2)}) collective-permute-start(bf16[512,512]{1,0:T(8,128)(2,1)} %get-tuple-element.14), channel_id=1, source_target_pairs={{0,1},{1,2},{2,3},{4,5},{5,6},{6,7},{8,9},{9,10},{10,11},{12,13},{... | collective-permute-start | bytes 1572872 | tf_op jit(solution)/shard_map/ppermute | solution.py:162
  197.5 5.6 %collective-permute-done.18 = bf16[512,512]{1,0:T(8,128)(2,1)S(1)} collective-permute-done((bf16[512,512]{1,0:T(8,128)(2,1)S(1)}, bf16[512,512]{1,0:T(8,128)(2,1)S(1)}, u32[]{:S(2)}, u32[]{:S(2)}) %collective-permute-start.18) | collective-permute-done | bytes 524320 | tf_op jit(solution)/shard_map/ppermute | solution.py:161
  205.9 8.9 %collective-permute-done.17 = bf16[512,512]{1,0:T(8,128)(2,1)} collective-permute-done((bf16[512,512]{1,0:T(8,128)(2,1)}, bf16[512,512]{1,0:T(8,128)(2,1)}, u32[]{:S(2)}, u32[]{:S(2)}) %collective-permute-start.17) | collective-permute-done | bytes 524320 | tf_op jit(solution)/shard_map/ppermute | solution.py:163
  214.8 14.0 %collective-permute-done.19 = bf16[512,512]{1,0:T(8,128)(2,1)} collective-permute-done((bf16[512,512]{1,0:T(8,128)(2,1)}, bf16[512,512]{1,0:T(8,128)(2,1)}, u32[]{:S(2)}, u32[]{:S(2)}) %collective-permute-start.19) | collective-permute-done | bytes 524320 | tf_op jit(solution)/shard_map/ppermute | solution.py:165
  232.9 25.6 %collective-permute-done.20 = bf16[512,512]{1,0:T(8,128)(2,1)S(1)} collective-permute-done((bf16[512,512]{1,0:T(8,128)(2,1)S(1)}, bf16[512,512]{1,0:T(8,128)(2,1)S(1)}, u32[]{:S(2)}, u32[]{:S(2)}) %collective-permute-start.20) | collective-permute-done | bytes 524320 | tf_op jit(solution)/shard_map/ppermute | solution.py:138
  259.8 4.8 %collective-permute-start.23 = (bf16[512,512]{1,0:T(8,128)(2,1)S(1)}, bf16[512,512]{1,0:T(8,128)(2,1)S(1)}, u32[]{:S(2)}, u32[]{:S(2)}) collective-permute-start(bf16[512,512]{1,0:T(8,128)(2,1)S(1)} %get-tuple-element.85), channel_id=1, source_target_pairs={{0,1},{1,2},{2,3},{4,5},{5,6},{6,7},{8,9},{9,10},{10,11},{12,13},{... | collective-permute-start | bytes 1572872 | tf_op jit(solution)/shard_map/ppermute | solution.py:139
  276.8 6.3 %convolution_convert_fusion = bf16[2048,1024]{1,0:T(8,128)(2,1)} fusion(bf16[1024,1024]{1,0:T(8,128)(2,1)S(1)} %copy-done.15, bf16[512,2048]{1,0:T(8,128)(2,1)S(1)} %collective-permute-done.24, bf16[512,2048]{1,0:T(8,128)(2,1)S(1)} %select_dynamic-update-slice_fusion), kind=kOutput, calls=%fused_computation.30 | convolution fusion | flops 4305453056 | bytes 10485760 | tf_op jit(solution)/shard_map/dot_general | solution.py:212
  283.2 9.0 %fusion.8 = bf16[1024,1024]{1,0:T(8,128)(2,1)S(1)} fusion(f32[1024,1024]{1,0:T(8,128)} %get-tuple-element.94, bf16[2048,1024]{1,0:T(8,128)(2,1)} %all-gather.2.cloned.1.call-done, bf16[512,2048]{1,0:T(8,128)(2,1)} %copy-done.14, bf16[512,2048]{1,0:T(8,128)(2,1)S(1)} %select_dynamic-update-slice_fusion), kind=kOutput, calls=%fused_computation.10 | convolution fusion | flops 4313841664 | bytes 14680064 | tf_op jit(solution)/shard_map/dot_general | solution.py:218
  292.2 4.8 %convolution_convert_fusion.2 = bf16[1024,2048]{1,0:T(8,128)(2,1)S(1)} fusion(bf16[1024,1024]{1,0:T(8,128)(2,1)S(1)} %fusion.8, bf16[2048,1024]{1,0:T(8,128)(2,1)S(1)} %bitcast.131), kind=kOutput, calls=%fused_computation.32 | convolution fusion | flops 4297064448 | bytes 10485760 | tf_op jit(solution)/shard_map/dot_general | solution.py:226
  298.6 6.6 %convolution_convert_fusion.1 = bf16[2048,1024]{1,0:T(8,128)(2,1)S(1)} fusion(bf16[1024,1024]{1,0:T(8,128)(2,1)S(1)} %fusion.8, bf16[512,2048]{1,0:T(8,128)(2,1)} %collective-permute-done.9, bf16[512,2048]{1,0:T(8,128)(2,1)S(1)} %copy-done.7), kind=kOutput, calls=%fused_computation.31 | convolution fusion | flops 4305453056 | bytes 10485760 | tf_op jit(solution)/shard_map/dot_general | solution.py:228
  308.7 39.4 %collective-permute-done.35 = bf16[512,1024]{1,0:T(8,128)(2,1)S(1)} collective-permute-done((bf16[512,1024]{1,0:T(8,128)(2,1)S(1)}, bf16[512,1024]{1,0:T(8,128)(2,1)S(1)}, u32[]{:S(2)}, u32[]{:S(2)}) %collective-permute-start.35) | collective-permute-done | bytes 1048608 | tf_op jit(solution)/shard_map/ppermute | solution.py:93
  357.5 5.4 %collective-permute-start.26 = (bf16[512,512]{1,0:T(8,128)(2,1)}, bf16[512,512]{1,0:T(8,128)(2,1)}, u32[]{:S(2)}, u32[]{:S(2)}) collective-permute-start(bf16[512,512]{1,0:T(8,128)(2,1)} %get-tuple-element.11), channel_id=1, source_target_pairs={{0,1},{1,2},{2,3},{4,5},{5,6},{6,7},{8,9},{9,10},{10,11},{12,13},{... | collective-permute-start | bytes 1572872 | tf_op jit(solution)/shard_map/ppermute | solution.py:162
  363.0 5.4 %collective-permute-done.28 = bf16[512,512]{1,0:T(8,128)(2,1)S(1)} collective-permute-done((bf16[512,512]{1,0:T(8,128)(2,1)S(1)}, bf16[512,512]{1,0:T(8,128)(2,1)S(1)}, u32[]{:S(2)}, u32[]{:S(2)}) %collective-permute-start.28) | collective-permute-done | bytes 524320 | tf_op jit(solution)/shard_map/ppermute | solution.py:161
  379.7 12.7 %collective-permute-done.29 = bf16[512,512]{1,0:T(8,128)(2,1)} collective-permute-done((bf16[512,512]{1,0:T(8,128)(2,1)}, bf16[512,512]{1,0:T(8,128)(2,1)}, u32[]{:S(2)}, u32[]{:S(2)}) %collective-permute-start.29) | collective-permute-done | bytes 524320 | tf_op jit(solution)/shard_map/ppermute | solution.py:165
  394.4 5.3 %collective-permute-start.32 = (f32[2,512]{1,0:T(2,128)S(1)}, f32[2,512]{1,0:T(2,128)S(1)}, u32[]{:S(2)}, u32[]{:S(2)}) collective-permute-start(f32[2,512]{1,0:T(2,128)S(1)} %pad_maximum_fusion.10), channel_id=1, source_target_pairs={{0,3},{1,0},{2,1},{3,2},{4,7},{5,4},{6,5},{7,6},{8,11},{9,8},{10,9... | collective-permute-start | bytes 12296 | tf_op jit(solution)/shard_map/ppermute | solution.py:172
  417.2 9.4 %fusion.197 = bf16[2,4,64,512]{3,2,1,0:T(8,128)(2,1)} fusion(f32[2,10,64,512]{3,2,1,0:T(8,128)S(1)} %maximum_convert_fusion.1, f32[512]{0:T(512)S(1)} %bitcast.195, f32[512]{0:T(512)S(1)} %bitcast.197, f32[512]{0:T(512)S(1)} %bitcast.141, f32[512]{0:T(512)S(1)} %bitcast.143, f32[512]{0:T(512)S(1)} %bitcast.145, f32[512]{0:T(512)S(1)} %bitcast.147, ...), kind=kLoop, calls=%fused_computation.303 | loop fusion | flops 26214400 | bytes 11110400 | tf_op jit(solution)/shard_map/convert_element_type | solution.py:248
  (161 shorter events, 139.7 us)
Async XLA Ops:
  7.2 162.9 %all-gather.2.cloned.1.call-start = ((), (), s32[]{:S(2)}) async-start(), calls=%async_computation.1 | async-start | bytes 5242880 | tf_op jit(solution)/shard_map/all_gather | solution.py:187
  40.8 26.2 %collective-permute-start.5 = (bf16[512,512]{1,0:T(8,128)(2,1)}, bf16[512,512]{1,0:T(8,128)(2,1)}, u32[]{:S(2)}, u32[]{:S(2)}) collective-permute-start(bf16[512,512]{1,0:T(8,128)(2,1)} %get-tuple-element.92), channel_id=1, source_target_pairs={{0,2},{1,3},{2,0},{3,1},{4,6},{5,7},{6,4},{7,5},{8,10},{9,11},{10,... | collective-permute-start | bytes 1572872 | tf_op jit(solution)/shard_map/ppermute | solution.py:138
  43.0 25.3 %collective-permute-start.14 = (bf16[256,1024]{1,0:T(8,128)(2,1)}, bf16[256,1024]{1,0:T(8,128)(2,1)}, u32[]{:S(2)}, u32[]{:S(2)}) collective-permute-start(bf16[256,1024]{1,0:T(8,128)(2,1)} %get-tuple-element.22), channel_id=1, source_target_pairs={{0,4},{4,0},{8,12},{12,8},{16,20},{20,16},{24,28},{28,24},{1,5},{5... | collective-permute-start | bytes 1572872 | tf_op jit(solution)/shard_map/ppermute | solution.py:68
  44.4 32.4 %collective-permute-start.10 = (bf16[256,1024]{1,0:T(8,128)(2,1)}, bf16[256,1024]{1,0:T(8,128)(2,1)S(1)}, u32[]{:S(2)}, u32[]{:S(2)}) collective-permute-start(bf16[256,1024]{1,0:T(8,128)(2,1)} %get-tuple-element.24), channel_id=1, source_target_pairs={{0,4},{4,0},{8,12},{12,8},{16,20},{20,16},{24,28},{28,24},{1,5},{5... | collective-permute-start | bytes 1572872 | tf_op jit(solution)/shard_map/ppermute | solution.py:68
  44.4 37.4 %collective-permute-start.7 = (bf16[512,512]{1,0:T(8,128)(2,1)}, bf16[512,512]{1,0:T(8,128)(2,1)}, u32[]{:S(2)}, u32[]{:S(2)}) collective-permute-start(bf16[512,512]{1,0:T(8,128)(2,1)} %get-tuple-element.92), channel_id=1, source_target_pairs={{1,0},{2,1},{3,2},{5,4},{6,5},{7,6},{9,8},{10,9},{11,10},{13,12},{... | collective-permute-start | bytes 1572872 | tf_op jit(solution)/shard_map/ppermute | solution.py:140
  67.0 16.3 %collective-permute-start.6 = (bf16[512,512]{1,0:T(8,128)(2,1)}, bf16[512,512]{1,0:T(8,128)(2,1)}, u32[]{:S(2)}, u32[]{:S(2)}) collective-permute-start(bf16[512,512]{1,0:T(8,128)(2,1)} %collective-permute-done.5), channel_id=1, source_target_pairs={{1,0},{2,3},{5,4},{6,7},{9,8},{10,11},{13,12},{14,15},{17,16},{18,... | collective-permute-start | bytes 1572872 | tf_op jit(solution)/shard_map/ppermute | solution.py:141
  71.3 340.2 %reduce-scatter.2.cloned.1.call-start = ((), (), s32[]{:S(2)}) async-start(), calls=%async_computation.2 | async-start | bytes 5242880 | tf_op jit(solution)/shard_map/reduce_scatter | solution.py:215
  71.4 16.8 %collective-permute-start.8 = (bf16[512,512]{1,0:T(8,128)(2,1)}, bf16[512,512]{1,0:T(8,128)(2,1)S(1)}, u32[]{:S(2)}, u32[]{:S(2)}) collective-permute-start(bf16[512,512]{1,0:T(8,128)(2,1)} %get-tuple-element.92), channel_id=1, source_target_pairs={{0,1},{1,2},{2,3},{4,5},{5,6},{6,7},{8,9},{9,10},{10,11},{12,13},{... | collective-permute-start | bytes 1572872 | tf_op jit(solution)/shard_map/ppermute | solution.py:139
  78.3 37.9 %collective-permute-start.11 = (bf16[512,1024]{1,0:T(8,128)(2,1)}, bf16[512,1024]{1,0:T(8,128)(2,1)}, u32[]{:S(2)}, u32[]{:S(2)}) collective-permute-start(bf16[512,1024]{1,0:T(8,128)(2,1)} %maximum_select_fusion.1), channel_id=1, source_target_pairs={{0,8},{4,20},{8,24},{12,4},{24,16},{28,12},{16,0},{20,28},{1,9},{5... | collective-permute-start | bytes 3145736 | tf_op jit(solution)/shard_map/ppermute | solution.py:76
  89.4 63.4 %collective-permute-start.9 = (bf16[512,2048]{1,0:T(8,128)(2,1)S(1)}, bf16[512,2048]{1,0:T(8,128)(2,1)}, u32[]{:S(2)}, u32[]{:S(2)}) collective-permute-start(bf16[512,2048]{1,0:T(8,128)(2,1)S(1)} %select_dynamic-update-slice_fusion.2), channel_id=1, source_target_pairs={{0,4},{4,0},{8,12},{12,8},{16,20},{20,16},{24,28},{28,24},{1,5},{5... | collective-permute-start | bytes 6291464 | tf_op jit(solution)/shard_map/ppermute | solution.py:68
  89.5 43.4 %collective-permute-start.12 = (bf16[512,1024]{1,0:T(8,128)(2,1)}, bf16[512,1024]{1,0:T(8,128)(2,1)}, u32[]{:S(2)}, u32[]{:S(2)}) collective-permute-start(bf16[512,1024]{1,0:T(8,128)(2,1)} %maximum_select_fusion.1), channel_id=1, source_target_pairs={{0,16},{4,12},{8,0},{12,28},{24,8},{28,20},{16,24},{20,4},{1,17},{... | collective-permute-start | bytes 3145736 | tf_op jit(solution)/shard_map/ppermute | solution.py:79
  116.2 35.3 %collective-permute-start.13 = (bf16[512,1024]{1,0:T(8,128)(2,1)}, bf16[512,1024]{1,0:T(8,128)(2,1)}, u32[]{:S(2)}, u32[]{:S(2)}) collective-permute-start(bf16[512,1024]{1,0:T(8,128)(2,1)} %collective-permute-done.11), channel_id=1, source_target_pairs={{0,8},{4,20},{8,24},{12,4},{24,16},{28,12},{16,0},{20,28},{1,9},{5... | collective-permute-start | bytes 3145736 | tf_op jit(solution)/shard_map/ppermute | solution.py:76
  190.8 24.0 %collective-permute-start.17 = (bf16[512,512]{1,0:T(8,128)(2,1)}, bf16[512,512]{1,0:T(8,128)(2,1)}, u32[]{:S(2)}, u32[]{:S(2)}) collective-permute-start(bf16[512,512]{1,0:T(8,128)(2,1)} %get-tuple-element.16), channel_id=1, source_target_pairs={{1,0},{2,1},{3,2},{5,4},{6,5},{7,6},{9,8},{10,9},{11,10},{13,12},{... | collective-permute-start | bytes 1572872 | tf_op jit(solution)/shard_map/ppermute | solution.py:163
  192.1 22.7 %collective-permute-start.16 = (bf16[512,512]{1,0:T(8,128)(2,1)}, bf16[512,512]{1,0:T(8,128)(2,1)}, u32[]{:S(2)}, u32[]{:S(2)}) collective-permute-start(bf16[512,512]{1,0:T(8,128)(2,1)} %get-tuple-element.14), channel_id=1, source_target_pairs={{0,1},{1,2},{2,3},{4,5},{5,6},{6,7},{8,9},{9,10},{10,11},{12,13},{... | collective-permute-start | bytes 1572872 | tf_op jit(solution)/shard_map/ppermute | solution.py:162
  204.0 24.8 %collective-permute-start.19 = (bf16[512,512]{1,0:T(8,128)(2,1)}, bf16[512,512]{1,0:T(8,128)(2,1)}, u32[]{:S(2)}, u32[]{:S(2)}) collective-permute-start(bf16[512,512]{1,0:T(8,128)(2,1)} %add_convert_fusion.3), channel_id=1, source_target_pairs={{0,2},{1,3},{2,0},{3,1},{4,6},{5,7},{6,4},{7,5},{8,10},{9,11},{10,... | collective-permute-start | bytes 1572872 | tf_op jit(solution)/shard_map/ppermute | solution.py:165
  231.5 27.0 %collective-permute-start.20 = (bf16[512,512]{1,0:T(8,128)(2,1)S(1)}, bf16[512,512]{1,0:T(8,128)(2,1)S(1)}, u32[]{:S(2)}, u32[]{:S(2)}) collective-permute-start(bf16[512,512]{1,0:T(8,128)(2,1)S(1)} %get-tuple-element.85), channel_id=1, source_target_pairs={{0,2},{1,3},{2,0},{3,1},{4,6},{5,7},{6,4},{7,5},{8,10},{9,11},{10,... | collective-permute-start | bytes 1572872 | tf_op jit(solution)/shard_map/ppermute | solution.py:138
  231.5 33.5 %collective-permute-start.22 = (bf16[512,512]{1,0:T(8,128)(2,1)S(1)}, bf16[512,512]{1,0:T(8,128)(2,1)S(1)}, u32[]{:S(2)}, u32[]{:S(2)}) collective-permute-start(bf16[512,512]{1,0:T(8,128)(2,1)S(1)} %get-tuple-element.85), channel_id=1, source_target_pairs={{1,0},{2,1},{3,2},{5,4},{6,5},{7,6},{9,8},{10,9},{11,10},{13,12},{... | collective-permute-start | bytes 1572872 | tf_op jit(solution)/shard_map/ppermute | solution.py:140
  297.2 53.2 %collective-permute-start.25 = (bf16[512,2048]{1,0:T(8,128)(2,1)S(1)}, bf16[512,2048]{1,0:T(8,128)(2,1)S(1)}, u32[]{:S(2)}, u32[]{:S(2)}) collective-permute-start(bf16[512,2048]{1,0:T(8,128)(2,1)S(1)} %slice.712), channel_id=1, source_target_pairs={{0,4},{4,0},{8,12},{12,8},{16,20},{20,16},{24,28},{28,24},{1,5},{5... | collective-permute-start | bytes 6291464 | tf_op jit(solution)/shard_map/ppermute | solution.py:68
  306.5 41.5 %collective-permute-start.35 = (bf16[512,1024]{1,0:T(8,128)(2,1)S(1)}, bf16[512,1024]{1,0:T(8,128)(2,1)S(1)}, u32[]{:S(2)}, u32[]{:S(2)}) collective-permute-start(bf16[512,1024]{1,0:T(8,128)(2,1)S(1)} %get-tuple-element.9), channel_id=1, source_target_pairs={{0,16},{4,12},{8,0},{12,28},{24,8},{28,20},{16,24},{20,4},{1,17},{... | collective-permute-start | bytes 3145736 | tf_op jit(solution)/shard_map/ppermute | solution.py:93
  308.7 64.0 %collective-permute-start.37 = (bf16[512,1024]{1,0:T(8,128)(2,1)}, bf16[512,1024]{1,0:T(8,128)(2,1)}, u32[]{:S(2)}, u32[]{:S(2)}) collective-permute-start(bf16[512,1024]{1,0:T(8,128)(2,1)} %get-tuple-element.10), channel_id=1, source_target_pairs={{0,8},{4,20},{8,24},{12,4},{24,16},{28,12},{16,0},{20,28},{1,9},{5... | collective-permute-start | bytes 3145736 | tf_op jit(solution)/shard_map/ppermute | solution.py:98
  349.5 23.3 %collective-permute-start.36 = (bf16[512,1024]{1,0:T(8,128)(2,1)}, bf16[512,1024]{1,0:T(8,128)(2,1)}, u32[]{:S(2)}, u32[]{:S(2)}) collective-permute-start(bf16[512,1024]{1,0:T(8,128)(2,1)} %fusion.19), channel_id=1, source_target_pairs={{0,16},{4,12},{8,0},{12,28},{24,8},{28,20},{16,24},{20,4},{1,17},{... | collective-permute-start | bytes 3145736 | tf_op jit(solution)/shard_map/ppermute | solution.py:96
  356.0 23.7 %collective-permute-start.27 = (bf16[512,512]{1,0:T(8,128)(2,1)}, bf16[512,512]{1,0:T(8,128)(2,1)}, u32[]{:S(2)}, u32[]{:S(2)}) collective-permute-start(bf16[512,512]{1,0:T(8,128)(2,1)} %get-tuple-element.13), channel_id=1, source_target_pairs={{1,0},{2,1},{3,2},{5,4},{6,5},{7,6},{9,8},{10,9},{11,10},{13,12},{... | collective-permute-start | bytes 1572872 | tf_op jit(solution)/shard_map/ppermute | solution.py:163
  357.5 22.1 %collective-permute-start.26 = (bf16[512,512]{1,0:T(8,128)(2,1)}, bf16[512,512]{1,0:T(8,128)(2,1)}, u32[]{:S(2)}, u32[]{:S(2)}) collective-permute-start(bf16[512,512]{1,0:T(8,128)(2,1)} %get-tuple-element.11), channel_id=1, source_target_pairs={{0,1},{1,2},{2,3},{4,5},{5,6},{6,7},{8,9},{9,10},{10,11},{12,13},{... | collective-permute-start | bytes 1572872 | tf_op jit(solution)/shard_map/ppermute | solution.py:162
  369.3 23.0 %collective-permute-start.29 = (bf16[512,512]{1,0:T(8,128)(2,1)}, bf16[512,512]{1,0:T(8,128)(2,1)}, u32[]{:S(2)}, u32[]{:S(2)}) collective-permute-start(bf16[512,512]{1,0:T(8,128)(2,1)} %add_convert_fusion.2), channel_id=1, source_target_pairs={{0,2},{1,3},{2,0},{3,1},{4,6},{5,7},{6,4},{7,5},{8,10},{9,11},{10,... | collective-permute-start | bytes 1572872 | tf_op jit(solution)/shard_map/ppermute | solution.py:165
  (34 other events, 594.9 us)
Sparse Core Ops, SparseCore 0:
  71.5 77.1 all-gather.1
  283.3 79.5 reduce-scatter.1

commit v2 on v0

--- a/solution.py
+++ b/solution.py
@@ -1,10 +1,485 @@
+import functools
+
 import jax
 import jax.numpy as jnp
 from jax import lax
+from jax.experimental import pallas as pl
+from jax.experimental.pallas import tpu as pltpu
 from jax.sharding import PartitionSpec as P
 
 C = 2048
 KS = 7
+REACH = KS // 2
+F32 = jnp.float32
+BF16 = jnp.bfloat16
+LAST = (((1,), (1,)), ((), ()))
+FIRST = (((0,), (0,)), ((), ()))
+SIBLING = [(i, i ^ 1) for i in range(8)]
+CHIPS = (0, 1, 3, 2)
+UP = [(0, 1), (1, 2), (2, 3)]
+DOWN = [(1, 0), (2, 1), (3, 2)]
+ACROSS = [(0, 2), (1, 3), (2, 0), (3, 1)]
+SAME_CORE = [[0, 2, 4, 6], [1, 3, 5, 7]]
+ANY = pl.BlockSpec(memory_space=pl.ANY)
+VMEM = pl.BlockSpec(memory_space=pltpu.VMEM)
+PARAMS = pltpu.CompilerParams(vmem_limit_bytes=52 * 2**20)
+HINT = pl.CostEstimate(flops=0, bytes_accessed=0, transcendentals=0)
+
+
+def ring_pairs(sense):
+    pairs = []
+    for place, chip in enumerate(CHIPS):
+        for core in (0, 1):
+            step = sense if core == 0 else -sense
+            pairs.append((2 * chip + core, 2 * CHIPS[(place + step) % 4] + core))
+    return pairs
+
+
+AHEAD = ring_pairs(1)
+BEHIND = ring_pairs(-1)
+
+
+def shape(dims, dtype=BF16):
+    return jax.ShapeDtypeStruct(dims, dtype)
+
+
+def call(body, ids, arrays, grid, ins, outs, shapes, scratch=(), after=(), aliases=None):
+    count = len(arrays)
+
+    def kernel(ids_ref, *refs):
+        body(ids_ref, *refs[:count], *refs[count + len(after) :])
+
+    return pl.pallas_call(
+        kernel,
+        grid_spec=pltpu.PrefetchScalarGridSpec(
+            num_scalar_prefetch=1,
+            grid=grid,
+            in_specs=list(ins) + [ANY] * len(after),
+            out_specs=outs,
+            scratch_shapes=scratch,
+        ),
+        out_shape=shapes,
+        compiler_params=PARAMS,
+        cost_estimate=HINT,
+        input_output_aliases=aliases or {},
+    )(ids, *arrays, *after)
+
+
+def later(ids, array, after):
+    return call(
+        lambda *refs: None, ids, [array], (), [ANY], ANY, shape(array.shape, array.dtype),
+        after=after, aliases={1: 0},
+    )
+
+
+def whole(dims):
+    return pl.BlockSpec(dims, lambda *_: (0,) * len(dims))
+
+
+def make_ids():
+    z = lax.axis_index("col")
+    row = lax.axis_index("row")
+    core = row % 2
+    sense = 1 - 2 * core
+    places = jnp.array([CHIPS.index(chip) for chip in range(4)], jnp.int32)
+    order = jnp.array(CHIPS, jnp.int32)
+    place = places[row // 2]
+    ring = [order[(place + sense * step + 4) % 4] for step in (0, -1, 1, 2)]
+    return jnp.stack([z, (z + 1) % 4, (z + 2) % 4, (z + 3) % 4, core] + ring).astype(jnp.int32)
+
+
+def move(body, ids, arrays, shapes, count, after=()):
+    def kernel(ids_ref, *refs):
+        sems = refs[-1]
+        pairs = list(body(ids_ref, refs[: len(arrays)], refs[len(arrays) : -1]))
+        copies = [pltpu.make_async_copy(src, dst, sems.at[i]) for i, (_, src, dst) in enumerate(pairs)]
+        for (when, _, _), copy in zip(pairs, copies):
+            if when is None:
+                copy.start()
+            else:
+                pl.when(when)(copy.start)
+        for (when, _, _), copy in zip(pairs, copies):
+            if when is None:
+                copy.wait()
+            else:
+                pl.when(when)(copy.wait)
+
+    return call(
+        kernel, ids, arrays, (), [ANY] * len(arrays), [VMEM] * len(shapes), shapes,
+        [pltpu.SemaphoreType.DMA((count,))], after,
+    )
+
+
+def start_of(index, size):
+    return pl.ds(pl.multiple_of(index * size, size), size)
+
+
+def give_half(ids, weight):
+    rows, cols = weight.shape
+
+    def body(i, s, t):
+        yield None, s[0].at[:, start_of(1 - i[4], cols // 2)], t[0]
+
+    return move(body, ids, [weight], [shape((rows, cols // 2))], 1)[0]
+
+
+def chip_rows(ids, weight, other):
+    rows, cols = weight.shape
+
+    def body(i, s, t):
+        yield None, s[0].at[:, start_of(i[4], cols // 2)], t[0].at[start_of(i[4], rows)]
+        yield None, s[1], t[0].at[start_of(1 - i[4], rows)]
+
+    return move(body, ids, [weight, other], [shape((2 * rows, cols // 2))], 2)[0]
+
+
+def stack_chips(ids, blocks):
+    rows, cols = blocks[0].shape
+
+    def body(i, s, t):
+        for k in range(4):
+            yield None, s[k], t[0].at[start_of(i[5 + k], rows)]
+
+    return move(body, ids, blocks, [shape((4 * rows, cols))], 4)[0]
+
+
+def ring_gather(ids, block):
+    one = lax.ppermute(block, "row", AHEAD)
+    two = lax.ppermute(block, "row", BEHIND)
+    far = lax.ppermute(one, "row", AHEAD)
+    return stack_chips(ids, [block, one, two, far])
+
+
+def col_gather(ids, block, before_far=(), before_end=()):
+    rows, cols = block.shape
+    across = lax.ppermute(block, "col", ACROSS)
+    above = lax.ppermute(block, "col", DOWN)
+    below = lax.ppermute(block, "col", UP)
+    if before_far:
+        across = later(ids, across, before_far)
+    far = lax.ppermute(across, "col", [(1, 0), (2, 3)])
+
+    def body(i, s, t):
+        def to(k):
+            return t[0].at[:, start_of(i[k], cols)]
+
+        z = i[0]
+        yield None, s[0], to(0)
+        yield None, s[2], to(2)
+        yield z < 3, s[1], to(1)
+        yield z == 3, s[4], to(1)
+        yield z > 0, s[3], to(3)
+        yield z == 0, s[4], to(3)
+
+    return move(
+        body, ids, [block, above, across, below, far], [shape((rows, 4 * cols))], 6, before_end
+    )[0]
+
+
+def gelu_parts(v):
+    cdf = 0.5 * (1.0 + lax.erf(v * 0.7071067811865476))
+    return v * cdf, cdf + v * jnp.exp(-0.5 * v * v) * 0.3989422804014327
+
+
+TILE = 256
+
+
+def expand(ids, own, sib, panel):
+    rows = own.shape[0]
+    hid = panel.shape[1]
+
+    def kernel(ids_ref, own_ref, sib_ref, w_ref, hidden_ref, slope_ref):
+        for half, x in enumerate((own_ref, sib_ref)):
+            at = pl.ds(half * rows, rows)
+            pre = jnp.dot(x[...], w_ref[...], preferred_element_type=F32)
+            act, slope = gelu_parts(pre)
+            hidden_ref[at] = act.astype(BF16)
+            slope_ref[at] = slope.astype(BF16)
+
+    tile = pl.BlockSpec((2 * rows, TILE), lambda t, i: (0, t))
+    return call(
+        kernel, ids, [own, sib, panel], (hid // TILE,),
+        [whole(own.shape), whole(sib.shape), pl.BlockSpec((C, TILE), lambda t, i: (0, t))],
+        [tile, tile], [shape((2 * rows, hid))] * 2,
+    )
+
+
+def expand_grad(ids, own, sib, panel, slope, after):
+    rows = own.shape[0]
+    hid = slope.shape[1]
+    steps = hid // TILE
+
+    def kernel(ids_ref, own_ref, sib_ref, w_ref, slope_ref, out_ref):
+        for half, x in enumerate((own_ref, sib_ref)):
+            at = pl.ds(half * rows, rows)
+            back = jnp.dot(x[...], w_ref[...], preferred_element_type=F32)
+            out_ref[at] = (back * slope_ref[at].astype(F32)).astype(BF16)
+
+    tile = pl.BlockSpec((2 * rows, TILE), lambda t, i: (0, t))
+    return call(
+        kernel, ids, [own, sib, panel, slope], (steps,),
+        [
+            whole(own.shape),
+            whole(sib.shape),
+            pl.BlockSpec((C, TILE), lambda t, i: (0, i[4] * steps + t)),
+            tile,
+        ],
+        tile, shape((2 * rows, hid)), after=after,
+    )
+
+
+def weight_grad(ids, own, sib, right, slots, after=()):
+    rows = own.shape[0]
+    hid = right.shape[1]
+    steps = 512 // TILE
+
+    def kernel(ids_ref, own_ref, sib_ref, r_ref, *outs):
+        acc = lax.dot_general(own_ref[...], r_ref[:rows], FIRST, preferred_element_type=F32)
+        acc += lax.dot_general(sib_ref[...], r_ref[rows:], FIRST, preferred_element_type=F32)
+        if not slots:
+            outs[0][...] = acc.astype(BF16)
+            return
+        for k in range(4):
+            @pl.when(pl.program_id(0) == k)
+            def _():
+                outs[k][...] = acc.astype(BF16)
+
+    if slots:
+        order = (8, 7, 6, 5)
+
+        def column(s, t, i):
+            first = jnp.where(s == 0, i[8], jnp.where(s == 1, i[7], jnp.where(s == 2, i[6], i[5])))
+            return 0, first * steps + t
+
+        outs = [
+            pl.BlockSpec(
+                (TILE, hid),
+                lambda s, t, i, k=k: (jnp.where(s == k, t, jnp.where(s < k, 0, steps - 1)), 0),
+            )
+            for k in range(4)
+        ]
+        shapes = [shape((512, hid))] * 4
+    else:
+        def column(s, t, i):
+            return 0, s * steps + t
+
+        outs = pl.BlockSpec((TILE, hid), lambda s, t, i: (s * steps + t, 0))
+        shapes = shape((C, hid))
+    cut = pl.BlockSpec((rows, TILE), column)
+    return call(
+        kernel, ids, [own, sib, right], (4, steps), [cut, cut, whole(right.shape)], outs, shapes,
+        after=after,
+    )
+
+
+def contract_sib(ids, left, panel, offset, after=()):
+    rows = left.shape[0] // 2
+    hid = left.shape[1]
+
+    def kernel(ids_ref, x_ref, w_ref, out_ref):
+        out_ref[...] = lax.dot_general(
+            x_ref[...], w_ref[...], LAST, preferred_element_type=F32
+        ).astype(BF16)
+
+    return call(
+        kernel, ids, [left, panel], (C // 512,),
+        [
+            pl.BlockSpec((rows, hid), lambda t, i: (1, 0)),
+            pl.BlockSpec((512, hid), lambda t, i: (t, i[4] * offset)),
+        ],
+        pl.BlockSpec((rows, 512), lambda t, i: (0, t)), shape((rows, C)), after=after,
+    )
+
+
+def contract_own(ids, left, panel, other, offset, after=()):
+    rows = left.shape[0] // 2
+    hid = left.shape[1]
+
+    def kernel(ids_ref, x_ref, w_ref, o_ref, *outs):
+        acc = lax.dot_general(x_ref[...], w_ref[...], LAST, preferred_element_type=F32)
+        acc = (acc + o_ref[...].astype(F32)).astype(BF16)
+        step = pl.program_id(0)
+        for k in range(4):
+            @pl.when(step == k)
+            def _():
+                outs[k][...] = acc
+
+        @pl.when(step == jnp.where(ids_ref[0] == 0, 3, 1))
+        def _():
+            outs[4][...] = acc
+
+    def pick(t, i):
+        return jnp.where(t == 0, i[0], jnp.where(t == 1, i[1], jnp.where(t == 2, i[2], i[3])))
+
+    return call(
+        kernel, ids, [left, panel, other], (4,),
+        [
+            pl.BlockSpec((rows, hid), lambda t, i: (0, 0)),
+            pl.BlockSpec((512, hid), lambda t, i: (pick(t, i), i[4] * offset)),
+            pl.BlockSpec((rows, 512), lambda t, i: (0, pick(t, i))),
+        ],
+        [whole((rows, 512))] * 5, [shape((rows, 512))] * 5, after=after,
+    )
+
+
+def col_scatter(blocks):
+    own, after, across, before, far = blocks
+    far = lax.ppermute(far, "col", [(0, 1), (3, 2)])
+    below = lax.ppermute(after, "col", UP)
+    above = lax.ppermute(before, "col", DOWN)
+    pair = (across.astype(F32) + far.astype(F32)).astype(BF16)
+    across = lax.ppermute(pair, "col", ACROSS)
+    return own.astype(F32) + below.astype(F32) + above.astype(F32) + across.astype(F32)
+
+
+def ring_scatter(blocks):
+    far, ahead, behind, own = blocks
+    one = lax.ppermute(far, "row", BEHIND)
+    two = lax.ppermute(ahead, "row", AHEAD)
+    one = lax.ppermute((one.astype(F32) + behind.astype(F32)).astype(BF16), "row", BEHIND)
+    return (own.astype(F32) + one.astype(F32) + two.astype(F32)).astype(BF16)
+
+
+def give_rows(ids, block):
+    rows, cols = block.shape
+
+    def body(i, s, t):
+        yield None, s[0].at[start_of(1 - i[4], rows // 2)], t[0]
+
+    return move(body, ids, [block], [shape((rows // 2, cols))], 1)[0]
+
+
+def own_rows(ids, block):
+    rows, cols = block.shape
+    other = lax.ppermute(give_rows(ids, block), "row", SIBLING)
+
+    def body(i, s, t):
+        yield None, s[0].at[start_of(i[4], rows // 2)], t[0].at[:, start_of(i[4], cols)]
+        yield None, s[1], t[0].at[:, start_of(1 - i[4], cols)]
+
+    return move(body, ids, [block, other], [shape((rows // 2, 2 * cols))], 2)[0]
+
+
+def taps(ids, low, mid, high, dw_kernel, flipped, extra=None, after=()):
+    images, rows, width, chans = mid.shape
+    lanes = 128
+    edge = 8
+
+    def kernel(ids_ref, *refs):
+        low_ref, mid_ref, high_ref, dw_ref = refs[:4]
+        out_ref, pad_ref = refs[-2:]
+        pad_ref[:, :edge] = jnp.zeros((rows + 2 * REACH, edge, lanes), F32)
+        pad_ref[:, edge + width :] = jnp.zeros((rows + 2 * REACH, edge, lanes), F32)
+        pad_ref[:REACH, edge : edge + width] = low_ref[0].astype(F32)
+        pad_ref[REACH : REACH + rows, edge : edge + width] = mid_ref[0].astype(F32)
+        pad_ref[REACH + rows :, edge : edge + width] = high_ref[0].astype(F32)
+        totals = [jnp.zeros((width, lanes), F32)] * rows
+        for off_col in range(KS):
+            tap_col = KS - 1 - off_col if flipped else off_col
+            for place in range(rows + 2 * REACH):
+                line = pad_ref[place, pl.ds(edge - REACH + off_col, width)]
+                for row in range(rows):
+                    off_row = place - row
+                    if 0 <= off_row < KS:
+                        tap_row = KS - 1 - off_row if flipped else off_row
+                        totals[row] += dw_ref[pl.ds(tap_row * KS + tap_col, 1)] * line
+        for row in range(rows):
+            if extra is None:
+                out_ref[0, row] = totals[row]
+            else:
+                out_ref[0, row] = (refs[4][0, row].astype(F32) + totals[row]).astype(BF16)
+
+    def strip(count):
+        return pl.BlockSpec((1, count, width, lanes), lambda b, c, i: (b, 0, 0, c))
+
+    arrays = [low, mid, high, dw_kernel.reshape(KS * KS, chans)]
+    ins = [strip(REACH), strip(rows), strip(REACH), pl.BlockSpec((KS * KS, lanes), lambda b, c, i: (0, c))]
+    if extra is not None:
+        arrays.append(extra)
+        ins.append(strip(rows))
+    return call(
+        kernel, ids, arrays, (images, chans // lanes), ins, strip(rows),
+        shape(mid.shape, F32 if extra is None else BF16),
+        [pltpu.VMEM((rows + 2 * REACH, width + 2 * edge, lanes), F32)], after,
+    )
+
+
+def rims(block):
+    count = lax.axis_size("row")
+    forward = [(i, i + 1) for i in range(count - 1)]
+    backward = [(i + 1, i) for i in range(count - 1)]
+    low = lax.ppermute(block[:, -REACH:], "row", forward)
+    high = lax.ppermute(block[:, :REACH], "row", backward)
+    return low, high
+
+
+def col_all(small):
+    count = lax.axis_size("col")
+    shifts = [
+        lax.ppermute(small, "col", [(i, (i + step) % count) for i in range(count)])
+        for step in range(1, count)
+    ]
+    return jnp.stack([small] + shifts)
+
+
+def on_device(images, dw_kernel, norm_gain, proj_in, proj_out, layer_scale, cotangent):
+    local_ch = images.shape[3]
+    pixels = images.shape[0] * images.shape[1] * images.shape[2]
+    ids = make_ids()
+
+    def swap(block):
+        return lax.ppermute(block, "row", SIBLING)
+
+    out_panel = lax.all_gather(proj_out, "row", axis=0, tiled=True)
+    cot_flat = cotangent.reshape(pixels, local_ch).astype(F32)
+    grad_branch = (cot_flat * layer_scale).astype(BF16)
+    low, high = rims(images)
+    in_block = chip_rows(ids, proj_in, swap(give_half(ids, proj_in)))
+    in_panel = ring_gather(ids, in_block)
+    grad_own = col_gather(ids, grad_branch, before_end=[in_panel])
+    grad_sib = swap(grad_own)
+
+    conv_out = taps(ids, low, images, high, dw_kernel, False, after=[in_block]).reshape(pixels, local_ch)
+    own_mean = jnp.mean(conv_out, axis=1)
+    own_dev = conv_out - own_mean[:, None]
+    stats = col_all(jnp.stack([own_mean, jnp.sum(own_dev * own_dev, axis=1)]))
+    row_mean = jnp.mean(stats[:, 0], axis=0)
+    spread = stats[:, 0] - row_mean
+    row_var = jnp.sum(stats[:, 1] + local_ch * (spread * spread), axis=0) / C
+    inv_std = lax.rsqrt(row_var + 1e-06)
+    normed = (conv_out - row_mean[:, None]) * inv_std[:, None]
+    scaled = (normed * norm_gain).astype(BF16)
+    in_own = col_gather(ids, scaled, before_far=[grad_own])
+    in_sib = swap(in_own)
+
+    hidden, slope = expand(ids, in_own, in_sib, in_panel)
+    out_part = weight_grad(ids, grad_own, grad_sib, hidden, False)
+    out_rows = lax.psum_scatter(
+        out_part, "row", scatter_dimension=0, tiled=True, axis_index_groups=SAME_CORE
+    )
+    grad_pre = expand_grad(ids, grad_own, grad_sib, out_panel, slope, [out_part])
+    back_give = contract_sib(ids, grad_pre, in_panel, 0)
+    back_sib = swap(back_give)
+    in_parts = weight_grad(ids, in_own, in_sib, grad_pre, True, [back_give])
+    back = contract_own(ids, grad_pre, in_panel, back_sib, 0, [in_parts[0]])
+    grad_scaled = col_scatter(back)
+    in_rows = ring_scatter(in_parts)
+    branch_give = contract_sib(ids, hidden, out_panel, 1, [back[0]])
+    branch = col_scatter(contract_own(ids, hidden, out_panel, swap(branch_give), 1))
+    residual_in = images.reshape(pixels, local_ch).astype(F32)
+    block_out = (residual_in + layer_scale * branch).astype(BF16).reshape(images.shape)
+
+    weighted = grad_scaled * norm_gain
+    sums = jnp.sum(
+        col_all(jnp.stack([jnp.sum(weighted, axis=1), jnp.sum(weighted * normed, axis=1)])), axis=0
+    )
+    grad_conv = inv_std[:, None] * (
+        weighted - sums[0][:, None] / C - normed * sums[1][:, None] / C
+    )
+    grad_conv = grad_conv.astype(BF16).reshape(images.shape)
+    low, high = rims(grad_conv)
+    grad_images = taps(ids, low, grad_conv, high, dw_kernel, True, cotangent)
+    return block_out, grad_images, own_rows(ids, in_rows), own_rows(ids, out_rows)
 
 
 def with_halo(block, sides, width):
@@ -42,7 +517,7 @@
     )
 
 
-def on_device(images, dw_kernel, norm_gain, proj_in, proj_out, layer_scale, cotangent):
+def on_any_mesh(images, dw_kernel, norm_gain, proj_in, proj_out, layer_scale, cotangent):
     img_batch, strip_rows, img_cols, local_ch = images.shape
     pixels = img_batch * strip_rows * img_cols
     reach = KS // 2
@@ -111,6 +586,7 @@
 
 
 def solution(mesh):
+    tuned = mesh.shape["row"] == 8 and mesh.shape["col"] == 4
     placed = (
         P(None, "row", None, "col"),
         P(None, None, "col"),
@@ -121,7 +597,7 @@
         P(None, "row", None, "col"),
     )
     return jax.shard_map(
-        on_device,
+        on_device if tuned else on_any_mesh,
         mesh=mesh,
         in_specs=placed,
         out_specs=(

time: 534 us -> 347 us (0.65)
  waiting for transfers between devices: 385 us -> 133 us
  Pallas kernels: 0 us -> 102 us
  matrix products: 61.5 us -> 0 us
  starting transfers between devices: 7 us -> 63.9 us
  blocking collectives: 30.1 us -> 0 us
  other arithmetic: 27.6 us -> 10.8 us
  local copies, waits for them, and re-layouts: 7.51 us -> 15.5 us
    reduce_scatter x4 -> x1, waiting for transfers between devices: 190 us -> 0.01 us  [on_device(): lax.psum_scatter(out_part, 'row', scatter_dimension=0, tiled=True, axis_i...]
    all_gather x3 -> x0, waiting for transfers between devices: 149 us -> none  [the longest x1 55 us: on_device(): in_panel = lax.all_gather(proj_in, 'row', axis=0, tiled=True)]
    ppermute x4 -> x39, waiting for transfers between devices: 5.4 us -> 133 us  [the longest x2 35.7 us: col_scatter(): across = lax.ppermute(pair, 'col', ACROSS)]
    pallas_call x0 -> x20, Pallas kernels: none -> 102 us  [call(): pl.pallas_call(kernel, grid_spec=pltpu.PrefetchScalarGridSpec(num_scalar_...]
    dot_general x6 -> x0, matrix products: 61.5 us -> none  [the longest x1 17.3 us: on_device(): hidden_pre = jnp.dot(full_in, in_panel, preferred_element_type=jnp.float32)]
    ppermute x4 -> x39, starting transfers between devices: 6.28 us -> 63.8 us  [the longest x1 7.27 us: ring_gather(): two = lax.ppermute(block, 'row', BEHIND)]
    all_gather x1, waiting for transfers between devices: 39 us -> 0.02 us  [on_device(): out_panel = lax.all_gather(proj_out, 'row', axis=0, tiled=True)]
    psum x3 -> x0, blocking collectives: 30.1 us -> none  [the longest x1 11.9 us: on_device(): row_mean = lax.psum(jnp.sum(conv_out, axis=1), 'col') / C]
  transfers between devices with their start and end apart: 12 -> 41, of which waited for: 10 -> 13; matrix products, arithmetic and copies ran while one was open for 9% -> 5% of each run, Pallas kernels for 0% -> 30%
where the time goes in v2:
time: 347 us; the launch traced here: 345 us
  waiting for transfers between devices  133 us (38%)
  Pallas kernels  102 us (29%)
  starting transfers between devices  63.9 us (18%)
  between operations  18.9 us (5%)
  local copies, waits for them, and re-layouts  15.5 us (4%)
  other arithmetic  10.8 us (3%)
    pallas_call x20, Pallas kernels, call(): pl.pallas_call(kernel, grid_spec=pltpu.PrefetchScalarGridSpec(num_scalar_...  102 us
    ppermute x2, waiting for transfers between devices, col_scatter(): across = lax.ppermute(pair, 'col', ACROSS)  35.7 us
    ppermute x1, waiting for transfers between devices, ring_gather(): two = lax.ppermute(block, 'row', BEHIND)  31.8 us
    ppermute x2, waiting for transfers between devices, col_scatter(): far = lax.ppermute(far, 'col', [(0, 1), (3, 2)])  13.9 us
    ppermute x2, waiting for transfers between devices, col_gather(): across = lax.ppermute(block, 'col', ACROSS)  11.6 us
    ppermute x2, waiting for transfers between devices, col_gather(): far = lax.ppermute(across, 'col', [(1, 0), (2, 3)])  11.1 us
    ppermute x2, waiting for transfers between devices, col_scatter(): below = lax.ppermute(after, 'col', UP)  9.24 us
    unnamed x50, local copies, waits for them, and re-layouts  8.92 us
  transfers between devices with their start and end apart: 41, of which 13 were waited for; matrix products, arithmetic and copies ran while one was open for 5% of the time, Pallas kernels for 30%

profile of v2, /device:TPU:0, one launch (start us, length us, event | category | flops | bytes accessed | tf_op | source)
XLA Modules:
  0.0 344.6 jit_solution(14081251501267352076)
XLA Ops:
  32.8 7.1 %shard_map.122 = f32[2,4,64,512]{3,2,1,0:T(8,128)} custom-call(s32[9]{0:T(128)S(1)} %stack.59.ids_ref, bf16[2,3,64,512]{3,2,1,0:T(8,128)(2,1)} %collective-permute-done.refs_0_, bf16[2,4,64,512]{3,2,1,0:T(8,128)(2,1)S(1)} %copy-done, bf16[2,3,64,512]{3,2,1,0:T(8,128)(2,1)} %collective-permute-done.1.refs_2_, f32[49,512]{1,0:T(8,128)S(1)} %reshape.84.refs_3_, ...), custom_call_target="tpu_custom_call" | custom-call | tf_op jit(solution)/shard_map/pallas_call | solution.py:52
  47.1 6.0 %collective-permute-done.9.refs_2_ = bf16[512,512]{1,0:T(8,128)(2,1)S(1)} collective-permute-done((bf16[512,512]{1,0:T(8,128)(2,1)S(1)}, bf16[512,512]{1,0:T(8,128)(2,1)S(1)}, u32[]{:S(2)}, u32[]{:S(2)}) %collective-permute-start.9) | collective-permute-done | bytes 524320 | tf_op jit(solution)/shard_map/ppermute | solution.py:155
  57.6 7.3 %collective-permute-start.13 = (bf16[512,1024]{1,0:T(8,128)(2,1)}, bf16[512,1024]{1,0:T(8,128)(2,1)S(1)}, u32[]{:S(2)}, u32[]{:S(2)}) collective-permute-start(bf16[512,1024]{1,0:T(8,128)(2,1)} %shard_map.121.refs_4_.refs_0_), channel_id=1, source_target_pairs={{0,16},{4,12},{8,0},{12,28},{24,8},{28,20},{16,24},{20,4},{1,17},{... | collective-permute-start | bytes 3145736 | tf_op jit(solution)/shard_map/ppermute | solution.py:148
  66.5 31.8 %collective-permute-done.13.refs_2_ = bf16[512,1024]{1,0:T(8,128)(2,1)S(1)} collective-permute-done((bf16[512,1024]{1,0:T(8,128)(2,1)}, bf16[512,1024]{1,0:T(8,128)(2,1)S(1)}, u32[]{:S(2)}, u32[]{:S(2)}) %collective-permute-start.13) | collective-permute-done | bytes 1048608 | tf_op jit(solution)/shard_map/ppermute | solution.py:148
  104.1 4.7 %shard_map.123.refs_5_.refs_2_.refs_1_ = bf16[2048,1024]{1,0:T(8,128)(2,1)} custom-call(s32[9]{0:T(128)S(1)} %stack.59.ids_ref, bf16[512,1024]{1,0:T(8,128)(2,1)} %shard_map.121.refs_4_.refs_0_, bf16[512,1024]{1,0:T(8,128)(2,1)} %collective-permute-done.12.refs_1_, bf16[512,1024]{1,0:T(8,128)(2,1)} %copy-done.11, bf16[512,1024]{1,0:T(8,128)(2,1)} %copy-done.13), custom_call_target="tpu_custom_call" | custom-call | tf_op jit(solution)/shard_map/pallas_call | solution.py:52
  114.1 5.7 %collective-permute-done.7.refs_0_ = bf16[512,512]{1,0:T(8,128)(2,1)S(1)} collective-permute-done((bf16[512,512]{1,0:T(8,128)(2,1)S(1)}, bf16[512,512]{1,0:T(8,128)(2,1)S(1)}, u32[]{:S(2)}, u32[]{:S(2)}) %collective-permute-start.7) | collective-permute-done | bytes 524320 | tf_op jit(solution)/shard_map/ppermute | solution.py:155
  121.8 7.9 %collective-permute-done.6.refs_1_ = bf16[512,512]{1,0:T(8,128)(2,1)S(1)} collective-permute-done((bf16[512,512]{1,0:T(8,128)(2,1)S(1)}, bf16[512,512]{1,0:T(8,128)(2,1)S(1)}, u32[]{:S(2)}, u32[]{:S(2)}) %collective-permute-start.6) | collective-permute-done | bytes 524320 | tf_op jit(solution)/shard_map/ppermute | solution.py:156
  129.7 11.1 %collective-permute-done.16.refs_4_ = bf16[512,512]{1,0:T(8,128)(2,1)S(1)} collective-permute-done((bf16[512,512]{1,0:T(8,128)(2,1)S(1)}, bf16[512,512]{1,0:T(8,128)(2,1)S(1)}, u32[]{:S(2)}, u32[]{:S(2)}) %collective-permute-start.16) | collective-permute-done | bytes 524320 | tf_op jit(solution)/shard_map/ppermute | solution.py:160
  145.5 6.0 %collective-permute-done.17.refs_1_ = bf16[512,2048]{1,0:T(8,128)(2,1)S(1)} collective-permute-done((bf16[512,2048]{1,0:T(8,128)(2,1)}, bf16[512,2048]{1,0:T(8,128)(2,1)S(1)}, u32[]{:S(2)}, u32[]{:S(2)}) %collective-permute-start.17) | collective-permute-done | bytes 2097184 | tf_op jit(solution)/shard_map/ppermute | solution.py:431
  152.8 10.5 %shard_map.127 = (bf16[1024,1024]{1,0:T(8,128)(2,1)}, bf16[1024,1024]{1,0:T(8,128)(2,1)}) custom-call(s32[9]{0:T(128)S(1)} %stack.59.ids_ref, bf16[512,2048]{1,0:T(8,128)(2,1)} %shard_map.126.refs_0_, bf16[512,2048]{1,0:T(8,128)(2,1)} %copy-done.9, bf16[2048,1024]{1,0:T(8,128)(2,1)} %shard_map.123.refs_5_.refs_2_.refs_1_), custom_call_target="tpu_custom_call" | custom-call | tf_op jit(solution)/shard_map/pallas_call | solution.py:52
  164.6 10.7 %shard_map.128.refs_4_ = bf16[2048,1024]{1,0:T(8,128)(2,1)} custom-call(s32[9]{0:T(128)S(1)} %stack.59.ids_ref, bf16[512,2048]{1,0:T(8,128)(2,1)} %shard_map.124.refs_1_.refs_0_, bf16[512,2048]{1,0:T(8,128)(2,1)} %copy-done.8, bf16[1024,1024]{1,0:T(8,128)(2,1)} %get-tuple-element.20.refs_2_.refs_0_), custom_call_target="tpu_custom_call" | custom-call | tf_op jit(solution)/shard_map/pallas_call | solution.py:52
  175.4 9.9 %shard_map.129.refs_0_.refs_2_ = bf16[1024,1024]{1,0:T(8,128)(2,1)} custom-call(s32[9]{0:T(128)S(1)} %stack.59.ids_ref, bf16[512,2048]{1,0:T(8,128)(2,1)} %shard_map.124.refs_1_.refs_0_, bf16[512,2048]{1,0:T(8,128)(2,1)} %copy-done.8, bf16[2048,2048]{1,0:T(8,128)(2,1)} %all-gather.2.cloned.1.call-done.refs_2_.refs_1_, ...), custom_call_target="tpu_custom_call" | custom-call | tf_op jit(solution)/shard_map/pallas_call | solution.py:52
  185.3 6.9 %shard_map.130.refs_3_ = bf16[512,2048]{1,0:T(8,128)(2,1)} custom-call(s32[9]{0:T(128)S(1)} %stack.59.ids_ref, bf16[1024,1024]{1,0:T(8,128)(2,1)} %shard_map.129.refs_0_.refs_2_, bf16[2048,1024]{1,0:T(8,128)(2,1)} %shard_map.123.refs_5_.refs_2_.refs_1_), custom_call_target="tpu_custom_call" | custom-call | tf_op jit(solution)/shard_map/pallas_call | solution.py:52
  192.4 11.2 %shard_map.131 = (bf16[512,1024]{1,0:T(8,128)(2,1)S(1)}, bf16[512,1024]{1,0:T(8,128)(2,1)}, bf16[512,1024]{1,0:T(8,128)(2,1)}, bf16[512,1024]{1,0:T(8,128)(2,1)}) custom-call(s32[9]{0:T(128)S(1)} %stack.59.ids_ref, bf16[512,2048]{1,0:T(8,128)(2,1)} %shard_map.126.refs_0_, bf16[512,2048]{1,0:T(8,128)(2,1)} %copy-done.9, ...), custom_call_target="tpu_custom_call" | custom-call | tf_op jit(solution)/shard_map/pallas_call | solution.py:52
  207.2 7.2 %shard_map.132 = (bf16[512,512]{1,0:T(8,128)(2,1)S(1)}, bf16[512,512]{1,0:T(8,128)(2,1)S(1)}, bf16[512,512]{1,0:T(8,128)(2,1)S(1)}, bf16[512,512]{1,0:T(8,128)(2,1)}, bf16[512,512]{1,0:T(8,128)(2,1)}) custom-call(s32[9]{0:T(128)S(1)} %stack.59.ids_ref, bf16[1024,1024]{1,0:T(8,128)(2,1)} %shard_map.129.refs_0_.refs_2_, ...), custom_call_target="tpu_custom_call" | custom-call | tf_op jit(solution)/shard_map/pallas_call | solution.py:52
  214.4 6.7 %shard_map.133 = bf16[512,2048]{1,0:T(8,128)(2,1)} custom-call(s32[9]{0:T(128)S(1)} %stack.59.ids_ref, bf16[1024,1024]{1,0:T(8,128)(2,1)} %get-tuple-element.20.refs_2_.refs_0_, bf16[2048,2048]{1,0:T(8,128)(2,1)} %all-gather.2.cloned.1.call-done.refs_2_.refs_1_, bf16[512,512]{1,0:T(8,128)(2,1)S(1)} %get-tuple-element.23.refs_2_), custom_call_target="tpu_custom_call" | custom-call | tf_op jit(solution)/shard_map/pallas_call | solution.py:52
  231.5 4.5 %collective-permute-done.27 = bf16[512,512]{1,0:T(8,128)(2,1)S(1)} collective-permute-done((bf16[512,512]{1,0:T(8,128)(2,1)S(1)}, bf16[512,512]{1,0:T(8,128)(2,1)S(1)}, u32[]{:S(2)}, u32[]{:S(2)}) %collective-permute-start.27) | collective-permute-done | bytes 524320 | tf_op jit(solution)/shard_map/ppermute | solution.py:327
  237.6 9.2 %collective-permute-done.25 = bf16[512,512]{1,0:T(8,128)(2,1)S(1)} collective-permute-done((bf16[512,512]{1,0:T(8,128)(2,1)S(1)}, bf16[512,512]{1,0:T(8,128)(2,1)S(1)}, u32[]{:S(2)}, u32[]{:S(2)}) %collective-permute-start.25) | collective-permute-done | bytes 524320 | tf_op jit(solution)/shard_map/ppermute | solution.py:328
  252.7 23.2 %collective-permute-done.28 = bf16[512,512]{1,0:T(8,128)(2,1)} collective-permute-done((bf16[512,512]{1,0:T(8,128)(2,1)S(1)}, bf16[512,512]{1,0:T(8,128)(2,1)}, u32[]{:S(2)}, u32[]{:S(2)}) %collective-permute-start.28) | collective-permute-done | bytes 524320 | tf_op jit(solution)/shard_map/ppermute | solution.py:331
  282.9 7.3 %shard_map.134 = (bf16[512,512]{1,0:T(8,128)(2,1)S(1)}, bf16[512,512]{1,0:T(8,128)(2,1)S(1)}, bf16[512,512]{1,0:T(8,128)(2,1)S(1)}, bf16[512,512]{1,0:T(8,128)(2,1)}, bf16[512,512]{1,0:T(8,128)(2,1)}) custom-call(s32[9]{0:T(128)S(1)} %stack.59.ids_ref, bf16[1024,1024]{1,0:T(8,128)(2,1)} %get-tuple-element.20.refs_2_.refs_0_, ...), custom_call_target="tpu_custom_call" | custom-call | tf_op jit(solution)/shard_map/pallas_call | solution.py:52
  296.9 9.3 %collective-permute-done.23 = bf16[512,512]{1,0:T(8,128)(2,1)S(1)} collective-permute-done((bf16[512,512]{1,0:T(8,128)(2,1)}, bf16[512,512]{1,0:T(8,128)(2,1)S(1)}, u32[]{:S(2)}, u32[]{:S(2)}) %collective-permute-start.23) | collective-permute-done | bytes 524320 | tf_op jit(solution)/shard_map/ppermute | solution.py:327
  306.3 3.8 %collective-permute-start.24 = (bf16[512,512]{1,0:T(8,128)(2,1)S(1)}, bf16[512,512]{1,0:T(8,128)(2,1)S(1)}, u32[]{:S(2)}, u32[]{:S(2)}) collective-permute-start(bf16[512,512]{1,0:T(8,128)(2,1)S(1)} %add_convert_fusion.3), channel_id=1, source_target_pairs={{0,2},{1,3},{2,0},{3,1},{4,6},{5,7},{6,4},{7,5},{8,10},{9,11},{10,... | collective-permute-start | bytes 1572872 | tf_op jit(solution)/shard_map/ppermute | solution.py:331
  318.0 5.6 %shard_map.135 = bf16[2,4,64,512]{3,2,1,0:T(8,128)(2,1)} custom-call(s32[9]{0:T(128)S(1)} %stack.59.ids_ref, bf16[2,3,64,512]{3,2,1,0:T(8,128)(2,1)S(1)} %collective-permute-done.32.refs_0_, bf16[2,4,64,512]{3,2,1,0:T(8,128)(2,1)S(1)} %bitcast.48, bf16[2,3,64,512]{3,2,1,0:T(8,128)(2,1)S(1)} %collective-permute-done.33.refs_2_, ...), custom_call_target="tpu_custom_call" | custom-call | tf_op jit(solution)/shard_map/pallas_call | solution.py:52
  323.6 12.4 %collective-permute-done.24 = bf16[512,512]{1,0:T(8,128)(2,1)S(1)} collective-permute-done((bf16[512,512]{1,0:T(8,128)(2,1)S(1)}, bf16[512,512]{1,0:T(8,128)(2,1)S(1)}, u32[]{:S(2)}, u32[]{:S(2)}) %collective-permute-start.24) | collective-permute-done | bytes 524320 | tf_op jit(solution)/shard_map/ppermute | solution.py:331
  (159 shorter events, 99.7 us)
Async XLA Ops:
  8.0 167.4 %all-gather.2.cloned.1.call-start = ((), (), s32[]{:S(2)}) async-start(), calls=%async_computation.1 | async-start | bytes 9437184 | tf_op jit(solution)/shard_map/all_gather | solution.py:433
  8.8 238.9 %reduce-scatter.2.cloned.1.call-start = ((), (), s32[]{:S(2)}) async-start(), calls=%async_computation.2 | async-start | bytes 5242880 | tf_op jit(solution)/shard_map/reduce_scatter | solution.py:457
  25.5 27.5 %collective-permute-start.9 = (bf16[512,512]{1,0:T(8,128)(2,1)S(1)}, bf16[512,512]{1,0:T(8,128)(2,1)S(1)}, u32[]{:S(2)}, u32[]{:S(2)}) collective-permute-start(bf16[512,512]{1,0:T(8,128)(2,1)S(1)} %fusion.refs_0_), channel_id=1, source_target_pairs={{0,2},{1,3},{2,0},{3,1},{4,6},{5,7},{6,4},{7,5},{8,10},{9,11},{10,... | collective-permute-start | bytes 1572872 | tf_op jit(solution)/shard_map/ppermute | solution.py:155
  31.8 34.3 %collective-permute-start.12 = (bf16[512,1024]{1,0:T(8,128)(2,1)}, bf16[512,1024]{1,0:T(8,128)(2,1)}, u32[]{:S(2)}, u32[]{:S(2)}) collective-permute-start(bf16[512,1024]{1,0:T(8,128)(2,1)} %shard_map.121.refs_4_.refs_0_), channel_id=1, source_target_pairs={{0,8},{4,20},{8,24},{12,4},{24,16},{28,12},{16,0},{20,28},{1,9},{5... | collective-permute-start | bytes 3145736 | tf_op jit(solution)/shard_map/ppermute | solution.py:147
  53.0 55.8 %collective-permute-start.10 = (bf16[512,512]{1,0:T(8,128)(2,1)S(1)}, bf16[512,512]{1,0:T(8,128)(2,1)S(1)}, u32[]{:S(2)}, u32[]{:S(2)}) collective-permute-start(bf16[512,512]{1,0:T(8,128)(2,1)S(1)} %fusion.refs_0_), channel_id=1, source_target_pairs={{0,1},{1,2},{2,3},{4,5},{5,6},{6,7},{8,9},{9,10},{10,11},{12,13},{... | collective-permute-start | bytes 1572872 | tf_op jit(solution)/shard_map/ppermute | solution.py:157
  56.2 53.9 %collective-permute-start.8 = (bf16[512,512]{1,0:T(8,128)(2,1)S(1)}, bf16[512,512]{1,0:T(8,128)(2,1)S(1)}, u32[]{:S(2)}, u32[]{:S(2)}) collective-permute-start(bf16[512,512]{1,0:T(8,128)(2,1)S(1)} %fusion.refs_0_), channel_id=1, source_target_pairs={{1,0},{2,1},{3,2},{5,4},{6,5},{7,6},{9,8},{10,9},{11,10},{13,12},{... | collective-permute-start | bytes 1572872 | tf_op jit(solution)/shard_map/ppermute | solution.py:156
  57.6 40.8 %collective-permute-start.13 = (bf16[512,1024]{1,0:T(8,128)(2,1)}, bf16[512,1024]{1,0:T(8,128)(2,1)S(1)}, u32[]{:S(2)}, u32[]{:S(2)}) collective-permute-start(bf16[512,1024]{1,0:T(8,128)(2,1)} %shard_map.121.refs_4_.refs_0_), channel_id=1, source_target_pairs={{0,16},{4,12},{8,0},{12,28},{24,8},{28,20},{16,24},{20,4},{1,17},{... | collective-permute-start | bytes 3145736 | tf_op jit(solution)/shard_map/ppermute | solution.py:148
  64.8 45.3 %collective-permute-start.11 = (bf16[512,512]{1,0:T(8,128)(2,1)S(1)}, bf16[512,512]{1,0:T(8,128)(2,1)S(1)}, u32[]{:S(2)}, u32[]{:S(2)}) collective-permute-start(bf16[512,512]{1,0:T(8,128)(2,1)S(1)} %collective-permute-done.9.refs_2_), channel_id=1, source_target_pairs={{1,0},{2,3},{5,4},{6,7},{9,8},{10,11},{13,12},{14,15},{17,16},{18,... | collective-permute-start | bytes 1572872 | tf_op jit(solution)/shard_map/ppermute | solution.py:160
  66.2 34.5 %collective-permute-start.14 = (bf16[512,1024]{1,0:T(8,128)(2,1)}, bf16[512,1024]{1,0:T(8,128)(2,1)S(1)}, u32[]{:S(2)}, u32[]{:S(2)}) collective-permute-start(bf16[512,1024]{1,0:T(8,128)(2,1)} %collective-permute-done.12.refs_1_), channel_id=1, source_target_pairs={{0,8},{4,20},{8,24},{12,4},{24,16},{28,12},{16,0},{20,28},{1,9},{5... | collective-permute-start | bytes 3145736 | tf_op jit(solution)/shard_map/ppermute | solution.py:149
  98.4 21.4 %collective-permute-start.7 = (bf16[512,512]{1,0:T(8,128)(2,1)S(1)}, bf16[512,512]{1,0:T(8,128)(2,1)S(1)}, u32[]{:S(2)}, u32[]{:S(2)}) collective-permute-start(bf16[512,512]{1,0:T(8,128)(2,1)S(1)} %multiply_convert_fusion.1.refs_0_), channel_id=1, source_target_pairs={{0,2},{1,3},{2,0},{3,1},{4,6},{5,7},{6,4},{7,5},{8,10},{9,11},{10,... | collective-permute-start | bytes 1572872 | tf_op jit(solution)/shard_map/ppermute | solution.py:155
  100.7 21.1 %collective-permute-start.15 = (bf16[512,512]{1,0:T(8,128)(2,1)S(1)}, bf16[512,512]{1,0:T(8,128)(2,1)S(1)}, u32[]{:S(2)}, u32[]{:S(2)}) collective-permute-start(bf16[512,512]{1,0:T(8,128)(2,1)S(1)} %multiply_convert_fusion.1.refs_0_), channel_id=1, source_target_pairs={{0,1},{1,2},{2,3},{4,5},{5,6},{6,7},{8,9},{9,10},{10,11},{12,13},{... | collective-permute-start | bytes 1572872 | tf_op jit(solution)/shard_map/ppermute | solution.py:157
  108.8 20.9 %collective-permute-start.6 = (bf16[512,512]{1,0:T(8,128)(2,1)S(1)}, bf16[512,512]{1,0:T(8,128)(2,1)S(1)}, u32[]{:S(2)}, u32[]{:S(2)}) collective-permute-start(bf16[512,512]{1,0:T(8,128)(2,1)S(1)} %multiply_convert_fusion.1.refs_0_), channel_id=1, source_target_pairs={{1,0},{2,1},{3,2},{5,4},{6,5},{7,6},{9,8},{10,9},{11,10},{13,12},{... | collective-permute-start | bytes 1572872 | tf_op jit(solution)/shard_map/ppermute | solution.py:156
  120.3 20.5 %collective-permute-start.16 = (bf16[512,512]{1,0:T(8,128)(2,1)S(1)}, bf16[512,512]{1,0:T(8,128)(2,1)S(1)}, u32[]{:S(2)}, u32[]{:S(2)}) collective-permute-start(bf16[512,512]{1,0:T(8,128)(2,1)S(1)} %shard_map.125.refs_2_), channel_id=1, source_target_pairs={{1,0},{2,3},{5,4},{6,7},{9,8},{10,11},{13,12},{14,15},{17,16},{18,... | collective-permute-start | bytes 1572872 | tf_op jit(solution)/shard_map/ppermute | solution.py:160
  203.6 24.0 %collective-permute-start.34 = (bf16[512,1024]{1,0:T(8,128)(2,1)S(1)}, bf16[512,1024]{1,0:T(8,128)(2,1)S(1)}, u32[]{:S(2)}, u32[]{:S(2)}) collective-permute-start(bf16[512,1024]{1,0:T(8,128)(2,1)S(1)} %get-tuple-element.22.refs_3_), channel_id=1, source_target_pairs={{0,16},{4,12},{8,0},{12,28},{24,8},{28,20},{16,24},{20,4},{1,17},{... | collective-permute-start | bytes 3145736 | tf_op jit(solution)/shard_map/ppermute | solution.py:337
  221.1 61.7 %collective-permute-start.20 = (bf16[512,2048]{1,0:T(8,128)(2,1)}, bf16[512,2048]{1,0:T(8,128)(2,1)}, u32[]{:S(2)}, u32[]{:S(2)}) collective-permute-start(bf16[512,2048]{1,0:T(8,128)(2,1)} %shard_map.133), channel_id=1, source_target_pairs={{0,4},{4,0},{8,12},{12,8},{16,20},{20,16},{24,28},{28,24},{1,5},{5... | collective-permute-start | bytes 6291464 | tf_op jit(solution)/shard_map/ppermute | solution.py:431
  223.8 54.1 %collective-permute-start.36 = (bf16[512,1024]{1,0:T(8,128)(2,1)}, bf16[512,1024]{1,0:T(8,128)(2,1)}, u32[]{:S(2)}, u32[]{:S(2)}) collective-permute-start(bf16[512,1024]{1,0:T(8,128)(2,1)} %get-tuple-element.35), channel_id=1, source_target_pairs={{0,8},{4,20},{8,24},{12,4},{24,16},{28,12},{16,0},{20,28},{1,9},{5... | collective-permute-start | bytes 3145736 | tf_op jit(solution)/shard_map/ppermute | solution.py:338
  224.2 22.7 %collective-permute-start.25 = (bf16[512,512]{1,0:T(8,128)(2,1)S(1)}, bf16[512,512]{1,0:T(8,128)(2,1)S(1)}, u32[]{:S(2)}, u32[]{:S(2)}) collective-permute-start(bf16[512,512]{1,0:T(8,128)(2,1)S(1)} %get-tuple-element.29), channel_id=1, source_target_pairs={{0,1},{1,2},{2,3},{4,5},{5,6},{6,7},{8,9},{9,10},{10,11},{12,13},{... | collective-permute-start | bytes 1572872 | tf_op jit(solution)/shard_map/ppermute | solution.py:328
  229.0 49.0 %collective-permute-start.35 = (bf16[512,1024]{1,0:T(8,128)(2,1)}, bf16[512,1024]{1,0:T(8,128)(2,1)}, u32[]{:S(2)}, u32[]{:S(2)}) collective-permute-start(bf16[512,1024]{1,0:T(8,128)(2,1)} %add_convert_fusion.1), channel_id=1, source_target_pairs={{0,16},{4,12},{8,0},{12,28},{24,8},{28,20},{16,24},{20,4},{1,17},{... | collective-permute-start | bytes 3145736 | tf_op jit(solution)/shard_map/ppermute | solution.py:339
  247.7 28.2 %collective-permute-start.28 = (bf16[512,512]{1,0:T(8,128)(2,1)S(1)}, bf16[512,512]{1,0:T(8,128)(2,1)}, u32[]{:S(2)}, u32[]{:S(2)}) collective-permute-start(bf16[512,512]{1,0:T(8,128)(2,1)S(1)} %add_convert_fusion.2), channel_id=1, source_target_pairs={{0,2},{1,3},{2,0},{3,1},{4,6},{5,7},{6,4},{7,5},{8,10},{9,11},{10,... | collective-permute-start | bytes 1572872 | tf_op jit(solution)/shard_map/ppermute | solution.py:331
  252.7 57.6 %collective-permute-start.38 = (bf16[256,1024]{1,0:T(8,128)(2,1)S(1)}, bf16[256,1024]{1,0:T(8,128)(2,1)S(1)}, u32[]{:S(2)}, u32[]{:S(2)}) collective-permute-start(bf16[256,1024]{1,0:T(8,128)(2,1)S(1)} %shard_map.138), channel_id=1, source_target_pairs={{0,4},{4,0},{8,12},{12,8},{16,20},{20,16},{24,28},{28,24},{1,5},{5... | collective-permute-start | bytes 1572872 | tf_op jit(solution)/shard_map/ppermute | solution.py:354
  282.8 28.7 %collective-permute-start.37 = (bf16[256,1024]{1,0:T(8,128)(2,1)S(1)}, bf16[256,1024]{1,0:T(8,128)(2,1)S(1)}, u32[]{:S(2)}, u32[]{:S(2)}) collective-permute-start(bf16[256,1024]{1,0:T(8,128)(2,1)S(1)} %shard_map.136), channel_id=1, source_target_pairs={{0,4},{4,0},{8,12},{12,8},{16,20},{20,16},{24,28},{28,24},{1,5},{5... | collective-permute-start | bytes 1572872 | tf_op jit(solution)/shard_map/ppermute | solution.py:354
  294.1 29.4 %collective-permute-start.21 = (bf16[512,512]{1,0:T(8,128)(2,1)S(1)}, bf16[512,512]{1,0:T(8,128)(2,1)S(1)}, u32[]{:S(2)}, u32[]{:S(2)}) collective-permute-start(bf16[512,512]{1,0:T(8,128)(2,1)S(1)} %get-tuple-element.25), channel_id=1, source_target_pairs={{0,1},{1,2},{2,3},{4,5},{5,6},{6,7},{8,9},{9,10},{10,11},{12,13},{... | collective-permute-start | bytes 1572872 | tf_op jit(solution)/shard_map/ppermute | solution.py:328
  295.6 28.0 %collective-permute-start.22 = (bf16[512,512]{1,0:T(8,128)(2,1)S(1)}, bf16[512,512]{1,0:T(8,128)(2,1)S(1)}, u32[]{:S(2)}, u32[]{:S(2)}) collective-permute-start(bf16[512,512]{1,0:T(8,128)(2,1)S(1)} %copy-done.23), channel_id=1, source_target_pairs={{1,0},{2,1},{3,2},{5,4},{6,5},{7,6},{9,8},{10,9},{11,10},{13,12},{... | collective-permute-start | bytes 1572872 | tf_op jit(solution)/shard_map/ppermute | solution.py:329
  306.3 29.7 %collective-permute-start.24 = (bf16[512,512]{1,0:T(8,128)(2,1)S(1)}, bf16[512,512]{1,0:T(8,128)(2,1)S(1)}, u32[]{:S(2)}, u32[]{:S(2)}) collective-permute-start(bf16[512,512]{1,0:T(8,128)(2,1)S(1)} %add_convert_fusion.3), channel_id=1, source_target_pairs={{0,2},{1,3},{2,0},{3,1},{4,6},{5,7},{6,4},{7,5},{8,10},{9,11},{10,... | collective-permute-start | bytes 1572872 | tf_op jit(solution)/shard_map/ppermute | solution.py:331
  (42 other events, 485.1 us)
Sparse Core Ops, SparseCore 0:
  10.8 79.3 all-gather.1
Sparse Core Ops, SparseCore 1:
  175.4 57.1 reduce-scatter.1

commit v3 on v0

--- a/solution.py
+++ b/solution.py
@@ -1,10 +1,450 @@
+import functools
+
 import jax
 import jax.numpy as jnp
+import numpy as np
 from jax import lax
+from jax.experimental import pallas as pl
+from jax.experimental.pallas import tpu as pltpu
 from jax.sharding import PartitionSpec as P
 
 C = 2048
 KS = 7
+REACH = KS // 2
+F32 = jnp.float32
+BF16 = jnp.bfloat16
+LAST = (((1,), (1,)), ((), ()))
+FIRST = (((0,), (0,)), ((), ()))
+SIBLING = [(i, i ^ 1) for i in range(8)]
+UP = [(0, 1), (1, 2), (2, 3)]
+DOWN = [(1, 0), (2, 1), (3, 2)]
+ACROSS = [(0, 2), (1, 3), (2, 0), (3, 1)]
+SAME_CORE = [[0, 2, 4, 6], [1, 3, 5, 7]]
+ANY = pl.BlockSpec(memory_space=pl.ANY)
+VMEM = pl.BlockSpec(memory_space=pltpu.VMEM)
+PARAMS = pltpu.CompilerParams(vmem_limit_bytes=52 * 2**20)
+HINT = pl.CostEstimate(flops=0, bytes_accessed=0, transcendentals=0)
+WORK = pl.CostEstimate(flops=2**32, bytes_accessed=12 * 2**20, transcendentals=0)
+
+
+def shape(dims, dtype=BF16):
+    return jax.ShapeDtypeStruct(dims, dtype)
+
+
+def call(
+    body, ids, arrays, grid, ins, outs, shapes, scratch=(), after=(), aliases=None
+):
+    count = len(arrays)
+
+    def kernel(ids_ref, *refs):
+        body(ids_ref, *refs[:count], *refs[count + len(after) :])
+
+    return pl.pallas_call(
+        kernel,
+        grid_spec=pltpu.PrefetchScalarGridSpec(
+            num_scalar_prefetch=1,
+            grid=grid,
+            in_specs=list(ins) + [ANY] * len(after),
+            out_specs=outs,
+            scratch_shapes=scratch,
+        ),
+        out_shape=shapes,
+        compiler_params=PARAMS,
+        cost_estimate=WORK if grid else HINT,
+        input_output_aliases=aliases or {},
+    )(ids, *arrays, *after)
+
+
+def later(ids, array, after):
+    return call(
+        lambda *refs: None, ids, [array], (), [ANY], ANY, shape(array.shape, array.dtype),
+        after=after, aliases={1: 0},
+    )
+
+
+def whole(dims):
+    return pl.BlockSpec(dims, lambda *_: (0,) * len(dims))
+
+
+def make_ids():
+    table = np.zeros((8, 4, 5), np.int32)
+    for row in range(8):
+        for z in range(4):
+            table[row, z] = [z, (z + 1) % 4, (z + 2) % 4, (z + 3) % 4, row % 2]
+    place = (lax.axis_index("row"), lax.axis_index("col"), 0)
+    return lax.dynamic_slice(jnp.asarray(table), place, (1, 1, 5)).reshape(5)
+
+
+def move(body, ids, arrays, shapes, count, after=()):
+    def kernel(ids_ref, *refs):
+        sems = refs[-1]
+        pairs = list(body(ids_ref, refs[: len(arrays)], refs[len(arrays) : -1]))
+        copies = [pltpu.make_async_copy(src, dst, sems.at[i]) for i, (_, src, dst) in enumerate(pairs)]
+        for (when, _, _), copy in zip(pairs, copies):
+            if when is None:
+                copy.start()
+            else:
+                pl.when(when)(copy.start)
+        for (when, _, _), copy in zip(pairs, copies):
+            if when is None:
+                copy.wait()
+            else:
+                pl.when(when)(copy.wait)
+
+    return call(
+        kernel, ids, arrays, (), [ANY] * len(arrays), [VMEM] * len(shapes), shapes,
+        [pltpu.SemaphoreType.DMA((count,))], after,
+    )
+
+
+def start_of(index, size):
+    return pl.ds(pl.multiple_of(index * size, size), size)
+
+
+def col_send(block):
+    across = lax.ppermute(block, "col", ACROSS)
+    above = lax.ppermute(block, "col", DOWN)
+    below = lax.ppermute(block, "col", UP)
+    return block, above, across, below
+
+
+def col_gather(ids, parts, before_far):
+    block, above, across, below = parts
+    rows, cols = block.shape
+    across = later(ids, across, before_far)
+    far = lax.ppermute(across, "col", [(1, 0), (2, 3)])
+
+    def body(i, s, t):
+        def to(k):
+            return t[0].at[:, start_of(i[k], cols)]
+
+        z = i[0]
+        yield None, s[0], to(0)
+        yield None, s[2], to(2)
+        yield z < 3, s[1], to(1)
+        yield z == 3, s[4], to(1)
+        yield z > 0, s[3], to(3)
+        yield z == 0, s[4], to(3)
+
+    return move(
+        body, ids, [block, above, across, below, far], [shape((rows, 4 * cols))], 6
+    )[0]
+
+
+def normalize(ids, parts, scale, gains):
+    rows, cols = scale.shape[0], parts[0].shape[1]
+
+    def kernel(ids_ref, *refs):
+        scale_ref, gain_ref, out_ref = refs[4:]
+        inverse = scale_ref[:, 4:5]
+        for k, place in enumerate((0, 3, 2, 1)):
+            value = (refs[k][:rows].astype(F32) + scale_ref[:, k : k + 1]) * inverse
+            value = value * gain_ref[k : k + 1]
+            out_ref[:, start_of(ids_ref[place], cols)] = value.astype(BF16)
+
+    return call(
+        kernel, ids, [*parts, scale, gains], (), [VMEM] * 6, VMEM, shape((rows, 4 * cols))
+    )
+
+
+def gelu_parts(v):
+    cdf = 0.5 * (1.0 + lax.erf(v * 0.7071067811865476))
+    return v * cdf, cdf + v * jnp.exp(-0.5 * v * v) * 0.3989422804014327
+
+
+TILE = 256
+
+
+def expand(ids, rows, panel, after=()):
+    hid = panel.shape[1] // 2
+    steps = hid // TILE
+
+    def kernel(ids_ref, x_ref, w_ref, hidden_ref, slope_ref):
+        pre = jnp.dot(x_ref[...], w_ref[...], preferred_element_type=F32)
+        act, slope = gelu_parts(pre)
+        hidden_ref[...] = act.astype(BF16)
+        slope_ref[...] = slope.astype(BF16)
+
+    tile = pl.BlockSpec((rows.shape[0], TILE), lambda t, i: (0, t))
+    return call(
+        kernel, ids, [rows, panel], (steps,),
+        [whole(rows.shape), pl.BlockSpec((C, TILE), lambda t, i: (0, i[4] * steps + t))],
+        [tile, tile], [shape((rows.shape[0], hid))] * 2, after=after,
+    )
+
+
+def expand_grad(ids, strips, panel, slopes, after):
+    rows, hid = slopes[0].shape
+    steps = hid // TILE
+
+    def kernel(ids_ref, own_ref, sib_ref, w_ref, own_slope, sib_slope, own_out, sib_out):
+        for x, slope, out in ((own_ref, own_slope, own_out), (sib_ref, sib_slope, sib_out)):
+            back = jnp.dot(x[...], w_ref[...], preferred_element_type=F32)
+            out[...] = (back * slope[...].astype(F32)).astype(BF16)
+
+    tile = pl.BlockSpec((rows, TILE), lambda t, i: (0, t))
+    return call(
+        kernel, ids, [*strips, panel, *slopes], (steps,),
+        [
+            whole(strips[0].shape),
+            whole(strips[1].shape),
+            pl.BlockSpec((C, TILE), lambda t, i: (0, i[4] * steps + t)),
+            tile,
+            tile,
+        ],
+        [tile, tile], [shape((rows, hid))] * 2, after=after,
+    )
+
+
+def weight_grad(ids, own, sib, right, after=()):
+    rows = own.shape[0]
+    hid = right[0].shape[1]
+    size = C // 4
+
+    def kernel(ids_ref, own_ref, sib_ref, own_right, sib_right, out_ref):
+        acc = lax.dot_general(own_ref[...], own_right[...], FIRST, preferred_element_type=F32)
+        acc += lax.dot_general(sib_ref[...], sib_right[...], FIRST, preferred_element_type=F32)
+        out_ref[...] = acc.astype(BF16)
+
+    cut = pl.BlockSpec((rows, size), lambda t, i: (0, t))
+    return call(
+        kernel, ids, [own, sib, *right], (4,), [cut, cut] + [whole((rows, hid))] * 2,
+        pl.BlockSpec((size, hid), lambda t, i: (t, 0)), shape((C, hid)), after=after,
+    )
+
+
+def contract(ids, left, panel, other=None, after=()):
+    rows, hid = left.shape
+
+    def kernel(ids_ref, x_ref, w_ref, *refs):
+        acc = lax.dot_general(x_ref[...], w_ref[...], LAST, preferred_element_type=F32)
+        if other is not None:
+            acc = acc + refs[0][...].astype(F32)
+        refs[-1][...] = acc.astype(BF16)
+
+    cut = pl.BlockSpec((rows, 512), lambda t, i: (0, t))
+    more = [] if other is None else [other]
+    return call(
+        kernel, ids, [left, panel, *more], (C // 512,),
+        [whole((rows, hid)), pl.BlockSpec((512, hid), lambda t, i: (t, i[4]))] + [cut] * len(more),
+        cut, shape((rows, C)), after=after,
+    )
+
+
+def contract_own(ids, left, panel, other, after=()):
+    rows, hid = left.shape
+
+    def kernel(ids_ref, x_ref, w_ref, o_ref, *outs):
+        acc = lax.dot_general(x_ref[...], w_ref[...], LAST, preferred_element_type=F32)
+        acc = (acc + o_ref[...].astype(F32)).astype(BF16)
+        for k in range(4):
+            @pl.when(pl.program_id(0) == k)
+            def _():
+                outs[k][...] = acc
+
+    return call(
+        kernel, ids, [left, panel, other], (4,),
+        [
+            whole((rows, hid)),
+            pl.BlockSpec((512, hid), lambda t, i: (i[t], i[4])),
+            pl.BlockSpec((rows, 512), lambda t, i: (0, i[t])),
+        ],
+        [whole((rows, 512))] * 4, [shape((rows, 512))] * 4, after=after,
+    )
+
+
+def give_rows(ids, block, after):
+    rows, cols = block.shape
+
+    def body(i, s, t):
+        yield None, s[0].at[start_of(1 - i[4], rows // 2)], t[0]
+
+    return move(body, ids, [block], [shape((rows // 2, cols))], 1, after)[0]
+
+
+def own_rows(ids, block, after=()):
+    rows, cols = block.shape
+    other = lax.ppermute(give_rows(ids, block, after), "row", SIBLING)
+
+    def body(i, s, t):
+        yield None, s[0].at[start_of(i[4], rows // 2)], t[0].at[:, start_of(i[4], cols)]
+        yield None, s[1], t[0].at[:, start_of(1 - i[4], cols)]
+
+    return move(body, ids, [block, other], [shape((rows // 2, 2 * cols))], 2)[0]
+
+
+def taps(ids, low, mid, high, dw_kernel, flipped, extra=None, after=()):
+    images, rows, width, chans = mid.shape
+    lanes = 128
+    edge = 8
+
+    def kernel(ids_ref, *refs):
+        low_ref, mid_ref, high_ref, dw_ref = refs[:4]
+        outs, pad_ref = refs[4 + (extra is not None) : -1], refs[-1]
+        pad_ref[:, :edge] = jnp.zeros((rows + 2 * REACH, edge, lanes), F32)
+        pad_ref[:, edge + width :] = jnp.zeros((rows + 2 * REACH, edge, lanes), F32)
+
+        @pl.loop(0, chans // lanes)
+        def _(chunk):
+            lane = start_of(chunk, lanes)
+            pad_ref[:REACH, edge : edge + width] = low_ref[0, :, :, lane].astype(F32)
+            pad_ref[REACH : REACH + rows, edge : edge + width] = mid_ref[0, :, :, lane].astype(F32)
+            pad_ref[REACH + rows :, edge : edge + width] = high_ref[0, :, :, lane].astype(F32)
+            totals = [jnp.zeros((width, lanes), F32)] * rows
+            for off_col in range(KS):
+                tap_col = KS - 1 - off_col if flipped else off_col
+                for place in range(rows + 2 * REACH):
+                    line = pad_ref[place, pl.ds(edge - REACH + off_col, width)]
+                    for row in range(rows):
+                        off_row = place - row
+                        if 0 <= off_row < KS:
+                            tap_row = KS - 1 - off_row if flipped else off_row
+                            totals[row] += dw_ref[pl.ds(tap_row * KS + tap_col, 1), lane] * line
+            for row in range(rows):
+                if extra is None:
+                    outs[0][0, row, :, lane] = totals[row]
+                else:
+                    total = refs[4][0, row, :, lane].astype(F32) + totals[row]
+                    outs[0][0, row, :, lane] = total.astype(BF16)
+
+        if extra is None:
+            for row in range(rows):
+                value = outs[0][0, row]
+                mean = jnp.sum(value, axis=1, keepdims=True) * (1.0 / chans)
+                value = value - mean
+                outs[0][0, row] = value
+                outs[1][0, row] = value.astype(BF16)
+                outs[2][0, row] = mean
+                outs[3][0, row] = jnp.sum(value * value, axis=1, keepdims=True)
+
+    def strip(count, last=chans):
+        return pl.BlockSpec((1, count, width, last), lambda b, i: (b, 0, 0, 0))
+
+    arrays = [low, mid, high, dw_kernel.reshape(KS * KS, chans)]
+    ins = [strip(REACH), strip(rows), strip(REACH), whole((KS * KS, chans))]
+    if extra is None:
+        thin = shape((images, rows, width, 1), F32)
+        outs = [strip(rows), strip(rows), strip(rows, 1), strip(rows, 1)]
+        shapes = [shape(mid.shape, F32), shape(mid.shape), thin, thin]
+    else:
+        arrays.append(extra)
+        ins.append(strip(rows))
+        outs, shapes = strip(rows), shape(mid.shape)
+    return call(
+        kernel, ids, arrays, (images,), ins, outs, shapes,
+        [pltpu.VMEM((rows + 2 * REACH, width + 2 * edge, lanes), F32)], after,
+    )
+
+
+def rims(block):
+    count = lax.axis_size("row")
+    forward = [(i, i + 1) for i in range(count - 1)]
+    backward = [(i + 1, i) for i in range(count - 1)]
+    low = lax.ppermute(block[:, -REACH:], "row", forward)
+    high = lax.ppermute(block[:, :REACH], "row", backward)
+    return low, high
+
+
+def split(row):
+    high = lax.reduce_precision(row, 8, 7)
+    mid = lax.reduce_precision(row - high, 8, 7)
+    return [part.astype(BF16) for part in (high, mid, row - high - mid)]
+
+
+def joined(rows):
+    return rows[0].astype(F32) + rows[1].astype(F32) + rows[2].astype(F32)
+
+
+def shifted(array, step):
+    count = lax.axis_size("col")
+    return lax.ppermute(array, "col", [(i, (i + step) % count) for i in range(count)])
+
+
+def added(blocks):
+    total = blocks[0].astype(F32)
+    for block in blocks[1:]:
+        total = total + block.astype(F32)
+    return total
+
+
+def row_scatter(whole_rows):
+    return lax.psum_scatter(
+        whole_rows, "row", scatter_dimension=0, tiled=True, axis_index_groups=SAME_CORE
+    )
+
+
+def on_device(images, dw_kernel, norm_gain, proj_in, proj_out, layer_scale, cotangent):
+    local_ch = images.shape[3]
+    pixels = images.shape[0] * images.shape[1] * images.shape[2]
+    ids = make_ids()
+
+    def swap(block):
+        return lax.ppermute(block, "row", SIBLING)
+
+    in_panel = lax.all_gather(proj_in, "row", axis=0, tiled=True)
+    out_panel = lax.all_gather(proj_out, "row", axis=0, tiled=True)
+    cot_flat = cotangent.reshape(pixels, local_ch).astype(F32)
+    grad_branch = (cot_flat * layer_scale).astype(BF16)
+    grad_parts = col_send(grad_branch)
+    low, high = rims(images)
+    centred, rounded, own_mean, own_square = taps(
+        ids, low, images, high, dw_kernel, False, after=[grad_parts[1], grad_parts[3]]
+    )
+    centred = centred.reshape(pixels, local_ch)
+    stats = [own_mean.reshape(pixels), own_square.reshape(pixels), norm_gain]
+    extra = jnp.stack(split(stats[0]) + split(stats[1]) + split(stats[2]))
+    extra = jnp.pad(extra, ((0, 16 - extra.shape[0]), (0, 0)))
+    rounded = jnp.concatenate([rounded.reshape(pixels, local_ch), extra])
+    parts = [rounded] + [shifted(rounded, step) for step in (1, 2, 3)]
+    grad_own = col_gather(ids, grad_parts, before_far=[rounded])
+    grad_sib = swap(grad_own)
+
+    means, squares, gains = (
+        jnp.stack([stats[k]] + [joined(part[pixels + 3 * k :]) for part in parts[1:]])
+        for k in range(3)
+    )
+    row_mean = jnp.mean(means, axis=0)
+    shifts = means - row_mean
+    squares = squares + local_ch * (shifts * shifts)
+    inv_std = lax.rsqrt(jnp.sum(squares, axis=0) / C + 1e-06)
+    scale = jnp.concatenate([shifts, inv_std[None]]).T
+    normed = (centred + shifts[0][:, None]) * inv_std[:, None]
+    in_own = normalize(ids, parts, later(ids, scale, [grad_own]), gains)
+    in_sib = swap(in_own)
+
+    hidden_own, slope_own = expand(ids, in_own, in_panel)
+    hidden_sib, slope_sib = expand(ids, in_sib, in_panel, [hidden_own])
+    hidden = hidden_own, hidden_sib
+    out_part = weight_grad(ids, grad_own, grad_sib, hidden)
+    out_rows = row_scatter(out_part)
+    grad_pre = expand_grad(
+        ids, (grad_own, grad_sib), out_panel, (slope_own, slope_sib), [out_part]
+    )
+    back_give = contract(ids, grad_pre[1], in_panel)
+    back_sib = swap(back_give)
+    in_part = weight_grad(ids, in_own, in_sib, grad_pre, [back_give])
+    in_rows = row_scatter(in_part)
+    branch_give = contract(ids, hidden_sib, out_panel, None, [in_part])
+    branch_sib = swap(branch_give)
+    back = contract_own(ids, grad_pre[0], in_panel, back_sib, [branch_give])
+    back_sent = [shifted(back[step], step) for step in (1, 2, 3)]
+    branch = contract_own(ids, hidden_own, out_panel, branch_sib, [back[0]])
+    back_sent[0] = later(ids, back_sent[0], [branch[0], *back_sent[1:]])
+    grad_scaled = added([back[0], *back_sent])
+    weighted = grad_scaled * norm_gain
+    sums = jnp.stack([jnp.sum(weighted, axis=1), jnp.sum(weighted * normed, axis=1)])
+    sums = sums + shifted(sums, 1) + shifted(sums, 2) + shifted(sums, 3)
+    branch_sent = [shifted(later(ids, branch[step], [sums]), step) for step in (1, 2, 3)]
+    branch = added([branch[0], *branch_sent])
+    residual_in = images.reshape(pixels, local_ch).astype(F32)
+    block_out = (residual_in + layer_scale * branch).astype(BF16).reshape(images.shape)
+    grad_conv = inv_std[:, None] * (
+        weighted - sums[0][:, None] / C - normed * sums[1][:, None] / C
+    )
+    grad_conv = grad_conv.astype(BF16).reshape(images.shape)
+    low, high = rims(grad_conv)
+    grad_images = taps(ids, low, grad_conv, high, dw_kernel, True, cotangent)
+    return block_out, grad_images, own_rows(ids, in_rows, [grad_images]), own_rows(ids, out_rows)
 
 
 def with_halo(block, sides, width):
@@ -42,7 +482,7 @@
     )
 
 
-def on_device(images, dw_kernel, norm_gain, proj_in, proj_out, layer_scale, cotangent):
+def on_any_mesh(images, dw_kernel, norm_gain, proj_in, proj_out, layer_scale, cotangent):
     img_batch, strip_rows, img_cols, local_ch = images.shape
     pixels = img_batch * strip_rows * img_cols
     reach = KS // 2
@@ -111,6 +551,7 @@
 
 
 def solution(mesh):
+    tuned = mesh.shape["row"] == 8 and mesh.shape["col"] == 4
     placed = (
         P(None, "row", None, "col"),
         P(None, None, "col"),
@@ -121,7 +562,7 @@
         P(None, "row", None, "col"),
     )
     return jax.shard_map(
-        on_device,
+        on_device if tuned else on_any_mesh,
         mesh=mesh,
         in_specs=placed,
         out_specs=(

time: 534 us -> 305 us (0.57)
  the two profiles are of different devices: /device:TPU:0 before, /device:TPU:12 now
where the time goes in v3:
time: 305 us; the launch traced here: 304 us
  waiting for transfers between devices  129 us (42%)
  Pallas kernels  95 us (31%)
  starting transfers between devices  40.3 us (13%)
  local copies, waits for them, and re-layouts  19.4 us (6%)
  between operations  14.3 us (5%)
  other arithmetic  5.47 us (2%)
    pallas_call x23, Pallas kernels, call(): pl.pallas_call(kernel, grid_spec=pltpu.PrefetchScalarGridSpec(num_scalar_...  95 us
    ppermute x12, waiting for transfers between devices, shifted(): lax.ppermute(array, 'col', [(i, (i + step) % count) for i in range(count)])  90 us
    ppermute x1, waiting for transfers between devices, col_gather(): far = lax.ppermute(across, 'col', [(1, 0), (2, 3)])  19.1 us
    unnamed x66, local copies, waits for them, and re-layouts  17.3 us
    ppermute x12, starting transfers between devices, shifted(): lax.ppermute(array, 'col', [(i, (i + step) % count) for i in range(count)])  14.9 us
    ppermute x2, waiting for transfers between devices, rims(): high = lax.ppermute(block[:, :REACH], 'row', backward)  11 us
    ppermute x2, waiting for transfers between devices, rims(): low = lax.ppermute(block[:, -REACH:], 'row', forward)  6.11 us
  transfers between devices with their start and end apart: 30, of which 14 were waited for; matrix products, arithmetic and copies ran while one was open for 2% of the time, Pallas kernels for 31%

profile of v3, /device:TPU:12, one launch (start us, length us, event | category | flops | bytes accessed | tf_op | source)
XLA Modules:
  0.0 303.8 jit_solution(8749387593032316949)
XLA Ops:
  8.9 3.5 %collective-permute-start.3 = (bf16[512,512]{1,0:T(8,128)(2,1)S(1)}, bf16[512,512]{1,0:T(8,128)(2,1)S(1)}, u32[]{:S(2)}, u32[]{:S(2)}) collective-permute-start(bf16[512,512]{1,0:T(8,128)(2,1)S(1)} %fusion.1.refs_0_), channel_id=1, source_target_pairs={{0,1},{1,2},{2,3},{4,5},{5,6},{6,7},{8,9},{9,10},{10,11},{12,13},{... | collective-permute-start | bytes 1572872 | tf_op jit(solution)/shard_map/ppermute | solution.py:107
  23.5 11.0 %collective-permute-done.1.refs_2_ = bf16[2,3,64,512]{3,2,1,0:T(8,128)(2,1)S(1)} collective-permute-done((bf16[2,3,64,512]{3,2,1,0:T(8,128)(2,1)}, bf16[2,3,64,512]{3,2,1,0:T(8,128)(2,1)S(1)}, u32[]{:S(2)}, u32[]{:S(2)}) %collective-permute-start.1) | collective-permute-done | bytes 393248 | tf_op jit(solution)/shard_map/ppermute | solution.py:344
  34.5 4.8 %collective-permute-done.refs_0_ = bf16[2,3,64,512]{3,2,1,0:T(8,128)(2,1)S(1)} collective-permute-done((bf16[2,3,64,512]{3,2,1,0:T(8,128)(2,1)}, bf16[2,3,64,512]{3,2,1,0:T(8,128)(2,1)S(1)}, u32[]{:S(2)}, u32[]{:S(2)}) %collective-permute-start) | collective-permute-done | bytes 393248 | tf_op jit(solution)/shard_map/ppermute | solution.py:343
  42.6 6.3 %shard_map.111 = (f32[2,4,64,512]{3,2,1,0:T(8,128)}, bf16[2,4,64,512]{3,2,1,0:T(8,128)(2,1)S(1)}, f32[2,4,64,1]{3,2,1,0:T(8,128)S(1)}, f32[2,4,64,1]{3,2,1,0:T(8,128)S(1)}) custom-call(s32[5]{0:T(128)S(1)} %dynamic-slice_bitcast_fusion.ids_ref, bf16[2,3,64,512]{3,2,1,0:T(8,128)(2,1)S(1)} %copy-done.14, bf16[2,4,64,512]{3,2,1,0:T(8,128)(2,1)} %refs_1_.1, ...), custom_call_target="tpu_custom_call" | custom-call | flops 4294967296 | bytes 12582912 | tf_op jit(solution)/shard_map/pallas_call | solution.py:42
  50.1 6.1 %collective-permute-start.8 = (bf16[512,512]{1,0:T(8,128)(2,1)S(1)}, bf16[512,512]{1,0:T(8,128)(2,1)S(1)}, u32[]{:S(2)}, u32[]{:S(2)}) collective-permute-start(bf16[512,512]{1,0:T(8,128)(2,1)S(1)} %shard_map.112.refs_2_), channel_id=1, source_target_pairs={{1,0},{2,3},{5,4},{6,7},{9,8},{10,11},{13,12},{14,15},{17,16},{18,... | collective-permute-start | bytes 1572872 | tf_op jit(solution)/shard_map/ppermute | solution.py:115
  57.1 19.1 %collective-permute-done.8.refs_4_ = bf16[512,512]{1,0:T(8,128)(2,1)S(1)} collective-permute-done((bf16[512,512]{1,0:T(8,128)(2,1)S(1)}, bf16[512,512]{1,0:T(8,128)(2,1)S(1)}, u32[]{:S(2)}, u32[]{:S(2)}) %collective-permute-start.8) | collective-permute-done | bytes 524320 | tf_op jit(solution)/shard_map/ppermute | solution.py:115
  77.0 3.2 %shard_map.113.refs_1_.refs_0_ = bf16[512,2048]{1,0:T(8,128)(2,1)} custom-call(s32[5]{0:T(128)S(1)} %dynamic-slice_bitcast_fusion.ids_ref, bf16[512,512]{1,0:T(8,128)(2,1)S(1)} %fusion.1.refs_0_, bf16[512,512]{1,0:T(8,128)(2,1)S(1)} %copy-done.4, bf16[512,512]{1,0:T(8,128)(2,1)S(1)} %shard_map.112.refs_2_, bf16[512,512]{1,0:T(8,128)(2,1)} %copy-done.25, ...), custom_call_target="tpu_custom_call" | custom-call | tf_op jit(solution)/shard_map/pallas_call | solution.py:42
  80.2 7.7 %collective-permute-done.6.refs_3_ = bf16[528,512]{1,0:T(8,128)(2,1)S(1)} collective-permute-done((bf16[528,512]{1,0:T(8,128)(2,1)S(1)}, bf16[528,512]{1,0:T(8,128)(2,1)S(1)}, u32[]{:S(2)}, u32[]{:S(2)}) %collective-permute-start.6) | collective-permute-done | bytes 540704 | tf_op jit(solution)/shard_map/ppermute | solution.py:360
  87.9 10.2 %collective-permute-done.4.refs_1_ = bf16[528,512]{1,0:T(8,128)(2,1)S(1)} collective-permute-done((bf16[528,512]{1,0:T(8,128)(2,1)S(1)}, bf16[528,512]{1,0:T(8,128)(2,1)S(1)}, u32[]{:S(2)}, u32[]{:S(2)}) %collective-permute-start.4) | collective-permute-done | bytes 540704 | tf_op jit(solution)/shard_map/ppermute | solution.py:360
  99.0 3.7 %shard_map.115.refs_0_ = bf16[512,2048]{1,0:T(8,128)(2,1)} custom-call(s32[5]{0:T(128)S(1)} %dynamic-slice_bitcast_fusion.ids_ref, bf16[528,512]{1,0:T(8,128)(2,1)S(1)} %fusion.4.refs_1_.refs_0_, bf16[528,512]{1,0:T(8,128)(2,1)S(1)} %collective-permute-done.4.refs_1_, bf16[528,512]{1,0:T(8,128)(2,1)S(1)} %collective-permute-done.5.refs_2_, ...), custom_call_target="tpu_custom_call" | custom-call | tf_op jit(solution)/shard_map/pallas_call | solution.py:42
  103.1 7.3 %shard_map.116 = (bf16[512,1024]{1,0:T(8,128)(2,1)S(1)}, bf16[512,1024]{1,0:T(8,128)(2,1)}) custom-call(s32[5]{0:T(128)S(1)} %dynamic-slice_bitcast_fusion.ids_ref, bf16[512,2048]{1,0:T(8,128)(2,1)} %shard_map.115.refs_0_, bf16[2048,2048]{1,0:T(8,128)(2,1)} %all-gather.3.cloned.1.call-done.refs_1_), custom_call_target="tpu_custom_call" | custom-call | flops 4294967296 | bytes 12582912 | tf_op jit(solution)/shard_map/pallas_call | solution.py:42
  113.1 7.2 %shard_map.117 = (bf16[512,1024]{1,0:T(8,128)(2,1)S(1)}, bf16[512,1024]{1,0:T(8,128)(2,1)}) custom-call(s32[5]{0:T(128)S(1)} %dynamic-slice_bitcast_fusion.ids_ref, bf16[512,2048]{1,0:T(8,128)(2,1)} %collective-permute-done.9.refs_0_.refs_1_, bf16[2048,2048]{1,0:T(8,128)(2,1)} %all-gather.3.cloned.1.call-done.refs_1_, bf16[512,1024]{1,0:T(8,128)(2,1)} %copy-done.17), custom_call_target="tpu_custom_call" | custom-call | flops 4294967296 | bytes 12582912 | tf_op jit(solution)/shard_map/pallas_call | solution.py:42
  122.7 8.6 %shard_map.118.refs_5_ = bf16[2048,1024]{1,0:T(8,128)(2,1)} custom-call(s32[5]{0:T(128)S(1)} %dynamic-slice_bitcast_fusion.ids_ref, bf16[512,2048]{1,0:T(8,128)(2,1)} %shard_map.113.refs_1_.refs_0_, bf16[512,2048]{1,0:T(8,128)(2,1)} %copy-done.23, bf16[512,1024]{1,0:T(8,128)(2,1)S(1)} %copy-done.18, bf16[512,1024]{1,0:T(8,128)(2,1)} %copy-done.15), custom_call_target="tpu_custom_call" | custom-call | flops 4294967296 | bytes 12582912 | tf_op jit(solution)/shard_map/pallas_call | solution.py:42
  131.5 9.5 %shard_map.119 = (bf16[512,1024]{1,0:T(8,128)(2,1)S(1)}, bf16[512,1024]{1,0:T(8,128)(2,1)}) custom-call(s32[5]{0:T(128)S(1)} %dynamic-slice_bitcast_fusion.ids_ref, bf16[512,2048]{1,0:T(8,128)(2,1)} %shard_map.113.refs_1_.refs_0_, bf16[512,2048]{1,0:T(8,128)(2,1)} %copy-done.23, bf16[2048,2048]{1,0:T(8,128)(2,1)} %all-gather.5.cloned.1.call-done.refs_2_.refs_1_, ...), custom_call_target="tpu_custom_call" | custom-call | flops 4294967296 | bytes 12582912 | tf_op jit(solution)/shard_map/pallas_call | solution.py:42
  142.6 6.4 %shard_map.120.refs_4_ = bf16[512,2048]{1,0:T(8,128)(2,1)} custom-call(s32[5]{0:T(128)S(1)} %dynamic-slice_bitcast_fusion.ids_ref, bf16[512,1024]{1,0:T(8,128)(2,1)S(1)} %copy-done.12, bf16[2048,2048]{1,0:T(8,128)(2,1)} %all-gather.3.cloned.1.call-done.refs_1_), custom_call_target="tpu_custom_call" | custom-call | flops 4294967296 | bytes 12582912 | tf_op jit(solution)/shard_map/pallas_call | solution.py:42
  149.0 8.7 %shard_map.121.refs_2_ = bf16[2048,1024]{1,0:T(8,128)(2,1)} custom-call(s32[5]{0:T(128)S(1)} %dynamic-slice_bitcast_fusion.ids_ref, bf16[512,2048]{1,0:T(8,128)(2,1)} %shard_map.115.refs_0_, bf16[512,2048]{1,0:T(8,128)(2,1)} %collective-permute-done.9.refs_0_.refs_1_, bf16[512,1024]{1,0:T(8,128)(2,1)S(1)} %get-tuple-element.29.refs_2_.refs_0_, ...), custom_call_target="tpu_custom_call" | custom-call | flops 4294967296 | bytes 12582912 | tf_op jit(solution)/shard_map/pallas_call | solution.py:42
  159.7 6.4 %shard_map.122.refs_3_ = bf16[512,2048]{1,0:T(8,128)(2,1)} custom-call(s32[5]{0:T(128)S(1)} %dynamic-slice_bitcast_fusion.ids_ref, bf16[512,1024]{1,0:T(8,128)(2,1)S(1)} %copy-done.16, bf16[2048,2048]{1,0:T(8,128)(2,1)} %all-gather.5.cloned.1.call-done.refs_2_.refs_1_, bf16[2048,1024]{1,0:T(8,128)(2,1)} %shard_map.121.refs_2_), custom_call_target="tpu_custom_call" | custom-call | flops 4294967296 | bytes 12582912 | tf_op jit(solution)/shard_map/pallas_call | solution.py:42
  167.8 7.0 %shard_map.123 = (bf16[512,512]{1,0:T(8,128)(2,1)S(1)}, bf16[512,512]{1,0:T(8,128)(2,1)S(1)}, bf16[512,512]{1,0:T(8,128)(2,1)S(1)}, bf16[512,512]{1,0:T(8,128)(2,1)}) custom-call(s32[5]{0:T(128)S(1)} %dynamic-slice_bitcast_fusion.ids_ref, bf16[512,1024]{1,0:T(8,128)(2,1)} %copy-done.11, bf16[2048,2048]{1,0:T(8,128)(2,1)} %all-gather.3.cloned.1.call-done.refs_1_, ...), custom_call_target="tpu_custom_call" | custom-call | flops 4294967296 | bytes 12582912 | tf_op jit(solution)/shard_map/pallas_call | solution.py:42
  181.7 7.0 %shard_map.124 = (bf16[512,512]{1,0:T(8,128)(2,1)S(1)}, bf16[512,512]{1,0:T(8,128)(2,1)S(1)}, bf16[512,512]{1,0:T(8,128)(2,1)S(1)}, bf16[512,512]{1,0:T(8,128)(2,1)}) custom-call(s32[5]{0:T(128)S(1)} %dynamic-slice_bitcast_fusion.ids_ref, bf16[512,1024]{1,0:T(8,128)(2,1)} %copy-done.17, bf16[2048,2048]{1,0:T(8,128)(2,1)} %all-gather.5.cloned.1.call-done.refs_2_.refs_1_, ...), custom_call_target="tpu_custom_call" | custom-call | flops 4294967296 | bytes 12582912 | tf_op jit(solution)/shard_map/pallas_call | solution.py:42
  190.4 31.6 %collective-permute-done.14.refs_2_ = bf16[512,512]{1,0:T(8,128)(2,1)S(1)} collective-permute-done((bf16[512,512]{1,0:T(8,128)(2,1)S(1)}, bf16[512,512]{1,0:T(8,128)(2,1)S(1)}, u32[]{:S(2)}, u32[]{:S(2)}) %collective-permute-start.14) | collective-permute-done | bytes 524320 | tf_op jit(solution)/shard_map/ppermute | solution.py:360
  240.9 5.6 %collective-permute-start.20 = (bf16[512,512]{1,0:T(8,128)(2,1)S(1)}, bf16[512,512]{1,0:T(8,128)(2,1)}, u32[]{:S(2)}, u32[]{:S(2)}) collective-permute-start(bf16[512,512]{1,0:T(8,128)(2,1)S(1)} %shard_map.127), channel_id=1, source_target_pairs={{0,2},{1,3},{2,0},{3,1},{4,6},{5,7},{6,4},{7,5},{8,10},{9,11},{10,... | collective-permute-start | bytes 1572872 | tf_op jit(solution)/shard_map/ppermute | solution.py:360
  247.9 4.9 %shard_map.129.refs_1_ = bf16[2,4,64,512]{3,2,1,0:T(8,128)(2,1)} custom-call(s32[5]{0:T(128)S(1)} %dynamic-slice_bitcast_fusion.ids_ref, bf16[2,3,64,512]{3,2,1,0:T(8,128)(2,1)S(1)} %collective-permute-done.22.refs_0_, bf16[2,4,64,512]{3,2,1,0:T(8,128)(2,1)S(1)} %bitcast.30, bf16[2,3,64,512]{3,2,1,0:T(8,128)(2,1)S(1)} %collective-permute-done.23.refs_2_, ...), custom_call_target="tpu_custom_call" | custom-call | flops 4294967296 | bytes 12582912 | tf_op jit(solution)/shard_map/pallas_call | solution.py:42
  257.9 28.1 %collective-permute-done.20 = bf16[512,512]{1,0:T(8,128)(2,1)} collective-permute-done((bf16[512,512]{1,0:T(8,128)(2,1)S(1)}, bf16[512,512]{1,0:T(8,128)(2,1)}, u32[]{:S(2)}, u32[]{:S(2)}) %collective-permute-start.20) | collective-permute-done | bytes 524320 | tf_op jit(solution)/shard_map/ppermute | solution.py:360
  286.0 5.4 %collective-permute-done.21 = bf16[512,512]{1,0:T(8,128)(2,1)} collective-permute-done((bf16[512,512]{1,0:T(8,128)(2,1)S(1)}, bf16[512,512]{1,0:T(8,128)(2,1)}, u32[]{:S(2)}, u32[]{:S(2)}) %collective-permute-start.21) | collective-permute-done | bytes 524320 | tf_op jit(solution)/shard_map/ppermute | solution.py:360
  (161 shorter events, 70.1 us)
Async XLA Ops:
  7.2 95.9 %all-gather.3.cloned.1.call-start = ((), (), s32[]{:S(2)}) async-start(), calls=%async_computation.2 | async-start | bytes 9437184 | tf_op jit(solution)/shard_map/all_gather | solution.py:384
  8.0 123.5 %all-gather.5.cloned.1.call-start = ((), (), s32[]{:S(2)}) async-start(), calls=%async_computation.3 | async-start | bytes 9437184 | tf_op jit(solution)/shard_map/all_gather | solution.py:385
  8.7 244.1 %reduce-scatter.5.cloned.1.call-start = ((), (), s32[]{:S(2)}) async-start(), calls=%async_computation.5 | async-start | bytes 5242880 | tf_op jit(solution)/shard_map/reduce_scatter | solution.py:371
  8.9 31.1 %collective-permute-start.3 = (bf16[512,512]{1,0:T(8,128)(2,1)S(1)}, bf16[512,512]{1,0:T(8,128)(2,1)S(1)}, u32[]{:S(2)}, u32[]{:S(2)}) collective-permute-start(bf16[512,512]{1,0:T(8,128)(2,1)S(1)} %fusion.1.refs_0_), channel_id=1, source_target_pairs={{0,1},{1,2},{2,3},{4,5},{5,6},{6,7},{8,9},{9,10},{10,11},{12,13},{... | collective-permute-start | bytes 1572872 | tf_op jit(solution)/shard_map/ppermute | solution.py:107
  12.4 28.4 %collective-permute-start.2 = (bf16[512,512]{1,0:T(8,128)(2,1)S(1)}, bf16[512,512]{1,0:T(8,128)(2,1)S(1)}, u32[]{:S(2)}, u32[]{:S(2)}) collective-permute-start(bf16[512,512]{1,0:T(8,128)(2,1)S(1)} %fusion.1.refs_0_), channel_id=1, source_target_pairs={{1,0},{2,1},{3,2},{5,4},{6,5},{7,6},{9,8},{10,9},{11,10},{13,12},{... | collective-permute-start | bytes 1572872 | tf_op jit(solution)/shard_map/ppermute | solution.py:106
  15.8 18.7 %collective-permute-start.1 = (bf16[2,3,64,512]{3,2,1,0:T(8,128)(2,1)}, bf16[2,3,64,512]{3,2,1,0:T(8,128)(2,1)S(1)}, u32[]{:S(2)}, u32[]{:S(2)}) collective-permute-start(bf16[2,3,64,512]{3,2,1,0:T(8,128)(2,1)} %get-tuple-element.54), channel_id=1, source_target_pairs={{4,0},{8,4},{12,8},{16,12},{20,16},{24,20},{28,24},{5,1},{9,5},{13... | collective-permute-start | bytes 1179656 | tf_op jit(solution)/shard_map/ppermute | solution.py:344
  18.0 21.3 %collective-permute-start = (bf16[2,3,64,512]{3,2,1,0:T(8,128)(2,1)}, bf16[2,3,64,512]{3,2,1,0:T(8,128)(2,1)S(1)}, u32[]{:S(2)}, u32[]{:S(2)}) collective-permute-start(bf16[2,3,64,512]{3,2,1,0:T(8,128)(2,1)} %get-tuple-element.55), channel_id=1, source_target_pairs={{0,4},{4,8},{8,12},{12,16},{16,20},{20,24},{24,28},{1,5},{5,9},{9,... | collective-permute-start | bytes 1179656 | tf_op jit(solution)/shard_map/ppermute | solution.py:343
  20.1 29.5 %collective-permute-start.7 = (bf16[512,512]{1,0:T(8,128)(2,1)S(1)}, bf16[512,512]{1,0:T(8,128)(2,1)S(1)}, u32[]{:S(2)}, u32[]{:S(2)}) collective-permute-start(bf16[512,512]{1,0:T(8,128)(2,1)S(1)} %fusion.1.refs_0_), channel_id=1, source_target_pairs={{0,2},{1,3},{2,0},{3,1},{4,6},{5,7},{6,4},{7,5},{8,10},{9,11},{10,... | collective-permute-start | bytes 1572872 | tf_op jit(solution)/shard_map/ppermute | solution.py:105
  49.5 38.4 %collective-permute-start.6 = (bf16[528,512]{1,0:T(8,128)(2,1)S(1)}, bf16[528,512]{1,0:T(8,128)(2,1)S(1)}, u32[]{:S(2)}, u32[]{:S(2)}) collective-permute-start(bf16[528,512]{1,0:T(8,128)(2,1)S(1)} %fusion.4.refs_1_.refs_0_), channel_id=1, source_target_pairs={{0,3},{1,0},{2,1},{3,2},{4,7},{5,4},{6,5},{7,6},{8,11},{9,8},{10,9... | collective-permute-start | bytes 1622024 | tf_op jit(solution)/shard_map/ppermute | solution.py:360
  50.1 26.1 %collective-permute-start.8 = (bf16[512,512]{1,0:T(8,128)(2,1)S(1)}, bf16[512,512]{1,0:T(8,128)(2,1)S(1)}, u32[]{:S(2)}, u32[]{:S(2)}) collective-permute-start(bf16[512,512]{1,0:T(8,128)(2,1)S(1)} %shard_map.112.refs_2_), channel_id=1, source_target_pairs={{1,0},{2,3},{5,4},{6,7},{9,8},{10,11},{13,12},{14,15},{17,16},{18,... | collective-permute-start | bytes 1572872 | tf_op jit(solution)/shard_map/ppermute | solution.py:115
  56.2 31.7 %collective-permute-start.5 = (bf16[528,512]{1,0:T(8,128)(2,1)S(1)}, bf16[528,512]{1,0:T(8,128)(2,1)S(1)}, u32[]{:S(2)}, u32[]{:S(2)}) collective-permute-start(bf16[528,512]{1,0:T(8,128)(2,1)S(1)} %fusion.4.refs_1_.refs_0_), channel_id=1, source_target_pairs={{0,2},{1,3},{2,0},{3,1},{4,6},{5,7},{6,4},{7,5},{8,10},{9,11},{10,... | collective-permute-start | bytes 1622024 | tf_op jit(solution)/shard_map/ppermute | solution.py:360
  56.3 41.8 %collective-permute-start.4 = (bf16[528,512]{1,0:T(8,128)(2,1)S(1)}, bf16[528,512]{1,0:T(8,128)(2,1)S(1)}, u32[]{:S(2)}, u32[]{:S(2)}) collective-permute-start(bf16[528,512]{1,0:T(8,128)(2,1)S(1)} %fusion.4.refs_1_.refs_0_), channel_id=1, source_target_pairs={{0,1},{1,2},{2,3},{3,0},{4,5},{5,6},{6,7},{7,4},{8,9},{9,10},{10,1... | collective-permute-start | bytes 1622024 | tf_op jit(solution)/shard_map/ppermute | solution.py:360
  102.6 18.7 %collective-permute-start.10 = (bf16[512,2048]{1,0:T(8,128)(2,1)}, bf16[512,2048]{1,0:T(8,128)(2,1)S(1)}, u32[]{:S(2)}, u32[]{:S(2)}) collective-permute-start(bf16[512,2048]{1,0:T(8,128)(2,1)} %shard_map.113.refs_1_.refs_0_), channel_id=1, source_target_pairs={{0,4},{4,0},{8,12},{12,8},{16,20},{20,16},{24,28},{28,24},{1,5},{5... | collective-permute-start | bytes 6291464 | tf_op jit(solution)/shard_map/ppermute | solution.py:382
  131.4 123.3 %reduce-scatter.3.cloned.1.call-start = ((), (), s32[]{:S(2)}) async-start(), calls=%async_computation.4 | async-start | bytes 5242880 | tf_op jit(solution)/shard_map/reduce_scatter | solution.py:371
  166.1 14.3 %collective-permute-start.11 = (bf16[512,2048]{1,0:T(8,128)(2,1)}, bf16[512,2048]{1,0:T(8,128)(2,1)S(1)}, u32[]{:S(2)}, u32[]{:S(2)}) collective-permute-start(bf16[512,2048]{1,0:T(8,128)(2,1)} %shard_map.122.refs_3_), channel_id=1, source_target_pairs={{0,4},{4,0},{8,12},{12,8},{16,20},{20,16},{24,28},{28,24},{1,5},{5... | collective-permute-start | bytes 6291464 | tf_op jit(solution)/shard_map/ppermute | solution.py:382
  175.6 14.8 %collective-permute-start.13 = (bf16[512,512]{1,0:T(8,128)(2,1)S(1)}, bf16[512,512]{1,0:T(8,128)(2,1)S(1)}, u32[]{:S(2)}, u32[]{:S(2)}) collective-permute-start(bf16[512,512]{1,0:T(8,128)(2,1)S(1)} %get-tuple-element.34), channel_id=1, source_target_pairs={{0,1},{1,2},{2,3},{3,0},{4,5},{5,6},{6,7},{7,4},{8,9},{9,10},{10,1... | collective-permute-start | bytes 1572872 | tf_op jit(solution)/shard_map/ppermute | solution.py:360
  176.8 45.3 %collective-permute-start.14 = (bf16[512,512]{1,0:T(8,128)(2,1)S(1)}, bf16[512,512]{1,0:T(8,128)(2,1)S(1)}, u32[]{:S(2)}, u32[]{:S(2)}) collective-permute-start(bf16[512,512]{1,0:T(8,128)(2,1)S(1)} %get-tuple-element.35), channel_id=1, source_target_pairs={{0,2},{1,3},{2,0},{3,1},{4,6},{5,7},{6,4},{7,5},{8,10},{9,11},{10,... | collective-permute-start | bytes 1572872 | tf_op jit(solution)/shard_map/ppermute | solution.py:360
  178.4 46.0 %collective-permute-start.15 = (bf16[512,512]{1,0:T(8,128)(2,1)}, bf16[512,512]{1,0:T(8,128)(2,1)S(1)}, u32[]{:S(2)}, u32[]{:S(2)}) collective-permute-start(bf16[512,512]{1,0:T(8,128)(2,1)} %get-tuple-element.36), channel_id=1, source_target_pairs={{0,3},{1,0},{2,1},{3,2},{4,7},{5,4},{6,5},{7,6},{8,11},{9,8},{10,9... | collective-permute-start | bytes 1572872 | tf_op jit(solution)/shard_map/ppermute | solution.py:360
  234.2 12.3 %collective-permute-start.23 = (bf16[2,3,64,512]{3,2,1,0:T(8,128)(2,1)S(1)}, bf16[2,3,64,512]{3,2,1,0:T(8,128)(2,1)S(1)}, u32[]{:S(2)}, u32[]{:S(2)}) collective-permute-start(bf16[2,3,64,512]{3,2,1,0:T(8,128)(2,1)S(1)} %get-tuple-element.52), channel_id=1, source_target_pairs={{4,0},{8,4},{12,8},{16,12},{20,16},{24,20},{28,24},{5,1},{9,5},{13... | collective-permute-start | bytes 1179656 | tf_op jit(solution)/shard_map/ppermute | solution.py:344
  240.4 17.6 %collective-permute-start.19 = (bf16[512,512]{1,0:T(8,128)(2,1)S(1)}, bf16[512,512]{1,0:T(8,128)(2,1)}, u32[]{:S(2)}, u32[]{:S(2)}) collective-permute-start(bf16[512,512]{1,0:T(8,128)(2,1)S(1)} %shard_map.126), channel_id=1, source_target_pairs={{0,1},{1,2},{2,3},{3,0},{4,5},{5,6},{6,7},{7,4},{8,9},{9,10},{10,1... | collective-permute-start | bytes 1572872 | tf_op jit(solution)/shard_map/ppermute | solution.py:360
  240.9 45.1 %collective-permute-start.20 = (bf16[512,512]{1,0:T(8,128)(2,1)S(1)}, bf16[512,512]{1,0:T(8,128)(2,1)}, u32[]{:S(2)}, u32[]{:S(2)}) collective-permute-start(bf16[512,512]{1,0:T(8,128)(2,1)S(1)} %shard_map.127), channel_id=1, source_target_pairs={{0,2},{1,3},{2,0},{3,1},{4,6},{5,7},{6,4},{7,5},{8,10},{9,11},{10,... | collective-permute-start | bytes 1572872 | tf_op jit(solution)/shard_map/ppermute | solution.py:360
  246.6 44.8 %collective-permute-start.21 = (bf16[512,512]{1,0:T(8,128)(2,1)S(1)}, bf16[512,512]{1,0:T(8,128)(2,1)}, u32[]{:S(2)}, u32[]{:S(2)}) collective-permute-start(bf16[512,512]{1,0:T(8,128)(2,1)S(1)} %shard_map.128), channel_id=1, source_target_pairs={{0,3},{1,0},{2,1},{3,2},{4,7},{5,4},{6,5},{7,6},{8,11},{9,8},{10,9... | collective-permute-start | bytes 1572872 | tf_op jit(solution)/shard_map/ppermute | solution.py:360
  254.6 39.3 %collective-permute-start.25 = (bf16[256,1024]{1,0:T(8,128)(2,1)S(1)}, bf16[256,1024]{1,0:T(8,128)(2,1)S(1)}, u32[]{:S(2)}, u32[]{:S(2)}) collective-permute-start(bf16[256,1024]{1,0:T(8,128)(2,1)S(1)} %shard_map.132), channel_id=1, source_target_pairs={{0,4},{4,0},{8,12},{12,8},{16,20},{20,16},{24,28},{28,24},{1,5},{5... | collective-permute-start | bytes 1572872 | tf_op jit(solution)/shard_map/ppermute | solution.py:267
  257.4 38.2 %collective-permute-start.24 = (bf16[256,1024]{1,0:T(8,128)(2,1)S(1)}, bf16[256,1024]{1,0:T(8,128)(2,1)S(1)}, u32[]{:S(2)}, u32[]{:S(2)}) collective-permute-start(bf16[256,1024]{1,0:T(8,128)(2,1)S(1)} %shard_map.130), channel_id=1, source_target_pairs={{0,4},{4,0},{8,12},{12,8},{16,20},{20,16},{24,28},{28,24},{1,5},{5... | collective-permute-start | bytes 1572872 | tf_op jit(solution)/shard_map/ppermute | solution.py:267
  (39 other events, 324.7 us)
Sparse Core Ops, SparseCore 0:
  9.9 62.8 all-gather.2
  74.7 54.3 all-gather.4
  132.1 52.9 reduce-scatter.4
  188.2 53.3 reduce-scatter.2

commit v4 on v3

--- a/solution.py
+++ b/solution.py
@@ -15,6 +15,7 @@
 BF16 = jnp.bfloat16
 LAST = (((1,), (1,)), ((), ()))
 FIRST = (((0,), (0,)), ((), ()))
+CHIPS = (0, 1, 3, 2)
 SIBLING = [(i, i ^ 1) for i in range(8)]
 UP = [(0, 1), (1, 2), (2, 3)]
 DOWN = [(1, 0), (2, 1), (3, 2)]
@@ -25,6 +26,19 @@
 PARAMS = pltpu.CompilerParams(vmem_limit_bytes=52 * 2**20)
 HINT = pl.CostEstimate(flops=0, bytes_accessed=0, transcendentals=0)
 WORK = pl.CostEstimate(flops=2**32, bytes_accessed=12 * 2**20, transcendentals=0)
+
+
+def ring_pairs(sense):
+    pairs = []
+    for place, chip in enumerate(CHIPS):
+        for core in (0, 1):
+            step = sense if core == 0 else -sense
+            pairs.append((2 * chip + core, 2 * CHIPS[(place + step) % 4] + core))
+    return pairs
+
+
+AHEAD = ring_pairs(1)
+BEHIND = ring_pairs(-1)
 
 
 def shape(dims, dtype=BF16):
@@ -67,12 +81,14 @@
 
 
 def make_ids():
-    table = np.zeros((8, 4, 5), np.int32)
+    table = np.zeros((8, 4, 9), np.int32)
     for row in range(8):
+        place, sense = CHIPS.index(row // 2), 1 - 2 * (row % 2)
+        ring = [CHIPS[(place + sense * step) % 4] for step in (0, -1, 1, 2)]
         for z in range(4):
-            table[row, z] = [z, (z + 1) % 4, (z + 2) % 4, (z + 3) % 4, row % 2]
+            table[row, z] = [z, (z + 1) % 4, (z + 2) % 4, (z + 3) % 4, row % 2] + ring
     place = (lax.axis_index("row"), lax.axis_index("col"), 0)
-    return lax.dynamic_slice(jnp.asarray(table), place, (1, 1, 5)).reshape(5)
+    return lax.dynamic_slice(jnp.asarray(table), place, (1, 1, 9)).reshape(9)
 
 
 def move(body, ids, arrays, shapes, count, after=()):
@@ -196,20 +212,31 @@
     )
 
 
-def weight_grad(ids, own, sib, right, after=()):
+def weight_grad(ids, own, sib, right, slots, after=()):
     rows = own.shape[0]
     hid = right[0].shape[1]
     size = C // 4
 
-    def kernel(ids_ref, own_ref, sib_ref, own_right, sib_right, out_ref):
+    def kernel(ids_ref, own_ref, sib_ref, own_right, sib_right, *outs):
         acc = lax.dot_general(own_ref[...], own_right[...], FIRST, preferred_element_type=F32)
         acc += lax.dot_general(sib_ref[...], sib_right[...], FIRST, preferred_element_type=F32)
-        out_ref[...] = acc.astype(BF16)
-
-    cut = pl.BlockSpec((rows, size), lambda t, i: (0, t))
-    return call(
-        kernel, ids, [own, sib, *right], (4,), [cut, cut] + [whole((rows, hid))] * 2,
-        pl.BlockSpec((size, hid), lambda t, i: (t, 0)), shape((C, hid)), after=after,
+        if not slots:
+            outs[0][...] = acc.astype(BF16)
+            return
+        for k in range(4):
+            @pl.when(pl.program_id(0) == k)
+            def _():
+                outs[k][...] = acc.astype(BF16)
+
+    if slots:
+        cut = pl.BlockSpec((rows, size), lambda t, i: (0, i[8 - t]))
+        outs, shapes = [whole((size, hid))] * 4, [shape((size, hid))] * 4
+    else:
+        cut = pl.BlockSpec((rows, size), lambda t, i: (0, t))
+        outs, shapes = pl.BlockSpec((size, hid), lambda t, i: (t, 0)), shape((C, hid))
+    return call(
+        kernel, ids, [own, sib, *right], (4,), [cut, cut] + [whole((rows, hid))] * 2, outs, shapes,
+        after=after,
     )
 
 
@@ -251,6 +278,16 @@
         ],
         [whole((rows, 512))] * 4, [shape((rows, 512))] * 4, after=after,
     )
+
+
+def ring_send(blocks):
+    return lax.ppermute(blocks[0], "row", BEHIND), lax.ppermute(blocks[1], "row", AHEAD)
+
+
+def ring_scatter(blocks, sent):
+    _, _, behind, own = blocks
+    one = lax.ppermute((sent[0].astype(F32) + behind.astype(F32)).astype(BF16), "row", BEHIND)
+    return (own.astype(F32) + one.astype(F32) + sent[1].astype(F32)).astype(BF16)
 
 
 def give_rows(ids, block, after):
@@ -415,36 +452,41 @@
     hidden_own, slope_own = expand(ids, in_own, in_panel)
     hidden_sib, slope_sib = expand(ids, in_sib, in_panel, [hidden_own])
     hidden = hidden_own, hidden_sib
-    out_part = weight_grad(ids, grad_own, grad_sib, hidden)
+    out_part = weight_grad(ids, grad_own, grad_sib, hidden, False)
     out_rows = row_scatter(out_part)
     grad_pre = expand_grad(
         ids, (grad_own, grad_sib), out_panel, (slope_own, slope_sib), [out_part]
     )
     back_give = contract(ids, grad_pre[1], in_panel)
     back_sib = swap(back_give)
-    in_part = weight_grad(ids, in_own, in_sib, grad_pre, [back_give])
-    in_rows = row_scatter(in_part)
-    branch_give = contract(ids, hidden_sib, out_panel, None, [in_part])
+    branch_give = contract(ids, hidden_sib, out_panel, None, [back_give])
     branch_sib = swap(branch_give)
     back = contract_own(ids, grad_pre[0], in_panel, back_sib, [branch_give])
     back_sent = [shifted(back[step], step) for step in (1, 2, 3)]
-    branch = contract_own(ids, hidden_own, out_panel, branch_sib, [back[0]])
-    back_sent[0] = later(ids, back_sent[0], [branch[0], *back_sent[1:]])
+    contrib = contract(ids, hidden_own, out_panel, branch_sib, [back[0]])
+    in_parts = weight_grad(ids, in_own, in_sib, grad_pre, True, [contrib])
+    in_sent = ring_send(in_parts)
+    back_sent[0] = later(ids, back_sent[0], [in_parts[0], *back_sent[1:]])
+    contrib = later(ids, contrib, [back_sent[0]])
+    branch = lax.psum_scatter(contrib, "col", scatter_dimension=1, tiled=True)
+    in_rows = ring_scatter(in_parts, in_sent)
+    seen = back_sent[0][:8, :128] + back_sent[0][8:16, :128]
+    back_sent[0] = later(ids, back_sent[0], [seen, *in_sent])
     grad_scaled = added([back[0], *back_sent])
     weighted = grad_scaled * norm_gain
     sums = jnp.stack([jnp.sum(weighted, axis=1), jnp.sum(weighted * normed, axis=1)])
     sums = sums + shifted(sums, 1) + shifted(sums, 2) + shifted(sums, 3)
-    branch_sent = [shifted(later(ids, branch[step], [sums]), step) for step in (1, 2, 3)]
-    branch = added([branch[0], *branch_sent])
-    residual_in = images.reshape(pixels, local_ch).astype(F32)
-    block_out = (residual_in + layer_scale * branch).astype(BF16).reshape(images.shape)
     grad_conv = inv_std[:, None] * (
         weighted - sums[0][:, None] / C - normed * sums[1][:, None] / C
     )
     grad_conv = grad_conv.astype(BF16).reshape(images.shape)
     low, high = rims(grad_conv)
     grad_images = taps(ids, low, grad_conv, high, dw_kernel, True, cotangent)
-    return block_out, grad_images, own_rows(ids, in_rows, [grad_images]), own_rows(ids, out_rows)
+    grad_in, grad_out = own_rows(ids, in_rows, [grad_images]), own_rows(ids, out_rows)
+    branch = later(ids, branch, [grad_in, grad_out])
+    residual_in = images.reshape(pixels, local_ch).astype(F32)
+    block_out = (residual_in + layer_scale * branch.astype(F32)).astype(BF16).reshape(images.shape)
+    return block_out, grad_images, grad_in, grad_out
 
 
 def with_halo(block, sides, width):
@@ -507,7 +549,7 @@
         contrib.astype(jnp.bfloat16), "col", scatter_dimension=1, tiled=True
     ).astype(jnp.float32)
     residual_in = images.reshape(pixels, local_ch).astype(jnp.float32)
-    block_out = (residual_in + layer_scale * branch).astype(jnp.bfloat16).reshape(images.shape)
+    block_out = (residual_in + layer_scale * branch.astype(F32)).astype(jnp.bfloat16).reshape(images.shape)
     cot_flat = cotangent.reshape(pixels, local_ch).astype(jnp.float32)
     grad_branch = (cot_flat * layer_scale).astype(jnp.bfloat16)
     full_grad = lax.all_gather(grad_branch, "col", axis=1, tiled=True)

time: 305 us -> 272 us (0.89)
  the two profiles are of different devices: /device:TPU:12 before, /device:TPU:0 now
where the time goes in v4:
time: 272 us; the launch traced here: 271 us
  Pallas kernels  96.3 us (35%)
  waiting for transfers between devices  75.8 us (28%)
  starting transfers between devices  60.9 us (22%)
  local copies, waits for them, and re-layouts  17.5 us (6%)
  between operations  14.3 us (5%)
  other arithmetic  5.93 us (2%)
    pallas_call x23, Pallas kernels, call(): pl.pallas_call(kernel, grid_spec=pltpu.PrefetchScalarGridSpec(num_scalar_...  96.3 us
    ppermute x9, waiting for transfers between devices, shifted(): lax.ppermute(array, 'col', [(i, (i + step) % count) for i in range(count)])  37.8 us
    ppermute x9, starting transfers between devices, shifted(): lax.ppermute(array, 'col', [(i, (i + step) % count) for i in range(count)])  23.5 us
    unnamed x62, local copies, waits for them, and re-layouts  15.4 us
    ppermute x1, waiting for transfers between devices, col_send(): across = lax.ppermute(block, 'col', ACROSS)  13.3 us
    ppermute x2, starting transfers between devices, own_rows(): other = lax.ppermute(give_rows(ids, block, after), 'row', SIBLING)  12.3 us
    ppermute x1, waiting for transfers between devices, ring_send(): lax.ppermute(blocks[1], 'row', AHEAD)  9.79 us
    ppermute x1, waiting for transfers between devices, col_gather(): far = lax.ppermute(across, 'col', [(1, 0), (2, 3)])  8.82 us
  transfers between devices with their start and end apart: 30, of which 9 were waited for; matrix products, arithmetic and copies ran while one was open for 3% of the time, Pallas kernels for 35%

profile of v4, /device:TPU:0, one launch (start us, length us, event | category | flops | bytes accessed | tf_op | source)
XLA Modules:
  0.0 270.7 jit_solution(15721684733101976025)
XLA Ops:
  8.9 5.0 %collective-permute-start.3 = (bf16[512,512]{1,0:T(8,128)(2,1)S(1)}, bf16[512,512]{1,0:T(8,128)(2,1)S(1)}, u32[]{:S(2)}, u32[]{:S(2)}) collective-permute-start(bf16[512,512]{1,0:T(8,128)(2,1)S(1)} %fusion.1.refs_0_), channel_id=1, source_target_pairs={{0,1},{1,2},{2,3},{4,5},{5,6},{6,7},{8,9},{9,10},{10,11},{12,13},{... | collective-permute-start | bytes 1572872 | tf_op jit(solution)/shard_map/ppermute | solution.py:123
  20.5 3.7 %collective-permute-start.7 = (bf16[512,512]{1,0:T(8,128)(2,1)S(1)}, bf16[512,512]{1,0:T(8,128)(2,1)S(1)}, u32[]{:S(2)}, u32[]{:S(2)}) collective-permute-start(bf16[512,512]{1,0:T(8,128)(2,1)S(1)} %fusion.1.refs_0_), channel_id=1, source_target_pairs={{0,2},{1,3},{2,0},{3,1},{4,6},{5,7},{6,4},{7,5},{8,10},{9,11},{10,... | collective-permute-start | bytes 1572872 | tf_op jit(solution)/shard_map/ppermute | solution.py:121
  31.4 6.3 %shard_map.111 = (f32[2,4,64,512]{3,2,1,0:T(8,128)}, bf16[2,4,64,512]{3,2,1,0:T(8,128)(2,1)S(1)}, f32[2,4,64,1]{3,2,1,0:T(8,128)S(1)}, f32[2,4,64,1]{3,2,1,0:T(8,128)S(1)}) custom-call(s32[9]{0:T(128)S(1)} %dynamic-slice_bitcast_fusion.ids_ref, bf16[2,3,64,512]{3,2,1,0:T(8,128)(2,1)S(1)} %copy-done.12, bf16[2,4,64,512]{3,2,1,0:T(8,128)(2,1)} %refs_1_.1, ...), custom_call_target="tpu_custom_call" | custom-call | flops 4294967296 | bytes 12582912 | tf_op jit(solution)/shard_map/pallas_call | solution.py:56
  40.8 13.3 %collective-permute-done.7.refs_0_ = bf16[512,512]{1,0:T(8,128)(2,1)S(1)} collective-permute-done((bf16[512,512]{1,0:T(8,128)(2,1)S(1)}, bf16[512,512]{1,0:T(8,128)(2,1)S(1)}, u32[]{:S(2)}, u32[]{:S(2)}) %collective-permute-start.7) | collective-permute-done | bytes 524320 | tf_op jit(solution)/shard_map/ppermute | solution.py:121
  56.0 10.7 %collective-permute-start.5 = (bf16[528,512]{1,0:T(8,128)(2,1)S(1)}, bf16[528,512]{1,0:T(8,128)(2,1)S(1)}, u32[]{:S(2)}, u32[]{:S(2)}) collective-permute-start(bf16[528,512]{1,0:T(8,128)(2,1)S(1)} %fusion.4.refs_1_.refs_0_), channel_id=1, source_target_pairs={{0,2},{1,3},{2,0},{3,1},{4,6},{5,7},{6,4},{7,5},{8,10},{9,11},{10,... | collective-permute-start | bytes 1622024 | tf_op jit(solution)/shard_map/ppermute | solution.py:397
  66.7 8.8 %collective-permute-done.8.refs_4_ = bf16[512,512]{1,0:T(8,128)(2,1)S(1)} collective-permute-done((bf16[512,512]{1,0:T(8,128)(2,1)S(1)}, bf16[512,512]{1,0:T(8,128)(2,1)S(1)}, u32[]{:S(2)}, u32[]{:S(2)}) %collective-permute-start.8) | collective-permute-done | bytes 524320 | tf_op jit(solution)/shard_map/ppermute | solution.py:131
  76.3 3.2 %shard_map.113.refs_1_.refs_0_ = bf16[512,2048]{1,0:T(8,128)(2,1)} custom-call(s32[9]{0:T(128)S(1)} %dynamic-slice_bitcast_fusion.ids_ref, bf16[512,512]{1,0:T(8,128)(2,1)S(1)} %fusion.1.refs_0_, bf16[512,512]{1,0:T(8,128)(2,1)S(1)} %copy-done.5, bf16[512,512]{1,0:T(8,128)(2,1)S(1)} %shard_map.112.refs_2_, bf16[512,512]{1,0:T(8,128)(2,1)} %copy-done.23, ...), custom_call_target="tpu_custom_call" | custom-call | tf_op jit(solution)/shard_map/pallas_call | solution.py:56
  79.6 21.7 %collective-permute-done.5.refs_2_ = bf16[528,512]{1,0:T(8,128)(2,1)S(1)} collective-permute-done((bf16[528,512]{1,0:T(8,128)(2,1)S(1)}, bf16[528,512]{1,0:T(8,128)(2,1)S(1)}, u32[]{:S(2)}, u32[]{:S(2)}) %collective-permute-start.5) | collective-permute-done | bytes 540704 | tf_op jit(solution)/shard_map/ppermute | solution.py:397
  102.1 3.7 %shard_map.115.refs_0_ = bf16[512,2048]{1,0:T(8,128)(2,1)} custom-call(s32[9]{0:T(128)S(1)} %dynamic-slice_bitcast_fusion.ids_ref, bf16[528,512]{1,0:T(8,128)(2,1)S(1)} %fusion.4.refs_1_.refs_0_, bf16[528,512]{1,0:T(8,128)(2,1)S(1)} %collective-permute-done.4.refs_1_, bf16[528,512]{1,0:T(8,128)(2,1)S(1)} %collective-permute-done.5.refs_2_, ...), custom_call_target="tpu_custom_call" | custom-call | tf_op jit(solution)/shard_map/pallas_call | solution.py:56
  106.3 7.2 %shard_map.116 = (bf16[512,1024]{1,0:T(8,128)(2,1)S(1)}, bf16[512,1024]{1,0:T(8,128)(2,1)}) custom-call(s32[9]{0:T(128)S(1)} %dynamic-slice_bitcast_fusion.ids_ref, bf16[512,2048]{1,0:T(8,128)(2,1)} %shard_map.115.refs_0_, bf16[2048,2048]{1,0:T(8,128)(2,1)} %all-gather.3.cloned.1.call-done.refs_1_), custom_call_target="tpu_custom_call" | custom-call | flops 4294967296 | bytes 12582912 | tf_op jit(solution)/shard_map/pallas_call | solution.py:56
  115.9 7.2 %shard_map.117 = (bf16[512,1024]{1,0:T(8,128)(2,1)S(1)}, bf16[512,1024]{1,0:T(8,128)(2,1)}) custom-call(s32[9]{0:T(128)S(1)} %dynamic-slice_bitcast_fusion.ids_ref, bf16[512,2048]{1,0:T(8,128)(2,1)} %copy-done.28, bf16[2048,2048]{1,0:T(8,128)(2,1)} %all-gather.3.cloned.1.call-done.refs_1_, bf16[512,1024]{1,0:T(8,128)(2,1)} %copy-done.13), custom_call_target="tpu_custom_call" | custom-call | flops 4294967296 | bytes 12582912 | tf_op jit(solution)/shard_map/pallas_call | solution.py:56
  124.1 8.7 %shard_map.118.refs_5_ = bf16[2048,1024]{1,0:T(8,128)(2,1)} custom-call(s32[9]{0:T(128)S(1)} %dynamic-slice_bitcast_fusion.ids_ref, bf16[512,2048]{1,0:T(8,128)(2,1)} %shard_map.113.refs_1_.refs_0_, bf16[512,2048]{1,0:T(8,128)(2,1)} %collective-permute-done.10.refs_1_, bf16[512,1024]{1,0:T(8,128)(2,1)S(1)} %copy-done.14, bf16[512,1024]{1,0:T(8,128)(2,1)} %copy-done.15), custom_call_target="tpu_custom_call" | custom-call | flops 4294967296 | bytes 12582912 | tf_op jit(solution)/shard_map/pallas_call | solution.py:56
  132.9 9.5 %shard_map.119 = (bf16[512,1024]{1,0:T(8,128)(2,1)S(1)}, bf16[512,1024]{1,0:T(8,128)(2,1)}) custom-call(s32[9]{0:T(128)S(1)} %dynamic-slice_bitcast_fusion.ids_ref, bf16[512,2048]{1,0:T(8,128)(2,1)} %shard_map.113.refs_1_.refs_0_, bf16[512,2048]{1,0:T(8,128)(2,1)} %collective-permute-done.10.refs_1_, ...), custom_call_target="tpu_custom_call" | custom-call | flops 4294967296 | bytes 12582912 | tf_op jit(solution)/shard_map/pallas_call | solution.py:56
  144.6 6.4 %shard_map.120.refs_2_ = bf16[512,2048]{1,0:T(8,128)(2,1)} custom-call(s32[9]{0:T(128)S(1)} %dynamic-slice_bitcast_fusion.ids_ref, bf16[512,1024]{1,0:T(8,128)(2,1)S(1)} %copy-done.10, bf16[2048,2048]{1,0:T(8,128)(2,1)} %all-gather.3.cloned.1.call-done.refs_1_), custom_call_target="tpu_custom_call" | custom-call | flops 4294967296 | bytes 12582912 | tf_op jit(solution)/shard_map/pallas_call | solution.py:56
  151.1 6.5 %shard_map.121.refs_3_ = bf16[512,2048]{1,0:T(8,128)(2,1)} custom-call(s32[9]{0:T(128)S(1)} %dynamic-slice_bitcast_fusion.ids_ref, bf16[512,1024]{1,0:T(8,128)(2,1)S(1)} %copy-done.16, bf16[2048,2048]{1,0:T(8,128)(2,1)} %all-gather.5.cloned.1.call-done.refs_2_.refs_1_, bf16[512,2048]{1,0:T(8,128)(2,1)} %shard_map.120.refs_2_), custom_call_target="tpu_custom_call" | custom-call | flops 4294967296 | bytes 12582912 | tf_op jit(solution)/shard_map/pallas_call | solution.py:56
  159.5 7.1 %shard_map.122 = (bf16[512,512]{1,0:T(8,128)(2,1)S(1)}, bf16[512,512]{1,0:T(8,128)(2,1)S(1)}, bf16[512,512]{1,0:T(8,128)(2,1)S(1)}, bf16[512,512]{1,0:T(8,128)(2,1)}) custom-call(s32[9]{0:T(128)S(1)} %dynamic-slice_bitcast_fusion.ids_ref, bf16[512,1024]{1,0:T(8,128)(2,1)} %copy-done.9, bf16[2048,2048]{1,0:T(8,128)(2,1)} %all-gather.3.cloned.1.call-done.refs_1_, ...), custom_call_target="tpu_custom_call" | custom-call | flops 4294967296 | bytes 12582912 | tf_op jit(solution)/shard_map/pallas_call | solution.py:56
  173.2 6.7 %shard_map.123.refs_4_.refs_0_ = bf16[512,2048]{1,0:T(8,128)(2,1)} custom-call(s32[9]{0:T(128)S(1)} %dynamic-slice_bitcast_fusion.ids_ref, bf16[512,1024]{1,0:T(8,128)(2,1)S(1)} %copy-done.14, bf16[2048,2048]{1,0:T(8,128)(2,1)} %all-gather.5.cloned.1.call-done.refs_2_.refs_1_, bf16[512,2048]{1,0:T(8,128)(2,1)} %copy-done.29, ...), custom_call_target="tpu_custom_call" | custom-call | flops 4294967296 | bytes 12582912 | tf_op jit(solution)/shard_map/pallas_call | solution.py:56
  179.9 10.2 %shard_map.124 = (bf16[512,1024]{1,0:T(8,128)(2,1)}, bf16[512,1024]{1,0:T(8,128)(2,1)}, bf16[512,1024]{1,0:T(8,128)(2,1)}, bf16[512,1024]{1,0:T(8,128)(2,1)}) custom-call(s32[9]{0:T(128)S(1)} %dynamic-slice_bitcast_fusion.ids_ref, bf16[512,2048]{1,0:T(8,128)(2,1)} %shard_map.115.refs_0_, bf16[512,2048]{1,0:T(8,128)(2,1)} %copy-done.28, ...), custom_call_target="tpu_custom_call" | custom-call | flops 4294967296 | bytes 12582912 | tf_op jit(solution)/shard_map/pallas_call | solution.py:56
  192.2 12.8 %collective-permute-done.14.refs_2_ = bf16[512,512]{1,0:T(8,128)(2,1)S(1)} collective-permute-done((bf16[512,512]{1,0:T(8,128)(2,1)S(1)}, bf16[512,512]{1,0:T(8,128)(2,1)S(1)}, u32[]{:S(2)}, u32[]{:S(2)}) %collective-permute-start.14) | collective-permute-done | bytes 524320 | tf_op jit(solution)/shard_map/ppermute | solution.py:397
  206.2 9.8 %collective-permute-done.18.refs_3_ = bf16[512,1024]{1,0:T(8,128)(2,1)} collective-permute-done((bf16[512,1024]{1,0:T(8,128)(2,1)}, bf16[512,1024]{1,0:T(8,128)(2,1)}, u32[]{:S(2)}, u32[]{:S(2)}) %collective-permute-start.18) | collective-permute-done | bytes 1048608 | tf_op jit(solution)/shard_map/ppermute | solution.py:284
  218.9 3.3 %collective-permute-start.21 = (f32[2,512]{1,0:T(2,128)S(1)}, f32[2,512]{1,0:T(2,128)S(1)}, u32[]{:S(2)}, u32[]{:S(2)}) collective-permute-start(f32[2,512]{1,0:T(2,128)S(1)} %pad_maximum_fusion.1), channel_id=1, source_target_pairs={{0,3},{1,0},{2,1},{3,2},{4,7},{5,4},{6,5},{7,6},{8,11},{9,8},{10,9... | collective-permute-start | bytes 12296 | tf_op jit(solution)/shard_map/ppermute | solution.py:397
  224.4 3.3 %collective-permute-done.19 = f32[2,512]{1,0:T(2,128)S(1)} collective-permute-done((f32[2,512]{1,0:T(2,128)S(1)}, f32[2,512]{1,0:T(2,128)S(1)}, u32[]{:S(2)}, u32[]{:S(2)}) %collective-permute-start.19) | collective-permute-done | bytes 4128 | tf_op jit(solution)/shard_map/ppermute | solution.py:397
  233.9 4.9 %shard_map.128.refs_1_ = bf16[2,4,64,512]{3,2,1,0:T(8,128)(2,1)} custom-call(s32[9]{0:T(128)S(1)} %dynamic-slice_bitcast_fusion.ids_ref, bf16[2,3,64,512]{3,2,1,0:T(8,128)(2,1)S(1)} %collective-permute-done.22.refs_0_, bf16[2,4,64,512]{3,2,1,0:T(8,128)(2,1)S(1)} %bitcast.30, bf16[2,3,64,512]{3,2,1,0:T(8,128)(2,1)S(1)} %collective-permute-done.23.refs_2_, ...), custom_call_target="tpu_custom_call" | custom-call | flops 4294967296 | bytes 12582912 | tf_op jit(solution)/shard_map/pallas_call | solution.py:56
  243.4 12.2 %collective-permute-start.24 = (bf16[256,1024]{1,0:T(8,128)(2,1)S(1)}, bf16[256,1024]{1,0:T(8,128)(2,1)S(1)}, u32[]{:S(2)}, u32[]{:S(2)}) collective-permute-start(bf16[256,1024]{1,0:T(8,128)(2,1)S(1)} %shard_map.129), channel_id=1, source_target_pairs={{0,4},{4,0},{8,12},{12,8},{16,20},{20,16},{24,28},{28,24},{1,5},{5... | collective-permute-start | bytes 1572872 | tf_op jit(solution)/shard_map/ppermute | solution.py:304
  (160 shorter events, 64.3 us)
Async XLA Ops:
  7.2 99.1 %all-gather.3.cloned.1.call-start = ((), (), s32[]{:S(2)}) async-start(), calls=%async_computation.2 | async-start | bytes 9437184 | tf_op jit(solution)/shard_map/all_gather | solution.py:421
  8.0 124.9 %all-gather.5.cloned.1.call-start = ((), (), s32[]{:S(2)}) async-start(), calls=%async_computation.3 | async-start | bytes 9437184 | tf_op jit(solution)/shard_map/all_gather | solution.py:422
  8.7 246.9 %reduce-scatter.5.cloned.1.call-start = ((), (), s32[]{:S(2)}) async-start(), calls=%async_computation.5 | async-start | bytes 5242880 | tf_op jit(solution)/shard_map/reduce_scatter | solution.py:408
  8.9 16.8 %collective-permute-start.3 = (bf16[512,512]{1,0:T(8,128)(2,1)S(1)}, bf16[512,512]{1,0:T(8,128)(2,1)S(1)}, u32[]{:S(2)}, u32[]{:S(2)}) collective-permute-start(bf16[512,512]{1,0:T(8,128)(2,1)S(1)} %fusion.1.refs_0_), channel_id=1, source_target_pairs={{0,1},{1,2},{2,3},{4,5},{5,6},{6,7},{8,9},{9,10},{10,11},{12,13},{... | collective-permute-start | bytes 1572872 | tf_op jit(solution)/shard_map/ppermute | solution.py:123
  13.9 15.8 %collective-permute-start.2 = (bf16[512,512]{1,0:T(8,128)(2,1)S(1)}, bf16[512,512]{1,0:T(8,128)(2,1)S(1)}, u32[]{:S(2)}, u32[]{:S(2)}) collective-permute-start(bf16[512,512]{1,0:T(8,128)(2,1)S(1)} %fusion.1.refs_0_), channel_id=1, source_target_pairs={{1,0},{2,1},{3,2},{5,4},{6,5},{7,6},{9,8},{10,9},{11,10},{13,12},{... | collective-permute-start | bytes 1572872 | tf_op jit(solution)/shard_map/ppermute | solution.py:122
  16.1 8.8 %collective-permute-start.1 = (bf16[2,3,64,512]{3,2,1,0:T(8,128)(2,1)}, bf16[2,3,64,512]{3,2,1,0:T(8,128)(2,1)S(1)}, u32[]{:S(2)}, u32[]{:S(2)}) collective-permute-start(bf16[2,3,64,512]{3,2,1,0:T(8,128)(2,1)} %get-tuple-element.54), channel_id=1, source_target_pairs={{4,0},{8,4},{12,8},{16,12},{20,16},{24,20},{28,24},{5,1},{9,5},{13... | collective-permute-start | bytes 1179656 | tf_op jit(solution)/shard_map/ppermute | solution.py:381
  17.4 7.5 %collective-permute-start = (bf16[2,3,64,512]{3,2,1,0:T(8,128)(2,1)}, bf16[2,3,64,512]{3,2,1,0:T(8,128)(2,1)S(1)}, u32[]{:S(2)}, u32[]{:S(2)}) collective-permute-start(bf16[2,3,64,512]{3,2,1,0:T(8,128)(2,1)} %get-tuple-element.55), channel_id=1, source_target_pairs={{0,4},{4,8},{8,12},{12,16},{16,20},{20,24},{24,28},{1,5},{5,9},{9,... | collective-permute-start | bytes 1179656 | tf_op jit(solution)/shard_map/ppermute | solution.py:380
  20.5 33.6 %collective-permute-start.7 = (bf16[512,512]{1,0:T(8,128)(2,1)S(1)}, bf16[512,512]{1,0:T(8,128)(2,1)S(1)}, u32[]{:S(2)}, u32[]{:S(2)}) collective-permute-start(bf16[512,512]{1,0:T(8,128)(2,1)S(1)} %fusion.1.refs_0_), channel_id=1, source_target_pairs={{0,2},{1,3},{2,0},{3,1},{4,6},{5,7},{6,4},{7,5},{8,10},{9,11},{10,... | collective-permute-start | bytes 1572872 | tf_op jit(solution)/shard_map/ppermute | solution.py:121
  38.3 41.3 %collective-permute-start.6 = (bf16[528,512]{1,0:T(8,128)(2,1)S(1)}, bf16[528,512]{1,0:T(8,128)(2,1)S(1)}, u32[]{:S(2)}, u32[]{:S(2)}) collective-permute-start(bf16[528,512]{1,0:T(8,128)(2,1)S(1)} %fusion.4.refs_1_.refs_0_), channel_id=1, source_target_pairs={{0,3},{1,0},{2,1},{3,2},{4,7},{5,4},{6,5},{7,6},{8,11},{9,8},{10,9... | collective-permute-start | bytes 1622024 | tf_op jit(solution)/shard_map/ppermute | solution.py:397
  54.7 20.9 %collective-permute-start.8 = (bf16[512,512]{1,0:T(8,128)(2,1)S(1)}, bf16[512,512]{1,0:T(8,128)(2,1)S(1)}, u32[]{:S(2)}, u32[]{:S(2)}) collective-permute-start(bf16[512,512]{1,0:T(8,128)(2,1)S(1)} %shard_map.112.refs_2_), channel_id=1, source_target_pairs={{1,0},{2,3},{5,4},{6,7},{9,8},{10,11},{13,12},{14,15},{17,16},{18,... | collective-permute-start | bytes 1572872 | tf_op jit(solution)/shard_map/ppermute | solution.py:131
  56.0 45.3 %collective-permute-start.5 = (bf16[528,512]{1,0:T(8,128)(2,1)S(1)}, bf16[528,512]{1,0:T(8,128)(2,1)S(1)}, u32[]{:S(2)}, u32[]{:S(2)}) collective-permute-start(bf16[528,512]{1,0:T(8,128)(2,1)S(1)} %fusion.4.refs_1_.refs_0_), channel_id=1, source_target_pairs={{0,2},{1,3},{2,0},{3,1},{4,6},{5,7},{6,4},{7,5},{8,10},{9,11},{10,... | collective-permute-start | bytes 1622024 | tf_op jit(solution)/shard_map/ppermute | solution.py:397
  66.7 34.5 %collective-permute-start.4 = (bf16[528,512]{1,0:T(8,128)(2,1)S(1)}, bf16[528,512]{1,0:T(8,128)(2,1)S(1)}, u32[]{:S(2)}, u32[]{:S(2)}) collective-permute-start(bf16[528,512]{1,0:T(8,128)(2,1)S(1)} %fusion.4.refs_1_.refs_0_), channel_id=1, source_target_pairs={{0,1},{1,2},{2,3},{3,0},{4,5},{5,6},{6,7},{7,4},{8,9},{9,10},{10,1... | collective-permute-start | bytes 1622024 | tf_op jit(solution)/shard_map/ppermute | solution.py:397
  105.8 8.7 %collective-permute-start.9 = (bf16[512,2048]{1,0:T(8,128)(2,1)}, bf16[512,2048]{1,0:T(8,128)(2,1)S(1)}, u32[]{:S(2)}, u32[]{:S(2)}) collective-permute-start(bf16[512,2048]{1,0:T(8,128)(2,1)} %shard_map.115.refs_0_), channel_id=1, source_target_pairs={{0,4},{4,0},{8,12},{12,8},{16,20},{20,16},{24,28},{28,24},{1,5},{5... | collective-permute-start | bytes 6291464 | tf_op jit(solution)/shard_map/ppermute | solution.py:419
  105.9 18.2 %collective-permute-start.10 = (bf16[512,2048]{1,0:T(8,128)(2,1)}, bf16[512,2048]{1,0:T(8,128)(2,1)}, u32[]{:S(2)}, u32[]{:S(2)}) collective-permute-start(bf16[512,2048]{1,0:T(8,128)(2,1)} %shard_map.113.refs_1_.refs_0_), channel_id=1, source_target_pairs={{0,4},{4,0},{8,12},{12,8},{16,20},{20,16},{24,28},{28,24},{1,5},{5... | collective-permute-start | bytes 6291464 | tf_op jit(solution)/shard_map/ppermute | solution.py:419
  132.8 128.2 %reduce-scatter.3.cloned.1.call-start = ((), (), s32[]{:S(2)}) async-start(), calls=%async_computation.4 | async-start | bytes 2621440 | tf_op jit(solution)/shard_map/reduce_scatter | solution.py:471
  157.5 14.3 %collective-permute-start.11 = (bf16[512,2048]{1,0:T(8,128)(2,1)}, bf16[512,2048]{1,0:T(8,128)(2,1)S(1)}, u32[]{:S(2)}, u32[]{:S(2)}) collective-permute-start(bf16[512,2048]{1,0:T(8,128)(2,1)} %shard_map.121.refs_3_), channel_id=1, source_target_pairs={{0,4},{4,0},{8,12},{12,8},{16,20},{20,16},{24,28},{28,24},{1,5},{5... | collective-permute-start | bytes 6291464 | tf_op jit(solution)/shard_map/ppermute | solution.py:419
  166.6 25.6 %collective-permute-start.13 = (bf16[512,512]{1,0:T(8,128)(2,1)S(1)}, bf16[512,512]{1,0:T(8,128)(2,1)S(1)}, u32[]{:S(2)}, u32[]{:S(2)}) collective-permute-start(bf16[512,512]{1,0:T(8,128)(2,1)S(1)} %get-tuple-element.32), channel_id=1, source_target_pairs={{0,1},{1,2},{2,3},{3,0},{4,5},{5,6},{6,7},{7,4},{8,9},{9,10},{10,1... | collective-permute-start | bytes 1572872 | tf_op jit(solution)/shard_map/ppermute | solution.py:397
  168.2 36.8 %collective-permute-start.14 = (bf16[512,512]{1,0:T(8,128)(2,1)S(1)}, bf16[512,512]{1,0:T(8,128)(2,1)S(1)}, u32[]{:S(2)}, u32[]{:S(2)}) collective-permute-start(bf16[512,512]{1,0:T(8,128)(2,1)S(1)} %get-tuple-element.34), channel_id=1, source_target_pairs={{0,2},{1,3},{2,0},{3,1},{4,6},{5,7},{6,4},{7,5},{8,10},{9,11},{10,... | collective-permute-start | bytes 1572872 | tf_op jit(solution)/shard_map/ppermute | solution.py:397
  170.7 34.4 %collective-permute-start.15 = (bf16[512,512]{1,0:T(8,128)(2,1)}, bf16[512,512]{1,0:T(8,128)(2,1)S(1)}, u32[]{:S(2)}, u32[]{:S(2)}) collective-permute-start(bf16[512,512]{1,0:T(8,128)(2,1)} %get-tuple-element.35), channel_id=1, source_target_pairs={{0,3},{1,0},{2,1},{3,2},{4,7},{5,4},{6,5},{7,6},{8,11},{9,8},{10,9... | collective-permute-start | bytes 1572872 | tf_op jit(solution)/shard_map/ppermute | solution.py:397
  190.2 25.8 %collective-permute-start.18 = (bf16[512,1024]{1,0:T(8,128)(2,1)}, bf16[512,1024]{1,0:T(8,128)(2,1)}, u32[]{:S(2)}, u32[]{:S(2)}) collective-permute-start(bf16[512,1024]{1,0:T(8,128)(2,1)} %get-tuple-element.38), channel_id=1, source_target_pairs={{0,8},{4,20},{8,24},{12,4},{24,16},{28,12},{16,0},{20,28},{1,9},{5... | collective-permute-start | bytes 3145736 | tf_op jit(solution)/shard_map/ppermute | solution.py:284
  191.4 24.6 %collective-permute-start.16 = (bf16[512,1024]{1,0:T(8,128)(2,1)}, bf16[512,1024]{1,0:T(8,128)(2,1)S(1)}, u32[]{:S(2)}, u32[]{:S(2)}) collective-permute-start(bf16[512,1024]{1,0:T(8,128)(2,1)} %get-tuple-element.33.refs_1_), channel_id=1, source_target_pairs={{0,16},{4,12},{8,0},{12,28},{24,8},{28,20},{16,24},{20,4},{1,17},{... | collective-permute-start | bytes 3145736 | tf_op jit(solution)/shard_map/ppermute | solution.py:284
  217.2 7.2 %collective-permute-start.20 = (f32[2,512]{1,0:T(2,128)S(1)}, f32[2,512]{1,0:T(2,128)S(1)}, u32[]{:S(2)}, u32[]{:S(2)}) collective-permute-start(f32[2,512]{1,0:T(2,128)S(1)} %pad_maximum_fusion.1), channel_id=1, source_target_pairs={{0,2},{1,3},{2,0},{3,1},{4,6},{5,7},{6,4},{7,5},{8,10},{9,11},{10,... | collective-permute-start | bytes 12296 | tf_op jit(solution)/shard_map/ppermute | solution.py:397
  222.5 16.3 %collective-permute-start.17 = (bf16[512,1024]{1,0:T(8,128)(2,1)S(1)}, bf16[512,1024]{1,0:T(8,128)(2,1)S(1)}, u32[]{:S(2)}, u32[]{:S(2)}) collective-permute-start(bf16[512,1024]{1,0:T(8,128)(2,1)S(1)} %add_convert_fusion.1), channel_id=1, source_target_pairs={{0,16},{4,12},{8,0},{12,28},{24,8},{28,20},{16,24},{20,4},{1,17},{... | collective-permute-start | bytes 3145736 | tf_op jit(solution)/shard_map/ppermute | solution.py:289
  243.4 14.1 %collective-permute-start.24 = (bf16[256,1024]{1,0:T(8,128)(2,1)S(1)}, bf16[256,1024]{1,0:T(8,128)(2,1)S(1)}, u32[]{:S(2)}, u32[]{:S(2)}) collective-permute-start(bf16[256,1024]{1,0:T(8,128)(2,1)S(1)} %shard_map.129), channel_id=1, source_target_pairs={{0,4},{4,0},{8,12},{12,8},{16,20},{20,16},{24,28},{28,24},{1,5},{5... | collective-permute-start | bytes 1572872 | tf_op jit(solution)/shard_map/ppermute | solution.py:304
  (37 other events, 216.0 us)
Sparse Core Ops, SparseCore 0:
  9.9 64.7 all-gather.2
  76.6 54.3 all-gather.4
  134.0 52.6 reduce-scatter.4
  206.3 52.9 reduce-scatter.2

commit v5 on v4

--- a/solution.py
+++ b/solution.py
@@ -23,7 +23,7 @@
 SAME_CORE = [[0, 2, 4, 6], [1, 3, 5, 7]]
 ANY = pl.BlockSpec(memory_space=pl.ANY)
 VMEM = pl.BlockSpec(memory_space=pltpu.VMEM)
-PARAMS = pltpu.CompilerParams(vmem_limit_bytes=52 * 2**20)
+PARAMS = pltpu.CompilerParams(vmem_limit_bytes=46 * 2**20)
 HINT = pl.CostEstimate(flops=0, bytes_accessed=0, transcendentals=0)
 WORK = pl.CostEstimate(flops=2**32, bytes_accessed=12 * 2**20, transcendentals=0)
 
@@ -168,7 +168,7 @@
     return v * cdf, cdf + v * jnp.exp(-0.5 * v * v) * 0.3989422804014327
 
 
-TILE = 256
+TILE = 512
 
 
 def expand(ids, rows, panel, after=()):
@@ -189,26 +189,23 @@
     )
 
 
-def expand_grad(ids, strips, panel, slopes, after):
-    rows, hid = slopes[0].shape
+def expand_grad(ids, strip, panel, slope, after):
+    rows, hid = slope.shape
     steps = hid // TILE
 
-    def kernel(ids_ref, own_ref, sib_ref, w_ref, own_slope, sib_slope, own_out, sib_out):
-        for x, slope, out in ((own_ref, own_slope, own_out), (sib_ref, sib_slope, sib_out)):
-            back = jnp.dot(x[...], w_ref[...], preferred_element_type=F32)
-            out[...] = (back * slope[...].astype(F32)).astype(BF16)
+    def kernel(ids_ref, x_ref, w_ref, slope_ref, out_ref):
+        back = jnp.dot(x_ref[...], w_ref[...], preferred_element_type=F32)
+        out_ref[...] = (back * slope_ref[...].astype(F32)).astype(BF16)
 
     tile = pl.BlockSpec((rows, TILE), lambda t, i: (0, t))
     return call(
-        kernel, ids, [*strips, panel, *slopes], (steps,),
+        kernel, ids, [strip, panel, slope], (steps,),
         [
-            whole(strips[0].shape),
-            whole(strips[1].shape),
+            whole(strip.shape),
             pl.BlockSpec((C, TILE), lambda t, i: (0, i[4] * steps + t)),
             tile,
-            tile,
         ],
-        [tile, tile], [shape((rows, hid))] * 2, after=after,
+        tile, shape((rows, hid)), after=after,
     )
 
 
@@ -249,11 +246,11 @@
             acc = acc + refs[0][...].astype(F32)
         refs[-1][...] = acc.astype(BF16)
 
-    cut = pl.BlockSpec((rows, 512), lambda t, i: (0, t))
+    cut = pl.BlockSpec((rows, 1024), lambda t, i: (0, t))
     more = [] if other is None else [other]
     return call(
-        kernel, ids, [left, panel, *more], (C // 512,),
-        [whole((rows, hid)), pl.BlockSpec((512, hid), lambda t, i: (t, i[4]))] + [cut] * len(more),
+        kernel, ids, [left, panel, *more], (C // 1024,),
+        [whole((rows, hid)), pl.BlockSpec((1024, hid), lambda t, i: (t, i[4]))] + [cut] * len(more),
         cut, shape((rows, C)), after=after,
     )
 
@@ -397,6 +394,20 @@
     return lax.ppermute(array, "col", [(i, (i + step) % count) for i in range(count)])
 
 
+def residual(ids, images, layer_scale, branch, after):
+    rows, chans = images.shape
+
+    def kernel(ids_ref, images_ref, scale_ref, branch_ref, out_ref):
+        value = images_ref[...].astype(F32) + scale_ref[...] * branch_ref[...].astype(F32)
+        out_ref[...] = value.astype(BF16)
+
+    cut = pl.BlockSpec((rows // 2, chans), lambda t, i: (t, 0))
+    return call(
+        kernel, ids, [images, layer_scale.reshape(1, chans), branch], (2,),
+        [cut, whole((1, chans)), cut], cut, shape((rows, chans)), after=after,
+    )
+
+
 def added(blocks):
     total = blocks[0].astype(F32)
     for block in blocks[1:]:
@@ -454,17 +465,16 @@
     hidden = hidden_own, hidden_sib
     out_part = weight_grad(ids, grad_own, grad_sib, hidden, False)
     out_rows = row_scatter(out_part)
-    grad_pre = expand_grad(
-        ids, (grad_own, grad_sib), out_panel, (slope_own, slope_sib), [out_part]
-    )
-    back_give = contract(ids, grad_pre[1], in_panel)
+    pre_sib = expand_grad(ids, grad_sib, out_panel, slope_sib, [out_part])
+    back_give = contract(ids, pre_sib, in_panel)
     back_sib = swap(back_give)
-    branch_give = contract(ids, hidden_sib, out_panel, None, [back_give])
+    pre_own = expand_grad(ids, grad_own, out_panel, slope_own, [back_give])
+    back = contract_own(ids, pre_own, in_panel, back_sib)
+    back_sent = [shifted(back[step], step) for step in (1, 2, 3)]
+    branch_give = contract(ids, hidden_sib, out_panel, None, [back[0]])
     branch_sib = swap(branch_give)
-    back = contract_own(ids, grad_pre[0], in_panel, back_sib, [branch_give])
-    back_sent = [shifted(back[step], step) for step in (1, 2, 3)]
     contrib = contract(ids, hidden_own, out_panel, branch_sib, [back[0]])
-    in_parts = weight_grad(ids, in_own, in_sib, grad_pre, True, [contrib])
+    in_parts = weight_grad(ids, in_own, in_sib, (pre_own, pre_sib), True, [contrib])
     in_sent = ring_send(in_parts)
     back_sent[0] = later(ids, back_sent[0], [in_parts[0], *back_sent[1:]])
     contrib = later(ids, contrib, [back_sent[0]])
@@ -483,9 +493,8 @@
     low, high = rims(grad_conv)
     grad_images = taps(ids, low, grad_conv, high, dw_kernel, True, cotangent)
     grad_in, grad_out = own_rows(ids, in_rows, [grad_images]), own_rows(ids, out_rows)
-    branch = later(ids, branch, [grad_in, grad_out])
-    residual_in = images.reshape(pixels, local_ch).astype(F32)
-    block_out = (residual_in + layer_scale * branch.astype(F32)).astype(BF16).reshape(images.shape)
+    flat = images.reshape(pixels, local_ch)
+    block_out = residual(ids, flat, layer_scale, branch, [grad_in, grad_out]).reshape(images.shape)
     return block_out, grad_images, grad_in, grad_out
 
 

time: 272 us -> 267 us (0.982)
  Pallas kernels: 96.3 us -> 83.1 us
  local copies, waits for them, and re-layouts: 17.5 us -> 22.3 us
  starting transfers between devices: 60.9 us -> 64.5 us
    pallas_call x23 -> x24, Pallas kernels: 96.3 us -> 83.1 us  [call(): pl.pallas_call(kernel, grid_spec=pltpu.PrefetchScalarGridSpec(num_scalar_...]
    ppermute x9, waiting for transfers between devices: 37.8 us -> 44.3 us  [shifted(): lax.ppermute(array, 'col', [(i, (i + step) % count) for i in range(count)])]
    ppermute x1, waiting for transfers between devices: 9.79 us -> 5.69 us  [ring_send(): lax.ppermute(blocks[1], 'row', AHEAD)]
    ppermute x9, starting transfers between devices: 23.5 us -> 27.1 us  [shifted(): lax.ppermute(array, 'col', [(i, (i + step) % count) for i in range(count)])]
    unnamed x62 -> x118, local copies, waits for them, and re-layouts: 15.4 us -> 18.6 us
    ppermute x1, waiting for transfers between devices: 13.3 us -> 10.5 us  [col_send(): across = lax.ppermute(block, 'col', ACROSS)]
  transfers between devices with their start and end apart: 30 -> 30, of which waited for: 9 -> 11; matrix products, arithmetic and copies ran while one was open for 3% -> 4% of each run, Pallas kernels for 35% -> 31%
where the time goes in v5:
time: 267 us; the launch traced here: 266 us
  Pallas kernels  83.1 us (31%)
  waiting for transfers between devices  76.1 us (29%)
  starting transfers between devices  64.5 us (24%)
  local copies, waits for them, and re-layouts  22.3 us (8%)
  between operations  14.6 us (5%)
  other arithmetic  5.71 us (2%)
    pallas_call x24, Pallas kernels, call(): pl.pallas_call(kernel, grid_spec=pltpu.PrefetchScalarGridSpec(num_scalar_...  83.1 us
    ppermute x9, waiting for transfers between devices, shifted(): lax.ppermute(array, 'col', [(i, (i + step) % count) for i in range(count)])  44.3 us
    ppermute x9, starting transfers between devices, shifted(): lax.ppermute(array, 'col', [(i, (i + step) % count) for i in range(count)])  27.1 us
    unnamed x118, local copies, waits for them, and re-layouts  18.6 us
    ppermute x2, starting transfers between devices, own_rows(): other = lax.ppermute(give_rows(ids, block, after), 'row', SIBLING)  12.1 us
    ppermute x1, waiting for transfers between devices, col_send(): across = lax.ppermute(block, 'col', ACROSS)  10.5 us
    ppermute x1, waiting for transfers between devices, col_gather(): far = lax.ppermute(across, 'col', [(1, 0), (2, 3)])  7.94 us
    ppermute x2, starting transfers between devices, rims(): low = lax.ppermute(block[:, -REACH:], 'row', forward)  6.98 us
  transfers between devices with their start and end apart: 30, of which 11 were waited for; matrix products, arithmetic and copies ran while one was open for 4% of the time, Pallas kernels for 31%

profile of v5, /device:TPU:0, one launch (start us, length us, event | category | flops | bytes accessed | tf_op | source)
XLA Modules:
  0.0 266.2 jit_solution(1063745333392578049)
XLA Ops:
  8.9 5.0 %collective-permute-start.3 = (bf16[512,512]{1,0:T(8,128)(2,1)S(1)}, bf16[512,512]{1,0:T(8,128)(2,1)S(1)}, u32[]{:S(2)}, u32[]{:S(2)}) collective-permute-start(bf16[512,512]{1,0:T(8,128)(2,1)S(1)} %fusion.1.refs_0_), channel_id=1, source_target_pairs={{0,1},{1,2},{2,3},{4,5},{5,6},{6,7},{8,9},{9,10},{10,11},{12,13},{... | collective-permute-start | bytes 1572872 | tf_op jit(solution)/shard_map/ppermute | solution.py:123
  17.4 3.8 %collective-permute-start = (bf16[2,3,64,512]{3,2,1,0:T(8,128)(2,1)}, bf16[2,3,64,512]{3,2,1,0:T(8,128)(2,1)}, u32[]{:S(2)}, u32[]{:S(2)}) collective-permute-start(bf16[2,3,64,512]{3,2,1,0:T(8,128)(2,1)} %get-tuple-element.51), channel_id=1, source_target_pairs={{0,4},{4,8},{8,12},{12,16},{16,20},{20,24},{24,28},{1,5},{5,9},{9,... | collective-permute-start | bytes 1179656 | tf_op jit(solution)/shard_map/ppermute | solution.py:377
  21.2 3.6 %collective-permute-start.7 = (bf16[512,512]{1,0:T(8,128)(2,1)S(1)}, bf16[512,512]{1,0:T(8,128)(2,1)S(1)}, u32[]{:S(2)}, u32[]{:S(2)}) collective-permute-start(bf16[512,512]{1,0:T(8,128)(2,1)S(1)} %fusion.1.refs_0_), channel_id=1, source_target_pairs={{0,2},{1,3},{2,0},{3,1},{4,6},{5,7},{6,4},{7,5},{8,10},{9,11},{10,... | collective-permute-start | bytes 1572872 | tf_op jit(solution)/shard_map/ppermute | solution.py:121
  30.6 5.5 %shard_map.111 = (f32[2,4,64,512]{3,2,1,0:T(8,128)S(1)}, bf16[2,4,64,512]{3,2,1,0:T(8,128)(2,1)S(1)}, f32[2,4,64,1]{3,2,1,0:T(8,128)S(1)}, f32[2,4,64,1]{3,2,1,0:T(8,128)S(1)}) custom-call(s32[9]{0:T(128)S(1)} %dynamic-slice_bitcast_fusion.ids_ref, bf16[2,3,64,512]{3,2,1,0:T(8,128)(2,1)} %collective-permute-done.refs_0_, ...), custom_call_target="tpu_custom_call" | custom-call | flops 4294967296 | bytes 12582912 | tf_op jit(solution)/shard_map/pallas_call | solution.py:56
  42.8 10.5 %collective-permute-done.7.refs_0_ = bf16[512,512]{1,0:T(8,128)(2,1)S(1)} collective-permute-done((bf16[512,512]{1,0:T(8,128)(2,1)S(1)}, bf16[512,512]{1,0:T(8,128)(2,1)S(1)}, u32[]{:S(2)}, u32[]{:S(2)}) %collective-permute-start.7) | collective-permute-done | bytes 524320 | tf_op jit(solution)/shard_map/ppermute | solution.py:121
  56.0 11.6 %collective-permute-start.5 = (bf16[528,512]{1,0:T(8,128)(2,1)S(1)}, bf16[528,512]{1,0:T(8,128)(2,1)S(1)}, u32[]{:S(2)}, u32[]{:S(2)}) collective-permute-start(bf16[528,512]{1,0:T(8,128)(2,1)S(1)} %fusion.3.refs_1_.refs_0_), channel_id=1, source_target_pairs={{0,2},{1,3},{2,0},{3,1},{4,6},{5,7},{6,4},{7,5},{8,10},{9,11},{10,... | collective-permute-start | bytes 1622024 | tf_op jit(solution)/shard_map/ppermute | solution.py:394
  67.6 7.9 %collective-permute-done.8.refs_4_ = bf16[512,512]{1,0:T(8,128)(2,1)S(1)} collective-permute-done((bf16[512,512]{1,0:T(8,128)(2,1)S(1)}, bf16[512,512]{1,0:T(8,128)(2,1)S(1)}, u32[]{:S(2)}, u32[]{:S(2)}) %collective-permute-start.8) | collective-permute-done | bytes 524320 | tf_op jit(solution)/shard_map/ppermute | solution.py:131
  77.5 24.6 %collective-permute-done.5.refs_2_ = bf16[528,512]{1,0:T(8,128)(2,1)S(1)} collective-permute-done((bf16[528,512]{1,0:T(8,128)(2,1)S(1)}, bf16[528,512]{1,0:T(8,128)(2,1)S(1)}, u32[]{:S(2)}, u32[]{:S(2)}) %collective-permute-start.5) | collective-permute-done | bytes 540704 | tf_op jit(solution)/shard_map/ppermute | solution.py:394
  113.7 6.1 %shard_map.116 = (bf16[512,1024]{1,0:T(8,128)(2,1)S(1)}, bf16[512,1024]{1,0:T(8,128)(2,1)S(1)}) custom-call(s32[9]{0:T(128)S(1)} %copy-done.33, bf16[512,2048]{1,0:T(8,128)(2,1)} %shard_map.115.refs_0_, bf16[2048,2048]{1,0:T(8,128)(2,1)} %all-gather.3.cloned.1.call-done.refs_1_), custom_call_target="tpu_custom_call" | custom-call | flops 4294967296 | bytes 12582912 | tf_op jit(solution)/shard_map/pallas_call | solution.py:56
  120.8 6.1 %shard_map.117 = (bf16[512,1024]{1,0:T(8,128)(2,1)S(1)}, bf16[512,1024]{1,0:T(8,128)(2,1)S(1)}) custom-call(s32[9]{0:T(128)S(1)} %copy-done.33, bf16[512,2048]{1,0:T(8,128)(2,1)} %collective-permute-done.9.refs_0_.refs_1_, bf16[2048,2048]{1,0:T(8,128)(2,1)} %all-gather.3.cloned.1.call-done.refs_1_, bf16[512,1024]{1,0:T(8,128)(2,1)S(1)} %get-tuple-element.23.refs_2_.refs_0_), custom_call_target="tpu_custom_call" | custom-call | flops 4294967296 | bytes 12582912 | tf_op jit(solution)/shard_map/pallas_call | solution.py:56
  126.9 8.0 %shard_map.118.refs_3_ = bf16[2048,1024]{1,0:T(8,128)(2,1)} custom-call(s32[9]{0:T(128)S(1)} %copy-done.33, bf16[512,2048]{1,0:T(8,128)(2,1)S(1)} %shard_map.113.refs_1_.refs_0_, bf16[512,2048]{1,0:T(8,128)(2,1)} %collective-permute-done.10.refs_1_.refs_0_, bf16[512,1024]{1,0:T(8,128)(2,1)S(1)} %get-tuple-element.23.refs_2_.refs_0_, ...), custom_call_target="tpu_custom_call" | custom-call | flops 4294967296 | bytes 12582912 | tf_op jit(solution)/shard_map/pallas_call | solution.py:56
  136.6 5.4 %shard_map.119.refs_0_.refs_3_ = bf16[512,1024]{1,0:T(8,128)(2,1)S(1)} custom-call(s32[9]{0:T(128)S(1)} %copy-done.34, bf16[512,2048]{1,0:T(8,128)(2,1)} %collective-permute-done.10.refs_1_.refs_0_, bf16[2048,2048]{1,0:T(8,128)(2,1)} %all-gather.5.cloned.1.call-done.refs_1_, bf16[512,1024]{1,0:T(8,128)(2,1)S(1)} %get-tuple-element.26.refs_2_, ...), custom_call_target="tpu_custom_call" | custom-call | flops 4294967296 | bytes 12582912 | tf_op jit(solution)/shard_map/pallas_call | solution.py:56
  142.0 4.9 %shard_map.120.refs_3_ = bf16[512,2048]{1,0:T(8,128)(2,1)S(1)} custom-call(s32[9]{0:T(128)S(1)} %copy-done.34, bf16[512,1024]{1,0:T(8,128)(2,1)S(1)} %shard_map.119.refs_0_.refs_3_, bf16[2048,2048]{1,0:T(8,128)(2,1)} %all-gather.3.cloned.1.call-done.refs_1_), custom_call_target="tpu_custom_call" | custom-call | flops 4294967296 | bytes 12582912 | tf_op jit(solution)/shard_map/pallas_call | solution.py:56
  147.0 4.9 %shard_map.121.refs_0_.refs_2_ = bf16[512,1024]{1,0:T(8,128)(2,1)S(1)} custom-call(s32[9]{0:T(128)S(1)} %copy-done.34, bf16[512,2048]{1,0:T(8,128)(2,1)S(1)} %shard_map.113.refs_1_.refs_0_, bf16[2048,2048]{1,0:T(8,128)(2,1)} %all-gather.5.cloned.1.call-done.refs_1_, bf16[512,1024]{1,0:T(8,128)(2,1)S(1)} %copy-done.41, bf16[512,2048]{1,0:T(8,128)(2,1)S(1)} %shard_map.120.refs_3_), custom_call_target="tpu_custom_call" | custom-call | flops 4294967296 | bytes 12582912 | tf_op jit(solution)/shard_map/pallas_call | solution.py:56
  151.9 5.7 %shard_map.122 = (bf16[512,512]{1,0:T(8,128)(2,1)S(1)}, bf16[512,512]{1,0:T(8,128)(2,1)S(1)}, bf16[512,512]{1,0:T(8,128)(2,1)S(1)}, bf16[512,512]{1,0:T(8,128)(2,1)S(1)}) custom-call(s32[9]{0:T(128)S(1)} %copy-done.34, bf16[512,1024]{1,0:T(8,128)(2,1)S(1)} %shard_map.121.refs_0_.refs_2_, bf16[2048,2048]{1,0:T(8,128)(2,1)} %all-gather.3.cloned.1.call-done.refs_1_, ...), custom_call_target="tpu_custom_call" | custom-call | flops 4294967296 | bytes 12582912 | tf_op jit(solution)/shard_map/pallas_call | solution.py:56
  157.6 4.9 %shard_map.123 = bf16[512,2048]{1,0:T(8,128)(2,1)S(1)} custom-call(s32[9]{0:T(128)S(1)} %copy-done.34, bf16[512,1024]{1,0:T(8,128)(2,1)S(1)} %copy-done.45, bf16[2048,2048]{1,0:T(8,128)(2,1)} %all-gather.5.cloned.1.call-done.refs_1_, bf16[512,512]{1,0:T(8,128)(2,1)S(1)} %get-tuple-element.27.refs_2_.refs_3_), custom_call_target="tpu_custom_call" | custom-call | flops 4294967296 | bytes 12582912 | tf_op jit(solution)/shard_map/pallas_call | solution.py:56
  168.1 5.8 %shard_map.124.refs_4_.refs_0_ = bf16[512,2048]{1,0:T(8,128)(2,1)} custom-call(s32[9]{0:T(128)S(1)} %copy-done.34, bf16[512,1024]{1,0:T(8,128)(2,1)S(1)} %copy-done.43, bf16[2048,2048]{1,0:T(8,128)(2,1)} %all-gather.5.cloned.1.call-done.refs_1_, bf16[512,2048]{1,0:T(8,128)(2,1)S(1)} %collective-permute-done.12.refs_2_, ...), custom_call_target="tpu_custom_call" | custom-call | flops 4294967296 | bytes 12582912 | tf_op jit(solution)/shard_map/pallas_call | solution.py:56
  173.8 8.8 %shard_map.125 = (bf16[512,1024]{1,0:T(8,128)(2,1)}, bf16[512,1024]{1,0:T(8,128)(2,1)}, bf16[512,1024]{1,0:T(8,128)(2,1)S(1)}, bf16[512,1024]{1,0:T(8,128)(2,1)S(1)}) custom-call(s32[9]{0:T(128)S(1)} %copy-done.34, bf16[512,2048]{1,0:T(8,128)(2,1)} %shard_map.115.refs_0_, bf16[512,2048]{1,0:T(8,128)(2,1)} %collective-permute-done.9.refs_0_.refs_1_, ...), custom_call_target="tpu_custom_call" | custom-call | flops 4294967296 | bytes 12582912 | tf_op jit(solution)/shard_map/pallas_call | solution.py:56
  185.6 15.9 %collective-permute-done.14.refs_2_ = bf16[512,512]{1,0:T(8,128)(2,1)S(1)} collective-permute-done((bf16[512,512]{1,0:T(8,128)(2,1)S(1)}, bf16[512,512]{1,0:T(8,128)(2,1)S(1)}, u32[]{:S(2)}, u32[]{:S(2)}) %collective-permute-start.14) | collective-permute-done | bytes 524320 | tf_op jit(solution)/shard_map/ppermute | solution.py:394
  203.8 5.7 %collective-permute-done.18.refs_3_ = bf16[512,1024]{1,0:T(8,128)(2,1)S(1)} collective-permute-done((bf16[512,1024]{1,0:T(8,128)(2,1)}, bf16[512,1024]{1,0:T(8,128)(2,1)S(1)}, u32[]{:S(2)}, u32[]{:S(2)}) %collective-permute-start.18) | collective-permute-done | bytes 1048608 | tf_op jit(solution)/shard_map/ppermute | solution.py:281
  210.7 4.5 %collective-permute-start.20 = (f32[2,512]{1,0:T(2,128)S(1)}, f32[2,512]{1,0:T(2,128)S(1)}, u32[]{:S(2)}, u32[]{:S(2)}) collective-permute-start(f32[2,512]{1,0:T(2,128)S(1)} %pad_maximum_fusion.1), channel_id=1, source_target_pairs={{0,2},{1,3},{2,0},{3,1},{4,6},{5,7},{6,4},{7,5},{8,10},{9,11},{10,... | collective-permute-start | bytes 12296 | tf_op jit(solution)/shard_map/ppermute | solution.py:394
  220.3 3.8 %collective-permute-done.19 = f32[2,512]{1,0:T(2,128)S(1)} collective-permute-done((f32[2,512]{1,0:T(2,128)S(1)}, f32[2,512]{1,0:T(2,128)S(1)}, u32[]{:S(2)}, u32[]{:S(2)}) %collective-permute-start.19) | collective-permute-done | bytes 4128 | tf_op jit(solution)/shard_map/ppermute | solution.py:394
  230.4 4.9 %shard_map.129.refs_1_ = bf16[2,4,64,512]{3,2,1,0:T(8,128)(2,1)} custom-call(s32[9]{0:T(128)S(1)} %copy-done.34, bf16[2,3,64,512]{3,2,1,0:T(8,128)(2,1)S(1)} %collective-permute-done.22.refs_0_, bf16[2,4,64,512]{3,2,1,0:T(8,128)(2,1)S(1)} %bitcast.29, bf16[2,3,64,512]{3,2,1,0:T(8,128)(2,1)S(1)} %collective-permute-done.23.refs_2_, ...), custom_call_target="tpu_custom_call" | custom-call | flops 4294967296 | bytes 12582912 | tf_op jit(solution)/shard_map/pallas_call | solution.py:56
  237.2 12.0 %collective-permute-start.24 = (bf16[256,1024]{1,0:T(8,128)(2,1)S(1)}, bf16[256,1024]{1,0:T(8,128)(2,1)S(1)}, u32[]{:S(2)}, u32[]{:S(2)}) collective-permute-start(bf16[256,1024]{1,0:T(8,128)(2,1)S(1)} %shard_map.130), channel_id=1, source_target_pairs={{0,4},{4,0},{8,12},{12,8},{16,20},{20,16},{24,28},{28,24},{1,5},{5... | collective-permute-start | bytes 1572872 | tf_op jit(solution)/shard_map/ppermute | solution.py:301
  (216 shorter events, 71.7 us)
Async XLA Ops:
  7.2 105.8 %all-gather.3.cloned.1.call-start = ((), (), s32[]{:S(2)}) async-start(), calls=%async_computation.2 | async-start | bytes 9437184 | tf_op jit(solution)/shard_map/all_gather | solution.py:432
  8.0 128.1 %all-gather.5.cloned.1.call-start = ((), (), s32[]{:S(2)}) async-start(), calls=%async_computation.3 | async-start | bytes 9437184 | tf_op jit(solution)/shard_map/all_gather | solution.py:433
  8.7 240.5 %reduce-scatter.5.cloned.1.call-start = ((), (), s32[]{:S(2)}) async-start(), calls=%async_computation.5 | async-start | bytes 5242880 | tf_op jit(solution)/shard_map/reduce_scatter | solution.py:419
  8.9 17.5 %collective-permute-start.3 = (bf16[512,512]{1,0:T(8,128)(2,1)S(1)}, bf16[512,512]{1,0:T(8,128)(2,1)S(1)}, u32[]{:S(2)}, u32[]{:S(2)}) collective-permute-start(bf16[512,512]{1,0:T(8,128)(2,1)S(1)} %fusion.1.refs_0_), channel_id=1, source_target_pairs={{0,1},{1,2},{2,3},{4,5},{5,6},{6,7},{8,9},{9,10},{10,11},{12,13},{... | collective-permute-start | bytes 1572872 | tf_op jit(solution)/shard_map/ppermute | solution.py:123
  13.9 15.8 %collective-permute-start.2 = (bf16[512,512]{1,0:T(8,128)(2,1)S(1)}, bf16[512,512]{1,0:T(8,128)(2,1)S(1)}, u32[]{:S(2)}, u32[]{:S(2)}) collective-permute-start(bf16[512,512]{1,0:T(8,128)(2,1)S(1)} %fusion.1.refs_0_), channel_id=1, source_target_pairs={{1,0},{2,1},{3,2},{5,4},{6,5},{7,6},{9,8},{10,9},{11,10},{13,12},{... | collective-permute-start | bytes 1572872 | tf_op jit(solution)/shard_map/ppermute | solution.py:122
  16.1 9.5 %collective-permute-start.1 = (bf16[2,3,64,512]{3,2,1,0:T(8,128)(2,1)}, bf16[2,3,64,512]{3,2,1,0:T(8,128)(2,1)S(1)}, u32[]{:S(2)}, u32[]{:S(2)}) collective-permute-start(bf16[2,3,64,512]{3,2,1,0:T(8,128)(2,1)} %get-tuple-element.50), channel_id=1, source_target_pairs={{4,0},{8,4},{12,8},{16,12},{20,16},{24,20},{28,24},{5,1},{9,5},{13... | collective-permute-start | bytes 1179656 | tf_op jit(solution)/shard_map/ppermute | solution.py:378
  17.4 8.9 %collective-permute-start = (bf16[2,3,64,512]{3,2,1,0:T(8,128)(2,1)}, bf16[2,3,64,512]{3,2,1,0:T(8,128)(2,1)}, u32[]{:S(2)}, u32[]{:S(2)}) collective-permute-start(bf16[2,3,64,512]{3,2,1,0:T(8,128)(2,1)} %get-tuple-element.51), channel_id=1, source_target_pairs={{0,4},{4,8},{8,12},{12,16},{16,20},{20,24},{24,28},{1,5},{5,9},{9,... | collective-permute-start | bytes 1179656 | tf_op jit(solution)/shard_map/ppermute | solution.py:377
  21.2 32.1 %collective-permute-start.7 = (bf16[512,512]{1,0:T(8,128)(2,1)S(1)}, bf16[512,512]{1,0:T(8,128)(2,1)S(1)}, u32[]{:S(2)}, u32[]{:S(2)}) collective-permute-start(bf16[512,512]{1,0:T(8,128)(2,1)S(1)} %fusion.1.refs_0_), channel_id=1, source_target_pairs={{0,2},{1,3},{2,0},{3,1},{4,6},{5,7},{6,4},{7,5},{8,10},{9,11},{10,... | collective-permute-start | bytes 1572872 | tf_op jit(solution)/shard_map/ppermute | solution.py:121
  40.3 37.2 %collective-permute-start.6 = (bf16[528,512]{1,0:T(8,128)(2,1)S(1)}, bf16[528,512]{1,0:T(8,128)(2,1)S(1)}, u32[]{:S(2)}, u32[]{:S(2)}) collective-permute-start(bf16[528,512]{1,0:T(8,128)(2,1)S(1)} %fusion.3.refs_1_.refs_0_), channel_id=1, source_target_pairs={{0,3},{1,0},{2,1},{3,2},{4,7},{5,4},{6,5},{7,6},{8,11},{9,8},{10,9... | collective-permute-start | bytes 1622024 | tf_op jit(solution)/shard_map/ppermute | solution.py:394
  53.9 21.6 %collective-permute-start.8 = (bf16[512,512]{1,0:T(8,128)(2,1)S(1)}, bf16[512,512]{1,0:T(8,128)(2,1)S(1)}, u32[]{:S(2)}, u32[]{:S(2)}) collective-permute-start(bf16[512,512]{1,0:T(8,128)(2,1)S(1)} %shard_map.112.refs_2_), channel_id=1, source_target_pairs={{1,0},{2,3},{5,4},{6,7},{9,8},{10,11},{13,12},{14,15},{17,16},{18,... | collective-permute-start | bytes 1572872 | tf_op jit(solution)/shard_map/ppermute | solution.py:131
  56.0 46.1 %collective-permute-start.5 = (bf16[528,512]{1,0:T(8,128)(2,1)S(1)}, bf16[528,512]{1,0:T(8,128)(2,1)S(1)}, u32[]{:S(2)}, u32[]{:S(2)}) collective-permute-start(bf16[528,512]{1,0:T(8,128)(2,1)S(1)} %fusion.3.refs_1_.refs_0_), channel_id=1, source_target_pairs={{0,2},{1,3},{2,0},{3,1},{4,6},{5,7},{6,4},{7,5},{8,10},{9,11},{10,... | collective-permute-start | bytes 1622024 | tf_op jit(solution)/shard_map/ppermute | solution.py:394
  67.6 34.5 %collective-permute-start.4 = (bf16[528,512]{1,0:T(8,128)(2,1)S(1)}, bf16[528,512]{1,0:T(8,128)(2,1)S(1)}, u32[]{:S(2)}, u32[]{:S(2)}) collective-permute-start(bf16[528,512]{1,0:T(8,128)(2,1)S(1)} %fusion.3.refs_1_.refs_0_), channel_id=1, source_target_pairs={{0,1},{1,2},{2,3},{3,0},{4,5},{5,6},{6,7},{7,4},{8,9},{9,10},{10,1... | collective-permute-start | bytes 1622024 | tf_op jit(solution)/shard_map/ppermute | solution.py:394
  112.5 8.2 %collective-permute-start.9 = (bf16[512,2048]{1,0:T(8,128)(2,1)}, bf16[512,2048]{1,0:T(8,128)(2,1)}, u32[]{:S(2)}, u32[]{:S(2)}) collective-permute-start(bf16[512,2048]{1,0:T(8,128)(2,1)} %shard_map.115.refs_0_), channel_id=1, source_target_pairs={{0,4},{4,0},{8,12},{12,8},{16,20},{20,16},{24,28},{28,24},{1,5},{5... | collective-permute-start | bytes 6291464 | tf_op jit(solution)/shard_map/ppermute | solution.py:430
  112.5 14.4 %collective-permute-start.10 = (bf16[512,2048]{1,0:T(8,128)(2,1)S(1)}, bf16[512,2048]{1,0:T(8,128)(2,1)}, u32[]{:S(2)}, u32[]{:S(2)}) collective-permute-start(bf16[512,2048]{1,0:T(8,128)(2,1)S(1)} %shard_map.113.refs_1_.refs_0_), channel_id=1, source_target_pairs={{0,4},{4,0},{8,12},{12,8},{16,20},{20,16},{24,28},{28,24},{1,5},{5... | collective-permute-start | bytes 6291464 | tf_op jit(solution)/shard_map/ppermute | solution.py:430
  135.9 120.0 %reduce-scatter.3.cloned.1.call-start = ((), (), s32[]{:S(2)}) async-start(), calls=%async_computation.4 | async-start | bytes 2621440 | tf_op jit(solution)/shard_map/reduce_scatter | solution.py:481
  162.5 5.5 %collective-permute-start.12 = (bf16[512,2048]{1,0:T(8,128)(2,1)S(1)}, bf16[512,2048]{1,0:T(8,128)(2,1)S(1)}, u32[]{:S(2)}, u32[]{:S(2)}) collective-permute-start(bf16[512,2048]{1,0:T(8,128)(2,1)S(1)} %shard_map.123), channel_id=1, source_target_pairs={{0,4},{4,0},{8,12},{12,8},{16,20},{20,16},{24,28},{28,24},{1,5},{5... | collective-permute-start | bytes 6291464 | tf_op jit(solution)/shard_map/ppermute | solution.py:430
  163.0 22.6 %collective-permute-start.13 = (bf16[512,512]{1,0:T(8,128)(2,1)S(1)}, bf16[512,512]{1,0:T(8,128)(2,1)S(1)}, u32[]{:S(2)}, u32[]{:S(2)}) collective-permute-start(bf16[512,512]{1,0:T(8,128)(2,1)S(1)} %get-tuple-element.28), channel_id=1, source_target_pairs={{0,1},{1,2},{2,3},{3,0},{4,5},{5,6},{6,7},{7,4},{8,9},{9,10},{10,1... | collective-permute-start | bytes 1572872 | tf_op jit(solution)/shard_map/ppermute | solution.py:394
  163.6 37.9 %collective-permute-start.14 = (bf16[512,512]{1,0:T(8,128)(2,1)S(1)}, bf16[512,512]{1,0:T(8,128)(2,1)S(1)}, u32[]{:S(2)}, u32[]{:S(2)}) collective-permute-start(bf16[512,512]{1,0:T(8,128)(2,1)S(1)} %get-tuple-element.30), channel_id=1, source_target_pairs={{0,2},{1,3},{2,0},{3,1},{4,6},{5,7},{6,4},{7,5},{8,10},{9,11},{10,... | collective-permute-start | bytes 1572872 | tf_op jit(solution)/shard_map/ppermute | solution.py:394
  165.1 36.4 %collective-permute-start.15 = (bf16[512,512]{1,0:T(8,128)(2,1)S(1)}, bf16[512,512]{1,0:T(8,128)(2,1)S(1)}, u32[]{:S(2)}, u32[]{:S(2)}) collective-permute-start(bf16[512,512]{1,0:T(8,128)(2,1)S(1)} %get-tuple-element.31), channel_id=1, source_target_pairs={{0,3},{1,0},{2,1},{3,2},{4,7},{5,4},{6,5},{7,6},{8,11},{9,8},{10,9... | collective-permute-start | bytes 1572872 | tf_op jit(solution)/shard_map/ppermute | solution.py:394
  183.6 25.9 %collective-permute-start.18 = (bf16[512,1024]{1,0:T(8,128)(2,1)}, bf16[512,1024]{1,0:T(8,128)(2,1)S(1)}, u32[]{:S(2)}, u32[]{:S(2)}) collective-permute-start(bf16[512,1024]{1,0:T(8,128)(2,1)} %get-tuple-element.34), channel_id=1, source_target_pairs={{0,8},{4,20},{8,24},{12,4},{24,16},{28,12},{16,0},{20,28},{1,9},{5... | collective-permute-start | bytes 3145736 | tf_op jit(solution)/shard_map/ppermute | solution.py:281
  183.8 25.7 %collective-permute-start.16 = (bf16[512,1024]{1,0:T(8,128)(2,1)}, bf16[512,1024]{1,0:T(8,128)(2,1)S(1)}, u32[]{:S(2)}, u32[]{:S(2)}) collective-permute-start(bf16[512,1024]{1,0:T(8,128)(2,1)} %get-tuple-element.29.refs_1_), channel_id=1, source_target_pairs={{0,16},{4,12},{8,0},{12,28},{24,8},{28,20},{16,24},{20,4},{1,17},{... | collective-permute-start | bytes 3145736 | tf_op jit(solution)/shard_map/ppermute | solution.py:281
  210.7 9.6 %collective-permute-start.20 = (f32[2,512]{1,0:T(2,128)S(1)}, f32[2,512]{1,0:T(2,128)S(1)}, u32[]{:S(2)}, u32[]{:S(2)}) collective-permute-start(f32[2,512]{1,0:T(2,128)S(1)} %pad_maximum_fusion.1), channel_id=1, source_target_pairs={{0,2},{1,3},{2,0},{3,1},{4,6},{5,7},{6,4},{7,5},{8,10},{9,11},{10,... | collective-permute-start | bytes 12296 | tf_op jit(solution)/shard_map/ppermute | solution.py:394
  219.0 16.5 %collective-permute-start.17 = (bf16[512,1024]{1,0:T(8,128)(2,1)S(1)}, bf16[512,1024]{1,0:T(8,128)(2,1)S(1)}, u32[]{:S(2)}, u32[]{:S(2)}) collective-permute-start(bf16[512,1024]{1,0:T(8,128)(2,1)S(1)} %add_convert_fusion.1), channel_id=1, source_target_pairs={{0,16},{4,12},{8,0},{12,28},{24,8},{28,20},{16,24},{20,4},{1,17},{... | collective-permute-start | bytes 3145736 | tf_op jit(solution)/shard_map/ppermute | solution.py:286
  237.2 14.0 %collective-permute-start.24 = (bf16[256,1024]{1,0:T(8,128)(2,1)S(1)}, bf16[256,1024]{1,0:T(8,128)(2,1)S(1)}, u32[]{:S(2)}, u32[]{:S(2)}) collective-permute-start(bf16[256,1024]{1,0:T(8,128)(2,1)S(1)} %shard_map.130), channel_id=1, source_target_pairs={{0,4},{4,0},{8,12},{12,8},{16,20},{20,16},{24,28},{28,24},{1,5},{5... | collective-permute-start | bytes 1572872 | tf_op jit(solution)/shard_map/ppermute | solution.py:301
  (65 other events, 484.3 us)
Sparse Core Ops, SparseCore 0:
  9.9 64.7 all-gather.2
  76.6 54.3 all-gather.4
  136.1 51.6 reduce-scatter.4
  203.0 52.8 reduce-scatter.2

commit v6 on v5

--- a/solution.py
+++ b/solution.py
@@ -491,8 +491,11 @@
     )
     grad_conv = grad_conv.astype(BF16).reshape(images.shape)
     low, high = rims(grad_conv)
-    grad_images = taps(ids, low, grad_conv, high, dw_kernel, True, cotangent)
-    grad_in, grad_out = own_rows(ids, in_rows, [grad_images]), own_rows(ids, out_rows)
+    grad_out = own_rows(ids, out_rows)
+    grad_images = taps(
+        ids, low, grad_conv, high, dw_kernel, True, cotangent, after=[grad_out]
+    )
+    grad_in = own_rows(ids, in_rows, [grad_images])
     flat = images.reshape(pixels, local_ch)
     block_out = residual(ids, flat, layer_scale, branch, [grad_in, grad_out]).reshape(images.shape)
     return block_out, grad_images, grad_in, grad_out

time: 267 us -> 291 us (1.090)
  waiting for transfers between devices: 76.1 us -> 101 us
    ppermute x1, waiting for transfers between devices: 5.69 us -> 22.9 us  [ring_send(): lax.ppermute(blocks[1], 'row', AHEAD)]
    ppermute x2, starting transfers between devices: 12.1 us -> 4.04 us  [own_rows(): other = lax.ppermute(give_rows(ids, block, after), 'row', SIBLING)]
    ppermute x9, starting transfers between devices: 27.1 us -> 33.3 us  [shifted(): lax.ppermute(array, 'col', [(i, (i + step) % count) for i in range(count)])]
    ppermute x1, waiting for transfers between devices: 0.21 us -> 4.76 us  [ring_scatter(): lax.ppermute((sent[0].astype(F32) + behind.astype(F32)).astype(BF16), 'ro...]
    ppermute x9, waiting for transfers between devices: 44.3 us -> 48.5 us  [shifted(): lax.ppermute(array, 'col', [(i, (i + step) % count) for i in range(count)])]
    unnamed x118 -> x116, local copies, waits for them, and re-layouts: 18.6 us -> 19.2 us
  transfers between devices with their start and end apart: 30 -> 30, of which waited for: 11 -> 9; matrix products, arithmetic and copies ran while one was open for 4% -> 4% of each run, Pallas kernels for 31% -> 28%
where the time goes in v6:
time: 291 us; the launch traced here: 290 us
  waiting for transfers between devices  101 us (35%)
  Pallas kernels  81.9 us (28%)
  starting transfers between devices  61.8 us (21%)
  local copies, waits for them, and re-layouts  22.7 us (8%)
  between operations  14.6 us (5%)
  other arithmetic  7.9 us (3%)
    pallas_call x24, Pallas kernels, call(): pl.pallas_call(kernel, grid_spec=pltpu.PrefetchScalarGridSpec(num_scalar_...  81.9 us
    ppermute x9, waiting for transfers between devices, shifted(): lax.ppermute(array, 'col', [(i, (i + step) % count) for i in range(count)])  48.5 us
    ppermute x9, starting transfers between devices, shifted(): lax.ppermute(array, 'col', [(i, (i + step) % count) for i in range(count)])  33.3 us
    ppermute x1, waiting for transfers between devices, ring_send(): lax.ppermute(blocks[1], 'row', AHEAD)  22.9 us
    unnamed x116, local copies, waits for them, and re-layouts  19.2 us
    ppermute x1, waiting for transfers between devices, col_send(): across = lax.ppermute(block, 'col', ACROSS)  10.5 us
    ppermute x1, waiting for transfers between devices, col_gather(): far = lax.ppermute(across, 'col', [(1, 0), (2, 3)])  7.94 us
    ppermute x2, starting transfers between devices, rims(): low = lax.ppermute(block[:, -REACH:], 'row', forward)  6.85 us
  transfers between devices with their start and end apart: 30, of which 9 were waited for; matrix products, arithmetic and copies ran while one was open for 4% of the time, Pallas kernels for 28%

profile of v6, /device:TPU:0, one launch (start us, length us, event | category | flops | bytes accessed | tf_op | source)
XLA Modules:
  0.0 289.7 jit_solution(1073046264117678386)
XLA Ops:
  8.9 5.0 %collective-permute-start.3 = (bf16[512,512]{1,0:T(8,128)(2,1)S(1)}, bf16[512,512]{1,0:T(8,128)(2,1)S(1)}, u32[]{:S(2)}, u32[]{:S(2)}) collective-permute-start(bf16[512,512]{1,0:T(8,128)(2,1)S(1)} %fusion.1.refs_0_), channel_id=1, source_target_pairs={{0,1},{1,2},{2,3},{4,5},{5,6},{6,7},{8,9},{9,10},{10,11},{12,13},{... | collective-permute-start | bytes 1572872 | tf_op jit(solution)/shard_map/ppermute | solution.py:123
  17.4 3.8 %collective-permute-start = (bf16[2,3,64,512]{3,2,1,0:T(8,128)(2,1)}, bf16[2,3,64,512]{3,2,1,0:T(8,128)(2,1)}, u32[]{:S(2)}, u32[]{:S(2)}) collective-permute-start(bf16[2,3,64,512]{3,2,1,0:T(8,128)(2,1)} %get-tuple-element.51), channel_id=1, source_target_pairs={{0,4},{4,8},{8,12},{12,16},{16,20},{20,24},{24,28},{1,5},{5,9},{9,... | collective-permute-start | bytes 1179656 | tf_op jit(solution)/shard_map/ppermute | solution.py:377
  30.6 5.5 %shard_map.111 = (f32[2,4,64,512]{3,2,1,0:T(8,128)S(1)}, bf16[2,4,64,512]{3,2,1,0:T(8,128)(2,1)S(1)}, f32[2,4,64,1]{3,2,1,0:T(8,128)S(1)}, f32[2,4,64,1]{3,2,1,0:T(8,128)S(1)}) custom-call(s32[9]{0:T(128)S(1)} %dynamic-slice_bitcast_fusion.ids_ref, bf16[2,3,64,512]{3,2,1,0:T(8,128)(2,1)} %collective-permute-done.refs_0_, ...), custom_call_target="tpu_custom_call" | custom-call | flops 4294967296 | bytes 12582912 | tf_op jit(solution)/shard_map/pallas_call | solution.py:56
  42.9 10.5 %collective-permute-done.7.refs_0_ = bf16[512,512]{1,0:T(8,128)(2,1)S(1)} collective-permute-done((bf16[512,512]{1,0:T(8,128)(2,1)S(1)}, bf16[512,512]{1,0:T(8,128)(2,1)S(1)}, u32[]{:S(2)}, u32[]{:S(2)}) %collective-permute-start.7) | collective-permute-done | bytes 524320 | tf_op jit(solution)/shard_map/ppermute | solution.py:121
  56.0 11.6 %collective-permute-start.5 = (bf16[528,512]{1,0:T(8,128)(2,1)S(1)}, bf16[528,512]{1,0:T(8,128)(2,1)S(1)}, u32[]{:S(2)}, u32[]{:S(2)}) collective-permute-start(bf16[528,512]{1,0:T(8,128)(2,1)S(1)} %fusion.3.refs_1_.refs_0_), channel_id=1, source_target_pairs={{0,2},{1,3},{2,0},{3,1},{4,6},{5,7},{6,4},{7,5},{8,10},{9,11},{10,... | collective-permute-start | bytes 1622024 | tf_op jit(solution)/shard_map/ppermute | solution.py:394
  67.6 7.9 %collective-permute-done.8.refs_4_ = bf16[512,512]{1,0:T(8,128)(2,1)S(1)} collective-permute-done((bf16[512,512]{1,0:T(8,128)(2,1)S(1)}, bf16[512,512]{1,0:T(8,128)(2,1)S(1)}, u32[]{:S(2)}, u32[]{:S(2)}) %collective-permute-start.8) | collective-permute-done | bytes 524320 | tf_op jit(solution)/shard_map/ppermute | solution.py:131
  77.5 24.6 %collective-permute-done.5.refs_2_ = bf16[528,512]{1,0:T(8,128)(2,1)S(1)} collective-permute-done((bf16[528,512]{1,0:T(8,128)(2,1)S(1)}, bf16[528,512]{1,0:T(8,128)(2,1)S(1)}, u32[]{:S(2)}, u32[]{:S(2)}) %collective-permute-start.5) | collective-permute-done | bytes 540704 | tf_op jit(solution)/shard_map/ppermute | solution.py:394
  113.6 6.1 %shard_map.116 = (bf16[512,1024]{1,0:T(8,128)(2,1)S(1)}, bf16[512,1024]{1,0:T(8,128)(2,1)S(1)}) custom-call(s32[9]{0:T(128)S(1)} %copy-done.31, bf16[512,2048]{1,0:T(8,128)(2,1)} %shard_map.115.refs_0_, bf16[2048,2048]{1,0:T(8,128)(2,1)} %all-gather.3.cloned.1.call-done.refs_1_), custom_call_target="tpu_custom_call" | custom-call | flops 4294967296 | bytes 12582912 | tf_op jit(solution)/shard_map/pallas_call | solution.py:56
  120.7 6.1 %shard_map.117 = (bf16[512,1024]{1,0:T(8,128)(2,1)S(1)}, bf16[512,1024]{1,0:T(8,128)(2,1)S(1)}) custom-call(s32[9]{0:T(128)S(1)} %copy-done.31, bf16[512,2048]{1,0:T(8,128)(2,1)} %collective-permute-done.9.refs_0_.refs_1_, bf16[2048,2048]{1,0:T(8,128)(2,1)} %all-gather.3.cloned.1.call-done.refs_1_, bf16[512,1024]{1,0:T(8,128)(2,1)S(1)} %get-tuple-element.23.refs_2_.refs_0_), custom_call_target="tpu_custom_call" | custom-call | flops 4294967296 | bytes 12582912 | tf_op jit(solution)/shard_map/pallas_call | solution.py:56
  126.9 8.0 %shard_map.118.refs_3_ = bf16[2048,1024]{1,0:T(8,128)(2,1)} custom-call(s32[9]{0:T(128)S(1)} %copy-done.31, bf16[512,2048]{1,0:T(8,128)(2,1)S(1)} %shard_map.113.refs_1_.refs_0_, bf16[512,2048]{1,0:T(8,128)(2,1)} %collective-permute-done.10.refs_1_.refs_0_, bf16[512,1024]{1,0:T(8,128)(2,1)S(1)} %get-tuple-element.23.refs_2_.refs_0_, ...), custom_call_target="tpu_custom_call" | custom-call | flops 4294967296 | bytes 12582912 | tf_op jit(solution)/shard_map/pallas_call | solution.py:56
  136.5 5.4 %shard_map.119.refs_0_.refs_3_ = bf16[512,1024]{1,0:T(8,128)(2,1)S(1)} custom-call(s32[9]{0:T(128)S(1)} %copy-done.32, bf16[512,2048]{1,0:T(8,128)(2,1)} %collective-permute-done.10.refs_1_.refs_0_, bf16[2048,2048]{1,0:T(8,128)(2,1)} %all-gather.5.cloned.1.call-done.refs_1_, bf16[512,1024]{1,0:T(8,128)(2,1)S(1)} %get-tuple-element.26.refs_2_, ...), custom_call_target="tpu_custom_call" | custom-call | flops 4294967296 | bytes 12582912 | tf_op jit(solution)/shard_map/pallas_call | solution.py:56
  141.9 4.9 %shard_map.120.refs_3_ = bf16[512,2048]{1,0:T(8,128)(2,1)S(1)} custom-call(s32[9]{0:T(128)S(1)} %copy-done.32, bf16[512,1024]{1,0:T(8,128)(2,1)S(1)} %shard_map.119.refs_0_.refs_3_, bf16[2048,2048]{1,0:T(8,128)(2,1)} %all-gather.3.cloned.1.call-done.refs_1_), custom_call_target="tpu_custom_call" | custom-call | flops 4294967296 | bytes 12582912 | tf_op jit(solution)/shard_map/pallas_call | solution.py:56
  146.9 4.9 %shard_map.121.refs_0_.refs_2_ = bf16[512,1024]{1,0:T(8,128)(2,1)S(1)} custom-call(s32[9]{0:T(128)S(1)} %copy-done.32, bf16[512,2048]{1,0:T(8,128)(2,1)S(1)} %shard_map.113.refs_1_.refs_0_, bf16[2048,2048]{1,0:T(8,128)(2,1)} %all-gather.5.cloned.1.call-done.refs_1_, bf16[512,1024]{1,0:T(8,128)(2,1)S(1)} %copy-done.40, bf16[512,2048]{1,0:T(8,128)(2,1)S(1)} %shard_map.120.refs_3_), custom_call_target="tpu_custom_call" | custom-call | flops 4294967296 | bytes 12582912 | tf_op jit(solution)/shard_map/pallas_call | solution.py:56
  151.9 5.7 %shard_map.122 = (bf16[512,512]{1,0:T(8,128)(2,1)S(1)}, bf16[512,512]{1,0:T(8,128)(2,1)S(1)}, bf16[512,512]{1,0:T(8,128)(2,1)S(1)}, bf16[512,512]{1,0:T(8,128)(2,1)S(1)}) custom-call(s32[9]{0:T(128)S(1)} %copy-done.32, bf16[512,1024]{1,0:T(8,128)(2,1)S(1)} %shard_map.121.refs_0_.refs_2_, bf16[2048,2048]{1,0:T(8,128)(2,1)} %all-gather.3.cloned.1.call-done.refs_1_, ...), custom_call_target="tpu_custom_call" | custom-call | flops 4294967296 | bytes 12582912 | tf_op jit(solution)/shard_map/pallas_call | solution.py:56
  157.5 4.9 %shard_map.123 = bf16[512,2048]{1,0:T(8,128)(2,1)S(1)} custom-call(s32[9]{0:T(128)S(1)} %copy-done.32, bf16[512,1024]{1,0:T(8,128)(2,1)S(1)} %copy-done.44, bf16[2048,2048]{1,0:T(8,128)(2,1)} %all-gather.5.cloned.1.call-done.refs_1_, bf16[512,512]{1,0:T(8,128)(2,1)S(1)} %get-tuple-element.27.refs_2_.refs_3_), custom_call_target="tpu_custom_call" | custom-call | flops 4294967296 | bytes 12582912 | tf_op jit(solution)/shard_map/pallas_call | solution.py:56
  168.0 5.8 %shard_map.124.refs_4_.refs_0_ = bf16[512,2048]{1,0:T(8,128)(2,1)} custom-call(s32[9]{0:T(128)S(1)} %copy-done.32, bf16[512,1024]{1,0:T(8,128)(2,1)S(1)} %copy-done.42, bf16[2048,2048]{1,0:T(8,128)(2,1)} %all-gather.5.cloned.1.call-done.refs_1_, bf16[512,2048]{1,0:T(8,128)(2,1)S(1)} %collective-permute-done.12.refs_2_, ...), custom_call_target="tpu_custom_call" | custom-call | flops 4294967296 | bytes 12582912 | tf_op jit(solution)/shard_map/pallas_call | solution.py:56
  173.8 7.5 %shard_map.125 = (bf16[512,1024]{1,0:T(8,128)(2,1)S(1)}, bf16[512,1024]{1,0:T(8,128)(2,1)S(1)}, bf16[512,1024]{1,0:T(8,128)(2,1)S(1)}, bf16[512,1024]{1,0:T(8,128)(2,1)S(1)}) custom-call(s32[9]{0:T(128)S(1)} %copy-done.32, bf16[512,2048]{1,0:T(8,128)(2,1)} %shard_map.115.refs_0_, bf16[512,2048]{1,0:T(8,128)(2,1)} %collective-permute-done.9.refs_0_.refs_1_, ...), custom_call_target="tpu_custom_call" | custom-call | flops 4294967296 | bytes 12582912 | tf_op jit(solution)/shard_map/pallas_call | solution.py:56
  181.3 20.1 %collective-permute-done.14.refs_2_ = bf16[512,512]{1,0:T(8,128)(2,1)S(1)} collective-permute-done((bf16[512,512]{1,0:T(8,128)(2,1)S(1)}, bf16[512,512]{1,0:T(8,128)(2,1)S(1)}, u32[]{:S(2)}, u32[]{:S(2)}) %collective-permute-start.14) | collective-permute-done | bytes 524320 | tf_op jit(solution)/shard_map/ppermute | solution.py:394
  205.5 22.9 %collective-permute-done.18.refs_3_ = bf16[512,1024]{1,0:T(8,128)(2,1)S(1)} collective-permute-done((bf16[512,1024]{1,0:T(8,128)(2,1)}, bf16[512,1024]{1,0:T(8,128)(2,1)S(1)}, u32[]{:S(2)}, u32[]{:S(2)}) %collective-permute-start.18) | collective-permute-done | bytes 1048608 | tf_op jit(solution)/shard_map/ppermute | solution.py:281
  229.6 10.7 %collective-permute-start.20 = (f32[2,512]{1,0:T(2,128)S(1)}, f32[2,512]{1,0:T(2,128)S(1)}, u32[]{:S(2)}, u32[]{:S(2)}) collective-permute-start(f32[2,512]{1,0:T(2,128)S(1)} %pad_maximum_fusion.1), channel_id=1, source_target_pairs={{0,2},{1,3},{2,0},{3,1},{4,6},{5,7},{6,4},{7,5},{8,10},{9,11},{10,... | collective-permute-start | bytes 12296 | tf_op jit(solution)/shard_map/ppermute | solution.py:394
  245.5 3.8 %collective-permute-done.19 = f32[2,512]{1,0:T(2,128)S(1)} collective-permute-done((f32[2,512]{1,0:T(2,128)S(1)}, f32[2,512]{1,0:T(2,128)S(1)}, u32[]{:S(2)}, u32[]{:S(2)}) %collective-permute-start.19) | collective-permute-done | bytes 4128 | tf_op jit(solution)/shard_map/ppermute | solution.py:394
  256.1 4.8 %collective-permute-done.17 = bf16[512,1024]{1,0:T(8,128)(2,1)} collective-permute-done((bf16[512,1024]{1,0:T(8,128)(2,1)}, bf16[512,1024]{1,0:T(8,128)(2,1)}, u32[]{:S(2)}, u32[]{:S(2)}) %collective-permute-start.17) | collective-permute-done | bytes 1048608 | tf_op jit(solution)/shard_map/ppermute | solution.py:286
  265.6 4.9 %shard_map.131.refs_1_ = bf16[2,4,64,512]{3,2,1,0:T(8,128)(2,1)} custom-call(s32[9]{0:T(128)S(1)} %copy-done.32, bf16[2,3,64,512]{3,2,1,0:T(8,128)(2,1)S(1)} %collective-permute-done.22.refs_0_, bf16[2,4,64,512]{3,2,1,0:T(8,128)(2,1)S(1)} %bitcast.29, bf16[2,3,64,512]{3,2,1,0:T(8,128)(2,1)S(1)} %collective-permute-done.23.refs_2_, ...), custom_call_target="tpu_custom_call" | custom-call | flops 4294967296 | bytes 12582912 | tf_op jit(solution)/shard_map/pallas_call | solution.py:56
  272.2 4.0 %collective-permute-start.25 = (bf16[256,1024]{1,0:T(8,128)(2,1)S(1)}, bf16[256,1024]{1,0:T(8,128)(2,1)S(1)}, u32[]{:S(2)}, u32[]{:S(2)}) collective-permute-start(bf16[256,1024]{1,0:T(8,128)(2,1)S(1)} %shard_map.132), channel_id=1, source_target_pairs={{0,4},{4,0},{8,12},{12,8},{16,20},{20,16},{24,28},{28,24},{1,5},{5... | collective-permute-start | bytes 1572872 | tf_op jit(solution)/shard_map/ppermute | solution.py:301
  (214 shorter events, 75.7 us)
Async XLA Ops:
  7.2 105.8 %all-gather.3.cloned.1.call-start = ((), (), s32[]{:S(2)}) async-start(), calls=%async_computation.2 | async-start | bytes 9437184 | tf_op jit(solution)/shard_map/all_gather | solution.py:432
  8.0 128.0 %all-gather.5.cloned.1.call-start = ((), (), s32[]{:S(2)}) async-start(), calls=%async_computation.3 | async-start | bytes 9437184 | tf_op jit(solution)/shard_map/all_gather | solution.py:433
  8.7 241.0 %reduce-scatter.5.cloned.1.call-start = ((), (), s32[]{:S(2)}) async-start(), calls=%async_computation.5 | async-start | bytes 5242880 | tf_op jit(solution)/shard_map/reduce_scatter | solution.py:419
  8.9 17.5 %collective-permute-start.3 = (bf16[512,512]{1,0:T(8,128)(2,1)S(1)}, bf16[512,512]{1,0:T(8,128)(2,1)S(1)}, u32[]{:S(2)}, u32[]{:S(2)}) collective-permute-start(bf16[512,512]{1,0:T(8,128)(2,1)S(1)} %fusion.1.refs_0_), channel_id=1, source_target_pairs={{0,1},{1,2},{2,3},{4,5},{5,6},{6,7},{8,9},{9,10},{10,11},{12,13},{... | collective-permute-start | bytes 1572872 | tf_op jit(solution)/shard_map/ppermute | solution.py:123
  13.9 15.8 %collective-permute-start.2 = (bf16[512,512]{1,0:T(8,128)(2,1)S(1)}, bf16[512,512]{1,0:T(8,128)(2,1)S(1)}, u32[]{:S(2)}, u32[]{:S(2)}) collective-permute-start(bf16[512,512]{1,0:T(8,128)(2,1)S(1)} %fusion.1.refs_0_), channel_id=1, source_target_pairs={{1,0},{2,1},{3,2},{5,4},{6,5},{7,6},{9,8},{10,9},{11,10},{13,12},{... | collective-permute-start | bytes 1572872 | tf_op jit(solution)/shard_map/ppermute | solution.py:122
  16.1 9.5 %collective-permute-start.1 = (bf16[2,3,64,512]{3,2,1,0:T(8,128)(2,1)}, bf16[2,3,64,512]{3,2,1,0:T(8,128)(2,1)S(1)}, u32[]{:S(2)}, u32[]{:S(2)}) collective-permute-start(bf16[2,3,64,512]{3,2,1,0:T(8,128)(2,1)} %get-tuple-element.50), channel_id=1, source_target_pairs={{4,0},{8,4},{12,8},{16,12},{20,16},{24,20},{28,24},{5,1},{9,5},{13... | collective-permute-start | bytes 1179656 | tf_op jit(solution)/shard_map/ppermute | solution.py:378
  17.4 9.0 %collective-permute-start = (bf16[2,3,64,512]{3,2,1,0:T(8,128)(2,1)}, bf16[2,3,64,512]{3,2,1,0:T(8,128)(2,1)}, u32[]{:S(2)}, u32[]{:S(2)}) collective-permute-start(bf16[2,3,64,512]{3,2,1,0:T(8,128)(2,1)} %get-tuple-element.51), channel_id=1, source_target_pairs={{0,4},{4,8},{8,12},{12,16},{16,20},{20,24},{24,28},{1,5},{5,9},{9,... | collective-permute-start | bytes 1179656 | tf_op jit(solution)/shard_map/ppermute | solution.py:377
  21.2 32.1 %collective-permute-start.7 = (bf16[512,512]{1,0:T(8,128)(2,1)S(1)}, bf16[512,512]{1,0:T(8,128)(2,1)S(1)}, u32[]{:S(2)}, u32[]{:S(2)}) collective-permute-start(bf16[512,512]{1,0:T(8,128)(2,1)S(1)} %fusion.1.refs_0_), channel_id=1, source_target_pairs={{0,2},{1,3},{2,0},{3,1},{4,6},{5,7},{6,4},{7,5},{8,10},{9,11},{10,... | collective-permute-start | bytes 1572872 | tf_op jit(solution)/shard_map/ppermute | solution.py:121
  40.3 37.2 %collective-permute-start.6 = (bf16[528,512]{1,0:T(8,128)(2,1)S(1)}, bf16[528,512]{1,0:T(8,128)(2,1)S(1)}, u32[]{:S(2)}, u32[]{:S(2)}) collective-permute-start(bf16[528,512]{1,0:T(8,128)(2,1)S(1)} %fusion.3.refs_1_.refs_0_), channel_id=1, source_target_pairs={{0,3},{1,0},{2,1},{3,2},{4,7},{5,4},{6,5},{7,6},{8,11},{9,8},{10,9... | collective-permute-start | bytes 1622024 | tf_op jit(solution)/shard_map/ppermute | solution.py:394
  53.9 21.7 %collective-permute-start.8 = (bf16[512,512]{1,0:T(8,128)(2,1)S(1)}, bf16[512,512]{1,0:T(8,128)(2,1)S(1)}, u32[]{:S(2)}, u32[]{:S(2)}) collective-permute-start(bf16[512,512]{1,0:T(8,128)(2,1)S(1)} %shard_map.112.refs_2_), channel_id=1, source_target_pairs={{1,0},{2,3},{5,4},{6,7},{9,8},{10,11},{13,12},{14,15},{17,16},{18,... | collective-permute-start | bytes 1572872 | tf_op jit(solution)/shard_map/ppermute | solution.py:131
  56.0 46.1 %collective-permute-start.5 = (bf16[528,512]{1,0:T(8,128)(2,1)S(1)}, bf16[528,512]{1,0:T(8,128)(2,1)S(1)}, u32[]{:S(2)}, u32[]{:S(2)}) collective-permute-start(bf16[528,512]{1,0:T(8,128)(2,1)S(1)} %fusion.3.refs_1_.refs_0_), channel_id=1, source_target_pairs={{0,2},{1,3},{2,0},{3,1},{4,6},{5,7},{6,4},{7,5},{8,10},{9,11},{10,... | collective-permute-start | bytes 1622024 | tf_op jit(solution)/shard_map/ppermute | solution.py:394
  67.6 34.5 %collective-permute-start.4 = (bf16[528,512]{1,0:T(8,128)(2,1)S(1)}, bf16[528,512]{1,0:T(8,128)(2,1)S(1)}, u32[]{:S(2)}, u32[]{:S(2)}) collective-permute-start(bf16[528,512]{1,0:T(8,128)(2,1)S(1)} %fusion.3.refs_1_.refs_0_), channel_id=1, source_target_pairs={{0,1},{1,2},{2,3},{3,0},{4,5},{5,6},{6,7},{7,4},{8,9},{9,10},{10,1... | collective-permute-start | bytes 1622024 | tf_op jit(solution)/shard_map/ppermute | solution.py:394
  112.5 14.4 %collective-permute-start.10 = (bf16[512,2048]{1,0:T(8,128)(2,1)S(1)}, bf16[512,2048]{1,0:T(8,128)(2,1)}, u32[]{:S(2)}, u32[]{:S(2)}) collective-permute-start(bf16[512,2048]{1,0:T(8,128)(2,1)S(1)} %shard_map.113.refs_1_.refs_0_), channel_id=1, source_target_pairs={{0,4},{4,0},{8,12},{12,8},{16,20},{20,16},{24,28},{28,24},{1,5},{5... | collective-permute-start | bytes 6291464 | tf_op jit(solution)/shard_map/ppermute | solution.py:430
  135.9 143.5 %reduce-scatter.3.cloned.1.call-start = ((), (), s32[]{:S(2)}) async-start(), calls=%async_computation.4 | async-start | bytes 2621440 | tf_op jit(solution)/shard_map/reduce_scatter | solution.py:481
  163.0 18.4 %collective-permute-start.13 = (bf16[512,512]{1,0:T(8,128)(2,1)S(1)}, bf16[512,512]{1,0:T(8,128)(2,1)S(1)}, u32[]{:S(2)}, u32[]{:S(2)}) collective-permute-start(bf16[512,512]{1,0:T(8,128)(2,1)S(1)} %get-tuple-element.28), channel_id=1, source_target_pairs={{0,1},{1,2},{2,3},{3,0},{4,5},{5,6},{6,7},{7,4},{8,9},{9,10},{10,1... | collective-permute-start | bytes 1572872 | tf_op jit(solution)/shard_map/ppermute | solution.py:394
  163.6 37.9 %collective-permute-start.14 = (bf16[512,512]{1,0:T(8,128)(2,1)S(1)}, bf16[512,512]{1,0:T(8,128)(2,1)S(1)}, u32[]{:S(2)}, u32[]{:S(2)}) collective-permute-start(bf16[512,512]{1,0:T(8,128)(2,1)S(1)} %get-tuple-element.30), channel_id=1, source_target_pairs={{0,2},{1,3},{2,0},{3,1},{4,6},{5,7},{6,4},{7,5},{8,10},{9,11},{10,... | collective-permute-start | bytes 1572872 | tf_op jit(solution)/shard_map/ppermute | solution.py:394
  165.1 36.4 %collective-permute-start.15 = (bf16[512,512]{1,0:T(8,128)(2,1)S(1)}, bf16[512,512]{1,0:T(8,128)(2,1)S(1)}, u32[]{:S(2)}, u32[]{:S(2)}) collective-permute-start(bf16[512,512]{1,0:T(8,128)(2,1)S(1)} %get-tuple-element.31), channel_id=1, source_target_pairs={{0,3},{1,0},{2,1},{3,2},{4,7},{5,4},{6,5},{7,6},{8,11},{9,8},{10,9... | collective-permute-start | bytes 1572872 | tf_op jit(solution)/shard_map/ppermute | solution.py:394
  202.7 25.7 %collective-permute-start.18 = (bf16[512,1024]{1,0:T(8,128)(2,1)}, bf16[512,1024]{1,0:T(8,128)(2,1)S(1)}, u32[]{:S(2)}, u32[]{:S(2)}) collective-permute-start(bf16[512,1024]{1,0:T(8,128)(2,1)} %copy-done.35), channel_id=1, source_target_pairs={{0,8},{4,20},{8,24},{12,4},{24,16},{28,12},{16,0},{20,28},{1,9},{5... | collective-permute-start | bytes 3145736 | tf_op jit(solution)/shard_map/ppermute | solution.py:281
  202.7 25.6 %collective-permute-start.16 = (bf16[512,1024]{1,0:T(8,128)(2,1)}, bf16[512,1024]{1,0:T(8,128)(2,1)S(1)}, u32[]{:S(2)}, u32[]{:S(2)}) collective-permute-start(bf16[512,1024]{1,0:T(8,128)(2,1)} %copy-done.9), channel_id=1, source_target_pairs={{0,16},{4,12},{8,0},{12,28},{24,8},{28,20},{16,24},{20,4},{1,17},{... | collective-permute-start | bytes 3145736 | tf_op jit(solution)/shard_map/ppermute | solution.py:281
  229.6 16.0 %collective-permute-start.20 = (f32[2,512]{1,0:T(2,128)S(1)}, f32[2,512]{1,0:T(2,128)S(1)}, u32[]{:S(2)}, u32[]{:S(2)}) collective-permute-start(f32[2,512]{1,0:T(2,128)S(1)} %pad_maximum_fusion.1), channel_id=1, source_target_pairs={{0,2},{1,3},{2,0},{3,1},{4,6},{5,7},{6,4},{7,5},{8,10},{9,11},{10,... | collective-permute-start | bytes 12296 | tf_op jit(solution)/shard_map/ppermute | solution.py:394
  245.1 15.8 %collective-permute-start.17 = (bf16[512,1024]{1,0:T(8,128)(2,1)}, bf16[512,1024]{1,0:T(8,128)(2,1)}, u32[]{:S(2)}, u32[]{:S(2)}) collective-permute-start(bf16[512,1024]{1,0:T(8,128)(2,1)} %add_convert_fusion.1), channel_id=1, source_target_pairs={{0,16},{4,12},{8,0},{12,28},{24,8},{28,20},{16,24},{20,4},{1,17},{... | collective-permute-start | bytes 3145736 | tf_op jit(solution)/shard_map/ppermute | solution.py:286
  251.6 11.2 %collective-permute-start.24 = (bf16[256,1024]{1,0:T(8,128)(2,1)S(1)}, bf16[256,1024]{1,0:T(8,128)(2,1)S(1)}, u32[]{:S(2)}, u32[]{:S(2)}) collective-permute-start(bf16[256,1024]{1,0:T(8,128)(2,1)S(1)} %shard_map.129), channel_id=1, source_target_pairs={{0,4},{4,0},{8,12},{12,8},{16,20},{20,16},{24,28},{28,24},{1,5},{5... | collective-permute-start | bytes 1572872 | tf_op jit(solution)/shard_map/ppermute | solution.py:301
  251.7 12.6 %collective-permute-start.23 = (bf16[2,3,64,512]{3,2,1,0:T(8,128)(2,1)S(1)}, bf16[2,3,64,512]{3,2,1,0:T(8,128)(2,1)S(1)}, u32[]{:S(2)}, u32[]{:S(2)}) collective-permute-start(bf16[2,3,64,512]{3,2,1,0:T(8,128)(2,1)S(1)} %get-tuple-element.48), channel_id=1, source_target_pairs={{4,0},{8,4},{12,8},{16,12},{20,16},{24,20},{28,24},{5,1},{9,5},{13... | collective-permute-start | bytes 1179656 | tf_op jit(solution)/shard_map/ppermute | solution.py:378
  253.0 11.4 %collective-permute-start.22 = (bf16[2,3,64,512]{3,2,1,0:T(8,128)(2,1)S(1)}, bf16[2,3,64,512]{3,2,1,0:T(8,128)(2,1)S(1)}, u32[]{:S(2)}, u32[]{:S(2)}) collective-permute-start(bf16[2,3,64,512]{3,2,1,0:T(8,128)(2,1)S(1)} %get-tuple-element.49), channel_id=1, source_target_pairs={{0,4},{4,8},{8,12},{12,16},{16,20},{20,24},{24,28},{1,5},{5,9},{9,... | collective-permute-start | bytes 1179656 | tf_op jit(solution)/shard_map/ppermute | solution.py:377
  (64 other events, 601.0 us)
Sparse Core Ops, SparseCore 0:
  9.9 64.7 all-gather.2
  76.6 54.3 all-gather.4
  136.0 51.5 reduce-scatter.4
  202.7 53.0 reduce-scatter.2
